TPU v7x, 32 devices: a whole 2x2x4 slice. The times are simulated.
32 devices in a mesh: dp: 4 (over y, core), heads: 2 (over x), hidden: 4 (over z).
Axes of the slice: x: 2, y: 2, z: 4, core: 2. Of those that a mesh axis runs over, the one named last changes fastest.
Arguments:
- patches: bfloat16 [32, 196, 768], P(('dp', 'heads', 'hidden')), may hold values from -6 to 6
- labels: int32 [32], P('dp'), may hold values from 0 to 999
- w_patch: float32 [768, 768], P(None, ('dp', 'heads', 'hidden')), may hold values from -0.21875 to 0.21875
- table: float32 [200, 768], P(None, ('dp', 'heads', 'hidden')), may hold values from -3 to 3
- gains: float32 [4, 768], P(None, ('dp', 'heads', 'hidden')), may hold values from 0.5 to 1.5
- w_head: float32 [768, 1000], P(('dp', 'heads', 'hidden')), may hold values from -6 to 6
- w_qkv: float32 [768, 3, 768], P(('dp', 'hidden'), None, 'heads'), may hold values from -0.21875 to 0.21875
- w_out: float32 [768, 768], P(('heads', 'hidden'), 'dp'), may hold values from -1.75 to 1.75
- w_up: float32 [768, 3072], P('dp', ('heads', 'hidden')), may hold values from -0.21875 to 0.21875
- w_down: float32 [3072, 768], P(('heads', 'hidden'), 'dp'), may hold values from -0.109375 to 0.109375
- first_patch: float32 [768, 768], P(None, ('dp', 'heads', 'hidden')), may hold values from -2.3841858e-07 to 2.3841858e-07
- first_table: float32 [200, 768], P(None, ('dp', 'heads', 'hidden')), may hold values from -2.3841858e-07 to 2.3841858e-07
- first_gains: float32 [4, 768], P(None, ('dp', 'heads', 'hidden')), may hold values from -7.1525574e-07 to 7.1525574e-07
- first_head: float32 [768, 1000], P(('dp', 'heads', 'hidden')), may hold values from -2.3841858e-07 to 2.3841858e-07
- first_qkv: float32 [768, 3, 768], P(('dp', 'hidden'), None, 'heads'), may hold values from -2.3841858e-07 to 2.3841858e-07
- first_out: float32 [768, 768], P(('heads', 'hidden'), 'dp'), may hold values from -2.3841858e-07 to 2.3841858e-07
- first_up: float32 [768, 3072], P('dp', ('heads', 'hidden')), may hold values from -2.3841858e-07 to 2.3841858e-07
- first_down: float32 [3072, 768], P(('heads', 'hidden'), 'dp'), may hold values from -2.3841858e-07 to 2.3841858e-07
- second_patch: float32 [768, 768], P(None, ('dp', 'heads', 'hidden')), may hold values from 1.1638214e-16 to 4.6552857e-16
- second_table: float32 [200, 768], P(None, ('dp', 'heads', 'hidden')), may hold values from 1.4547768e-17 to 5.819107e-17
- second_gains: float32 [4, 768], P(None, ('dp', 'heads', 'hidden')), may hold values from 1.0474392e-15 to 4.189757e-15
- second_head: float32 [768, 1000], P(('dp', 'heads', 'hidden')), may hold values from 1.1638214e-16 to 4.6552857e-16
- second_qkv: float32 [768, 3, 768], P(('dp', 'hidden'), None, 'heads'), may hold values from 1.1638214e-16 to 4.6552857e-16
- second_out: float32 [768, 768], P(('heads', 'hidden'), 'dp'), may hold values from 1.1638214e-16 to 4.6552857e-16
- second_up: float32 [768, 3072], P('dp', ('heads', 'hidden')), may hold values from 5.819107e-18 to 2.3276427e-17
- second_down: float32 [3072, 768], P(('heads', 'hidden'), 'dp'), may hold values from 1.1638214e-16 to 4.6552857e-16
Outputs:
- loss_sum: float32 [], replicated
- grad_norm: float32 [], replicated
- new_first_patch: float32 [768, 768], P(None, ('dp', 'heads', 'hidden'))
- new_first_table: float32 [200, 768], P(None, ('dp', 'heads', 'hidden'))
- new_first_gains: float32 [4, 768], P(None, ('dp', 'heads', 'hidden'))
- new_first_head: float32 [768, 1000], P(('dp', 'heads', 'hidden'))
- new_first_qkv: float32 [768, 3, 768], P(('dp', 'hidden'), None, 'heads')
- new_first_out: float32 [768, 768], P(('heads', 'hidden'), 'dp')
- new_first_up: float32 [768, 3072], P('dp', ('heads', 'hidden'))
- new_first_down: float32 [3072, 768], P(('heads', 'hidden'), 'dp')
- new_second_patch: float32 [768, 768], P(None, ('dp', 'heads', 'hidden'))
- new_second_table: float32 [200, 768], P(None, ('dp', 'heads', 'hidden'))
- new_second_gains: float32 [4, 768], P(None, ('dp', 'heads', 'hidden'))
- new_second_head: float32 [768, 1000], P(('dp', 'heads', 'hidden'))
- new_second_qkv: float32 [768, 3, 768], P(('dp', 'hidden'), None, 'heads')
- new_second_out: float32 [768, 768], P(('heads', 'hidden'), 'dp')
- new_second_up: float32 [768, 3072], P('dp', ('heads', 'hidden'))
- new_second_down: float32 [3072, 768], P(('heads', 'hidden'), 'dp')
- new_w_patch: float32 [768, 768], P(None, ('dp', 'heads', 'hidden'))
- new_table: float32 [200, 768], P(None, ('dp', 'heads', 'hidden'))
- new_gains: float32 [4, 768], P(None, ('dp', 'heads', 'hidden'))
- new_w_head: float32 [768, 1000], P(('dp', 'heads', 'hidden'))
- new_w_qkv: float32 [768, 3, 768], P(('dp', 'hidden'), None, 'heads')
- new_w_out: float32 [768, 768], P(('heads', 'hidden'), 'dp')
- new_w_up: float32 [768, 3072], P('dp', ('heads', 'hidden'))
- new_w_down: float32 [3072, 768], P(('heads', 'hidden'), 'dp')
All inputs are finite; a program needn't handle non-finite values.
Results may differ from a plain program's by a relative error of at most 0.014.
The roundings to bfloat16 on the way count: a program that leaves them out, or rounds other values in their place, can miss the bound.
Values may be sent and summed in bfloat16 or wider, within the bound.
A program may use at most 128 MiB of HBM per device.

v0:
```python
import jax
import jax.numpy as jnp
from jax import lax
from jax.sharding import PartitionSpec as P

HD = 64
PD = 768
STEP = 10


beta_one = 0.9
beta_two = 0.999
adam_eps = 1e-08
decay_rate = 0.01
learn_rate = 0.5
clip_at = 0.001
norm_eps = 1e-06
highest = lax.Precision.HIGHEST


def layer_norm(values):
    center = values - jnp.mean(values, axis=-1, keepdims=True)
    return center * lax.rsqrt(jnp.mean(center * center, axis=-1, keepdims=True) + norm_eps)


def head_loss(stream_out, targets, final_gain, head_weight, npatch, total_images):
    normed_out, norm_back = jax.vjp(layer_norm, stream_out)
    final = normed_out * final_gain
    pooled_b = jnp.mean(final[:, :npatch], axis=1).astype(jnp.bfloat16)
    logits = jnp.dot(pooled_b, head_weight, preferred_element_type=jnp.float32)
    log_total = jax.nn.logsumexp(logits, axis=-1)
    onehot = (targets[:, None] == lax.broadcasted_iota(jnp.int32, logits.shape, 1)).astype(
        jnp.float32
    )
    terms = log_total - jnp.sum(logits * onehot, axis=-1)
    d_logits = (jnp.exp(logits - log_total[:, None]) - onehot) / total_images
    d_pooled = jnp.dot(d_logits, head_weight.astype(jnp.float32).T, precision=highest)
    count, seq_len, width = stream_out.shape
    spread = jnp.broadcast_to(d_pooled[:, None, :] / npatch, (count, npatch, width))
    d_final = jnp.concatenate(
        [spread, jnp.zeros((count, seq_len - npatch, width), jnp.float32)], axis=1
    )
    d_stream = norm_back(d_final * final_gain)[0]
    d_gain_rows = jnp.sum(d_final * normed_out, axis=1)
    return (terms, pooled_b, d_logits, d_stream, d_gain_rows)


def per_device(
    patches,
    labels,
    w_patch,
    table,
    gains,
    w_head,
    w_qkv,
    w_out,
    w_up,
    w_down,
    first_patch,
    first_table,
    first_gains,
    first_head,
    first_qkv,
    first_out,
    first_up,
    first_down,
    second_patch,
    second_table,
    second_gains,
    second_head,
    second_qkv,
    second_out,
    second_up,
    second_down,
):
    masters = [w_patch, table, gains, w_head, w_qkv, w_out, w_up, w_down]
    firsts = [
        first_patch,
        first_table,
        first_gains,
        first_head,
        first_qkv,
        first_out,
        first_up,
        first_down,
    ]
    seconds = [
        second_patch,
        second_table,
        second_gains,
        second_head,
        second_qkv,
        second_out,
        second_up,
        second_down,
    ]
    bfloat = jnp.bfloat16
    single = jnp.float32
    patch_b, table_b, gains_b, head_b = (
        lax.all_gather(w_patch.astype(bfloat), ("dp", "heads", "hidden"), axis=1, tiled=True),
        lax.all_gather(table.astype(bfloat), ("dp", "heads", "hidden"), axis=1, tiled=True),
        lax.all_gather(gains.astype(bfloat), ("dp", "heads", "hidden"), axis=1, tiled=True),
        lax.all_gather(w_head.astype(bfloat), ("dp", "heads", "hidden"), axis=0, tiled=True),
    )
    qkv_b = lax.all_gather(w_qkv.astype(bfloat), ("dp", "hidden"), axis=0, tiled=True)
    out_b, up_b, down_b = (
        lax.all_gather(w_out.astype(bfloat), "dp", axis=1, tiled=True),
        lax.all_gather(w_up.astype(bfloat), "dp", axis=0, tiled=True),
        lax.all_gather(w_down.astype(bfloat), "dp", axis=1, tiled=True),
    )
    gain_vals = gains_b.astype(single)
    table_vals = table_b.astype(single)
    n_hidden = lax.axis_size("hidden")
    n_own = patches.shape[0]
    npatch = patches.shape[1]
    seq_len = table_b.shape[0]
    width = patch_b.shape[1]
    group_width = qkv_b.shape[2]
    group_heads = group_width // HD
    own_index = lax.axis_index("heads") * n_hidden + lax.axis_index("hidden")
    total_images = labels.shape[0] * lax.axis_size("dp")
    embedded = jnp.dot(patches.reshape(n_own * npatch, PD), patch_b, preferred_element_type=single)
    embedded = embedded.reshape(n_own, npatch, width) + table_vals[:npatch]
    registers = jnp.broadcast_to(table_vals[npatch:], (n_own, seq_len - npatch, width))
    stream_own = jnp.concatenate([embedded, registers], axis=1).astype(bfloat)
    stream_in = lax.all_gather(stream_own, ("heads", "hidden"), axis=0, tiled=True)
    n_img = stream_in.shape[0]
    row_count = n_img * seq_len
    stream_flat = stream_in.astype(single).reshape(row_count, width)
    normed_b = (layer_norm(stream_flat) * gain_vals[0]).astype(bfloat)
    n_att = n_img // n_hidden
    att_start = lax.axis_index("hidden") * n_att
    normed_att = lax.dynamic_slice_in_dim(
        normed_b.reshape(n_img, seq_len, width), att_start, n_att, 0
    )
    query_gain = lax.dynamic_slice_in_dim(
        gain_vals[2], lax.axis_index("heads") * group_width, group_width, 0
    ).reshape(group_heads, HD)
    key_gain = lax.dynamic_slice_in_dim(
        gain_vals[3], lax.axis_index("heads") * group_width, group_width, 0
    ).reshape(group_heads, HD)
    mixed = jnp.einsum("bsd,dcf->bscf", normed_att, qkv_b, preferred_element_type=single)
    mixed = mixed.reshape(n_att, seq_len, 3, group_heads, HD)
    query_norm, query_back = jax.vjp(layer_norm, mixed[:, :, 0])
    key_norm, key_back = jax.vjp(layer_norm, mixed[:, :, 1])
    queries = (query_norm * query_gain).astype(bfloat)
    keys = (key_norm * key_gain).astype(bfloat)
    values = mixed[:, :, 2].astype(bfloat)
    scale = HD ** (-0.5)
    scores = jnp.einsum("bqhd,bkhd->bhqk", queries, keys, preferred_element_type=single) * scale
    probs = jax.nn.softmax(scores, axis=-1)
    probs_b = probs.astype(bfloat)
    heads_out = jnp.einsum("bhqk,bkhd->bqhd", probs_b, values, preferred_element_type=single)
    heads_out = heads_out.astype(bfloat).reshape(n_att * seq_len, group_width)
    columns = lax.all_to_all(heads_out, "hidden", split_axis=1, concat_axis=0, tiled=True)
    attn_part = jnp.dot(columns, out_b, preferred_element_type=single)
    upper = jnp.dot(normed_b, up_b, preferred_element_type=single)
    activated, gelu_back = jax.vjp(jax.nn.gelu, upper)
    activated_b = activated.astype(bfloat)
    partial_sum = attn_part + jnp.dot(activated_b, down_b, preferred_element_type=single)
    total = lax.psum(partial_sum, ("heads", "hidden"))
    stream_out = (stream_flat + total).reshape(n_img, seq_len, width)
    terms, pooled_b, d_logits, d_stream, d_gain_rows = head_loss(
        stream_out, labels, gain_vals[1], head_b, npatch, total_images
    )
    loss_terms = lax.dynamic_slice_in_dim(terms, own_index * n_own, n_own, 0)
    pooled_own = lax.dynamic_slice_in_dim(pooled_b, own_index * n_own, n_own, 0)
    logits_own = lax.dynamic_slice_in_dim(d_logits, own_index * n_own, n_own, 0)
    d_head = jnp.dot(pooled_own.astype(single).T, logits_own, precision=highest)
    d_final_gain = jnp.sum(
        lax.dynamic_slice_in_dim(d_gain_rows, own_index * n_own, n_own, 0), axis=0
    )
    d_stream_own = lax.dynamic_slice_in_dim(d_stream, own_index * n_own, n_own, 0)
    d_branch = d_stream.reshape(row_count, width).astype(bfloat)
    d_activated = jnp.dot(d_branch, down_b.T, preferred_element_type=single)
    d_upper = gelu_back(d_activated)[0].astype(bfloat)
    d_down = jnp.dot(activated_b.T, d_branch, preferred_element_type=single)
    d_up = jnp.dot(normed_b.T, d_upper, preferred_element_type=single)
    d_normed = jnp.dot(d_upper, up_b.T, preferred_element_type=single)
    d_out = jnp.dot(columns.T, d_branch, preferred_element_type=single)
    d_columns = jnp.dot(d_branch, out_b.T, preferred_element_type=single).astype(bfloat)
    d_heads = lax.all_to_all(d_columns, "hidden", split_axis=0, concat_axis=1, tiled=True).reshape(
        n_att, seq_len, group_heads, HD
    )
    d_probs = jnp.einsum("bqhd,bkhd->bhqk", d_heads, values, preferred_element_type=single)
    d_values = jnp.einsum("bhqk,bqhd->bkhd", probs_b, d_heads, preferred_element_type=single)
    d_scores = (probs * (d_probs - jnp.sum(probs * d_probs, axis=-1, keepdims=True))).astype(bfloat)
    d_query_norm = (
        jnp.einsum("bhqk,bkhd->bqhd", d_scores, keys, preferred_element_type=single) * scale
    )
    d_key_norm = (
        jnp.einsum("bhqk,bqhd->bkhd", d_scores, queries, preferred_element_type=single) * scale
    )
    d_queries = query_back(d_query_norm * query_gain)[0]
    d_keys = key_back(d_key_norm * key_gain)[0]
    d_query_gain = jnp.sum(d_query_norm * query_norm, axis=(0, 1)).reshape(group_width)
    d_key_gain = jnp.sum(d_key_norm * key_norm, axis=(0, 1)).reshape(group_width)
    d_mixed = (
        jnp.stack([d_queries, d_keys, d_values], axis=2)
        .astype(bfloat)
        .reshape(n_att, seq_len, 3, group_width)
    )
    d_qkv = jnp.einsum("bsd,bscf->dcf", normed_att, d_mixed, preferred_element_type=single)
    d_att_in = jnp.einsum("bscf,dcf->bsd", d_mixed, qkv_b, preferred_element_type=single)
    d_normed = d_normed.reshape(n_img, seq_len, width)
    d_normed = lax.dynamic_update_slice_in_dim(
        d_normed, lax.dynamic_slice_in_dim(d_normed, att_start, n_att, 0) + d_att_in, att_start, 0
    )
    d_normed_own = lax.psum_scatter(
        d_normed.reshape(row_count, width).astype(jnp.bfloat16),
        ("heads", "hidden"),
        scatter_dimension=0,
        tiled=True,
    ).astype(jnp.float32)
    d_normed_own = d_normed_own.reshape(n_own, seq_len, width)
    normed_own, block_back = jax.vjp(layer_norm, stream_own.astype(single))
    d_stream_in = d_stream_own + block_back(d_normed_own * gain_vals[0])[0]
    d_block_gain = jnp.sum(d_normed_own * normed_own, axis=(0, 1))
    d_patch = jnp.dot(
        patches.reshape(n_own * npatch, PD).astype(single).T,
        d_stream_in[:, :npatch].reshape(n_own * npatch, width),
        precision=highest,
    )
    d_table = jnp.sum(d_stream_in, axis=0)
    zero_row = jnp.zeros((width,), single)
    gain_offset = lax.axis_index("heads") * group_width
    d_gains = jnp.stack(
        [
            d_block_gain,
            d_final_gain,
            lax.dynamic_update_slice_in_dim(zero_row, d_query_gain, gain_offset, 0),
            lax.dynamic_update_slice_in_dim(zero_row, d_key_gain, gain_offset, 0),
        ]
    )
    grad_patch, grad_table, grad_gains, grad_head = (
        lax.psum_scatter(d_patch, ("dp", "heads", "hidden"), scatter_dimension=1, tiled=True),
        lax.psum_scatter(d_table, ("dp", "heads", "hidden"), scatter_dimension=1, tiled=True),
        lax.psum_scatter(d_gains, ("dp", "heads", "hidden"), scatter_dimension=1, tiled=True),
        lax.psum_scatter(d_head, ("dp", "heads", "hidden"), scatter_dimension=0, tiled=True),
    )
    grad_qkv = lax.psum_scatter(d_qkv, ("dp", "hidden"), scatter_dimension=0, tiled=True)
    grad_out, grad_up, grad_down = (
        lax.psum_scatter(d_out.astype(jnp.bfloat16), "dp", scatter_dimension=1, tiled=True).astype(
            jnp.float32
        ),
        lax.psum_scatter(d_up.astype(jnp.bfloat16), "dp", scatter_dimension=0, tiled=True).astype(
            jnp.float32
        ),
        lax.psum_scatter(d_down.astype(jnp.bfloat16), "dp", scatter_dimension=1, tiled=True).astype(
            jnp.float32
        ),
    )
    grads = [grad_patch, grad_table, grad_gains, grad_head, grad_qkv, grad_out, grad_up, grad_down]
    grad_squares = jnp.stack([jnp.sum(grad * grad) for grad in grads])
    weight_squares = jnp.stack([jnp.sum(master * master) for master in masters])
    grad_squares, weight_squares, loss_sum = lax.psum(
        (grad_squares, weight_squares, jnp.sum(loss_terms)), ("dp", "heads", "hidden")
    )
    grad_norm = jnp.sqrt(jnp.sum(grad_squares))
    clip = jnp.minimum(1.0, clip_at / grad_norm)
    new_firsts, new_seconds, updates = ([], [], [])
    for master, first, second, grad in zip(masters, firsts, seconds, grads):
        clipped = grad * clip
        first_new = beta_one * first + (1.0 - beta_one) * clipped
        second_new = beta_two * second + (1.0 - beta_two) * clipped * clipped
        update = (
            first_new
            / (1.0 - beta_one**STEP)
            / (jnp.sqrt(second_new / (1.0 - beta_two**STEP)) + adam_eps)
        )
        updates.append(update + decay_rate * master)
        new_firsts.append(first_new)
        new_seconds.append(second_new)
    update_squares = lax.psum(
        jnp.stack([jnp.sum(update * update) for update in updates]), ("dp", "heads", "hidden")
    )
    ratios = jnp.sqrt(weight_squares) / jnp.sqrt(update_squares)
    new_weights = [
        master - learn_rate * ratios[number] * update
        for number, (master, update) in enumerate(zip(masters, updates))
    ]
    return (
        loss_sum,
        grad_norm,
        new_firsts[0],
        new_firsts[1],
        new_firsts[2],
        new_firsts[3],
        new_firsts[4],
        new_firsts[5],
        new_firsts[6],
        new_firsts[7],
        new_seconds[0],
        new_seconds[1],
        new_seconds[2],
        new_seconds[3],
        new_seconds[4],
        new_seconds[5],
        new_seconds[6],
        new_seconds[7],
        new_weights[0],
        new_weights[1],
        new_weights[2],
        new_weights[3],
        new_weights[4],
        new_weights[5],
        new_weights[6],
        new_weights[7],
    )


def solution(mesh):
    placed = (
        P(("dp", "heads", "hidden"), None, None),
        P("dp"),
        P(None, ("dp", "heads", "hidden")),
        P(None, ("dp", "heads", "hidden")),
        P(None, ("dp", "heads", "hidden")),
        P(("dp", "heads", "hidden"), None),
        P(("dp", "hidden"), None, "heads"),
        P(("heads", "hidden"), "dp"),
        P("dp", ("heads", "hidden")),
        P(("heads", "hidden"), "dp"),
        P(None, ("dp", "heads", "hidden")),
        P(None, ("dp", "heads", "hidden")),
        P(None, ("dp", "heads", "hidden")),
        P(("dp", "heads", "hidden"), None),
        P(("dp", "hidden"), None, "heads"),
        P(("heads", "hidden"), "dp"),
        P("dp", ("heads", "hidden")),
        P(("heads", "hidden"), "dp"),
        P(None, ("dp", "heads", "hidden")),
        P(None, ("dp", "heads", "hidden")),
        P(None, ("dp", "heads", "hidden")),
        P(("dp", "heads", "hidden"), None),
        P(("dp", "hidden"), None, "heads"),
        P(("heads", "hidden"), "dp"),
        P("dp", ("heads", "hidden")),
        P(("heads", "hidden"), "dp"),
    )
    return jax.shard_map(
        per_device,
        mesh=mesh,
        in_specs=placed,
        out_specs=(
            P(),
            P(),
            P(None, ("dp", "heads", "hidden")),
            P(None, ("dp", "heads", "hidden")),
            P(None, ("dp", "heads", "hidden")),
            P(("dp", "heads", "hidden"), None),
            P(("dp", "hidden"), None, "heads"),
            P(("heads", "hidden"), "dp"),
            P("dp", ("heads", "hidden")),
            P(("heads", "hidden"), "dp"),
            P(None, ("dp", "heads", "hidden")),
            P(None, ("dp", "heads", "hidden")),
            P(None, ("dp", "heads", "hidden")),
            P(("dp", "heads", "hidden"), None),
            P(("dp", "hidden"), None, "heads"),
            P(("heads", "hidden"), "dp"),
            P("dp", ("heads", "hidden")),
            P(("heads", "hidden"), "dp"),
            P(None, ("dp", "heads", "hidden")),
            P(None, ("dp", "heads", "hidden")),
            P(None, ("dp", "heads", "hidden")),
            P(("dp", "heads", "hidden"), None),
            P(("dp", "hidden"), None, "heads"),
            P(("heads", "hidden"), "dp"),
            P("dp", ("heads", "hidden")),
            P(("heads", "hidden"), "dp"),
        ),
        check_vma=False,
    )
```

profile of v0, /device:TPU:0, one launch (start us, length us, event | category | flops | bytes accessed | tf_op | source)
XLA Modules:
  0.0 1191.3 jit_solution(12246861165087383472)
XLA Ops:
  9.6 73.5 %all_gather.28 = bf16[200,768]{0,1:T(8,128)(2,1)S(1)} all-gather(bf16[200,24]{0,1:T(8,128)(2,1)S(1)} %convert_element_type.150), channel_id=1, replica_groups=mesh['dp'=4,'heads'=2,'hidden'=4] {'dp','heads','hidden'}, dimensions={1}, use_global_device_ids=true | all-gather | bytes 316800 | tf_op jit(solution)/shard_map/all_gather | solution.py:101
  83.5 2.0 fusion.34
  88.9 63.7 %all-gather = bf16[32,24,4]{1,2,0:T(4,128)(2,1)S(1)} all-gather(bf16[1,24,4]{1,2,0:T(4,128)(2,1)S(1)} %get-tuple-element.168), channel_id=1, replica_groups=mesh['dp'=4,'heads'=2,'hidden'=4] {'dp','heads','hidden'}, dimensions={0}, use_global_device_ids=true | all-gather | bytes 6336 | tf_op jit(solution)/shard_map/all_gather | solution.py:102
  155.1 6.1 all_gather.32
  161.1 11.2 all_gather.34
  172.3 8.1 all_gather.33
  180.4 2.3 convert_reduce_fusion
  183.4 3.0 broadcast_subtract_fusion
  187.2 3.0 fusion.20
  193.2 4.4 fusion.110
  197.6 2.3 fusion.35
  201.0 2.0 all_to_all.26
  203.0 4.1 all-to-all-start
  213.9 4.1 fusion.91
  219.7 2.1 copy.133
  221.7 2.1 all_to_all.29
  223.8 5.7 convolution_add_fusion
  233.9 168.5 %all-reduce.5.cloned.1.call-done = f32[1600,768]{1,0:T(8,128)} async-done(((f32[1600,768]{1,0:T(8,128)}), f32[1600,768]{1,0:T(8,128)}) %all-reduce.5.cloned.1.call-update) | async-done | bytes 4915216 | tf_op jit(solution)/shard_map/psum | solution.py:161
  402.4 5.2 fusion.106
  407.7 3.1 multiply_reduce_fusion
  410.9 2.9 subtract_multiply_fusion
  414.2 46.0 %all-gather.12.cloned.1.call-done = bf16[768,1000]{1,0:T(8,128)(2,1)} async-done(((bf16[24,1000]{1,0:T(8,128)(2,1)}), bf16[768,1000]{1,0:T(8,128)(2,1)}) %all-gather.12.cloned.1.call-update) | async-done | bytes 1536016 | tf_op jit(solution)/shard_map/all_gather | solution.py:103
  460.2 1.8 fusion.111
  463.5 2.7 convolution_multiply_fusion
  466.6 4.5 fusion.4
  473.0 3.8 fusion.103
  478.4 2.3 all_to_all.30
  482.6 4.1 all-to-all-start.1
  486.9 4.7 fusion.14
  492.7 3.7 fusion.113
  496.4 2.7 all-to-all-done.1
  499.1 2.0 reshape.453
  501.1 4.8 multiply_reduce_fusion.2
  507.2 1.9 copy.143
  509.2 2.9 multiply_convert_fusion.1
  517.1 1.9 copy.141
  519.0 2.3 fusion.36
  521.2 2.2 add_convert_fusion
  524.6 4.2 fusion.28
  528.9 4.1 convert_element_type.176
  535.3 4.5 convolution_convert_fusion.2
  540.1 4.3 convolution_convert_fusion.1
  546.0 1.9 broadcast_multiply_fusion
  548.0 4.5 convolution_bitcast_fusion
  553.7 47.5 %reduce-scatter.14.cloned.1.call-done = bf16[200,768]{1,0:T(8,128)(2,1)} async-done(((bf16[1600,768]{1,0:T(8,128)(2,1)}), bf16[200,768]{1,0:T(8,128)(2,1)}) %reduce-scatter.14.cloned.1.call-update) | async-done | bytes 307216 | tf_op jit(solution)/shard_map/reduce_scatter | solution.py:209
  606.5 2.7 convolution_bitcast_fusion.1
  610.5 12.4 %reduce-scatter.28.cloned.1.call-done = bf16[192,96]{1,0:T(8,128)(2,1)} async-done(((bf16[768,96]{1,0:T(8,128)(2,1)}), bf16[192,96]{1,0:T(8,128)(2,1)}) %reduce-scatter.28.cloned.1.call-update) | async-done | bytes 36880
  624.6 23.0 %reduce-scatter.22.cloned.1.call-done = bf16[192,384]{1,0:T(8,128)(2,1)} async-done(((bf16[768,384]{1,0:T(8,128)(2,1)}), bf16[192,384]{1,0:T(8,128)(2,1)}) %reduce-scatter.22.cloned.1.call-update) | async-done | bytes 147472 | tf_op jit(solution)/shard_map/reduce_scatter | solution.py:246
  649.3 23.2 %reduce-scatter.24.cloned.1.call-done = bf16[384,192]{0,1:T(8,128)(2,1)} async-done(((bf16[384,768]{0,1:T(8,128)(2,1)}), bf16[384,192]{0,1:T(8,128)(2,1)}) %reduce-scatter.24.cloned.1.call-update) | async-done | bytes 147472 | tf_op jit(solution)/shard_map/reduce_scatter | solution.py:249
  674.1 106.0 %reduce-scatter.18.cloned.1.call-done = f32[24,1000]{1,0:T(8,128)} async-done(((f32[768,1000]{1,0:T(8,128)}), f32[24,1000]{1,0:T(8,128)}) %reduce-scatter.18.cloned.1.call-update) | async-done | bytes 96016 | tf_op jit(solution)/shard_map/reduce_scatter | solution.py:239
  781.6 40.3 %all-reduce.1 = f32[4,768]{1,0:T(4,128)S(1)} all-reduce(f32[4,768]{1,0:T(4,128)S(1)} %pad_maximum_fusion.5), channel_id=5, replica_groups=mesh['dp'=4,'heads'=2,'hidden'=4] {'dp','heads','hidden'}, use_global_device_ids=true, to_apply=%region_36.0.clone | all-reduce | flops 3072 | bytes 24576
  822.6 29.5 %reduce-scatter.20.cloned.1.call-done = f32[48,3,384]{2,0,1:T(8,128)} async-done(((f32[768,3,384]{2,0,1:T(8,128)}), f32[48,3,384]{2,0,1:T(8,128)}) %reduce-scatter.20.cloned.1.call-update) | async-done | bytes 221200 | tf_op jit(solution)/shard_map/reduce_scatter | solution.py:241
  853.7 98.5 %reduce-scatter.26.cloned.1.call-done = f32[24,200]{1,0:T(8,128)} async-done(((f32[768,200]{1,0:T(8,128)}), f32[24,200]{1,0:T(8,128)}) %reduce-scatter.26.cloned.1.call-update) | async-done | bytes 19216
  953.6 102.8 %reduce-scatter.16.cloned.1.call-done = f32[768,24]{0,1:T(8,128)} async-done(((f32[768,768]{0,1:T(8,128)}), f32[768,24]{0,1:T(8,128)}) %reduce-scatter.16.cloned.1.call-update) | async-done | bytes 73744 | tf_op jit(solution)/shard_map/reduce_scatter | solution.py:236
  1057.9 5.3 stack.122
  1063.7 39.9 %psum.37 = f32[8]{0:T(128)S(1)} all-reduce(f32[8]{0:T(128)S(1)} %stack.122), channel_id=1, replica_groups=mesh['dp'=4,'heads'=2,'hidden'=4] {'dp','heads','hidden'}, use_global_device_ids=true, to_apply=%region_48.0 | all-reduce | flops 8 | bytes 64 | tf_op jit(solution)/shard_map/psum | solution.py:256
  1107.0 2.0 multiply_reduce_fusion.23
  1109.1 2.2 multiply_reduce_fusion.20
  1113.0 1.9 multiply_reduce_fusion.11
  1114.9 2.2 multiply_reduce_fusion.8
  1117.0 2.2 multiply_reduce_fusion.9
  1119.3 5.2 stack.131
  1124.5 5.2 stack.140
  1129.7 39.5 %all-reduce.2 = (f32[]{:T(128)}, f32[8]{0:T(128)S(1)}, f32[8]{0:T(128)S(1)}) all-reduce(f32[]{:T(128)} %bitcast.17, f32[8]{0:T(128)S(1)} %stack.140, f32[8]{0:T(128)S(1)} %stack.131), channel_id=1, replica_groups=mesh['dp'=4,'heads'=2,'hidden'=4] {'dp','heads','hidden'}, use_global_device_ids=true, to_apply=%region_15.0 | all-reduce | flops 17 | bytes 136 | tf_op jit(solution)/shard_map/psum | solution.py:256
  (322 shorter events, 80.5 us)
Async XLA Ops:
  7.2 76.3 %copy-start = (bf16[1,196,768]{2,1,0:T(8,128)(2,1)S(1)}, bf16[1,196,768]{2,1,0:T(8,128)(2,1)}, u32[]{:S(2)}) copy-start(bf16[1,196,768]{2,1,0:T(8,128)(2,1)} %param.26) | copy-start | bytes 903172
  7.2 76.2 %all-gather.6.cloned.1.call-start = ((), (), s32[]{:S(2)}) async-start(), calls=%async_computation.10 | async-start | bytes 1216512 | tf_op jit(solution)/shard_map/all_gather | solution.py:100
  8.8 171.6 %all-gather.8.cloned.1.call-start = ((), (), s32[]{:S(2)}) async-start(), calls=%async_computation.11 | async-start | bytes 2764800 | tf_op jit(solution)/shard_map/all_gather | solution.py:126
  83.3 69.5 %copy-start.20 = (bf16[200,768]{1,0:T(8,128)(2,1)}, bf16[200,768]{1,0:T(8,128)(2,1)S(1)}, u32[]{:S(2)}) copy-start(bf16[200,768]{1,0:T(8,128)(2,1)S(1)} %copy.124) | copy-start | bytes 921604
  83.3 5.0 copy-start.75
  83.3 71.6 %copy-start.26 = (f32[96,192]{1,0:T(8,128)S(1)}, f32[96,192]{1,0:T(8,128)}, u32[]{:S(2)}) copy-start(f32[96,192]{1,0:T(8,128)} %param.33) | copy-start | bytes 221188
  83.3 71.7 %copy-start.11 = (f32[192,384]{1,0:T(8,128)S(1)}, f32[192,384]{1,0:T(8,128)}, u32[]{:S(2)}) copy-start(f32[192,384]{1,0:T(8,128)} %param.34) | copy-start | bytes 884740
  83.4 71.6 %copy-start.9 = (f32[384,192]{0,1:T(8,128)S(1)}, f32[384,192]{0,1:T(8,128)}, u32[]{:S(2)}) copy-start(f32[384,192]{0,1:T(8,128)} %param.35) | copy-start | bytes 884740
  87.6 99.6 %all-gather.10.cloned.1.call-start = ((), (), s32[]{:S(2)}) async-start(), calls=%async_computation.12 | async-start | bytes 1880064 | tf_op jit(solution)/shard_map/all_gather | solution.py:105
  203.0 16.7 %all-to-all-start = ((bf16[400,4,96]{0,2,1:T(8,128)(2,1)}), bf16[400,4,96]{0,2,1:T(8,128)(2,1)}, u32[]{:S(2)}, u32[]{:S(2)}) async-start(bf16[400,4,96]{0,2,1:T(8,128)(2,1)} %all_to_all.26), calls=%async_computation | async-start | bytes 786432 | tf_op jit(solution)/shard_map/all_to_all | solution.py:155
  207.2 195.2 %all-reduce.5.cloned.1.call-start = ((), (), s32[]{:S(2)}) async-start(), calls=%async_computation.13 | async-start | bytes 9830400 | tf_op jit(solution)/shard_map/psum | solution.py:161
  229.6 230.6 %all-gather.12.cloned.1.call-start = ((), (), s32[]{:S(2)}) async-start(), calls=%async_computation.14 | async-start | bytes 1622016 | tf_op jit(solution)/shard_map/all_gather | solution.py:103
  407.6 63.5 %copy-start.53 = (f32[8,200]{1,0:T(8,128)}, f32[8,200]{1,0:T(8,128)S(1)}, u32[]{:S(2)}) copy-start(f32[8,200]{1,0:T(8,128)S(1)} %div.243) | copy-start | bytes 19204
  410.8 60.3 %copy-start.54 = (f32[8,200]{1,0:T(8,128)}, f32[8,200]{1,0:T(8,128)S(1)}, u32[]{:S(2)}) copy-start(f32[8,200]{1,0:T(8,128)S(1)} %rsqrt.58) | copy-start | bytes 19204
  413.8 48.2 %copy-start.81 = (s32[8]{0:T(128)S(1)}, s32[8]{0:T(128)}, u32[]{:S(2)}) copy-start(s32[8]{0:T(128)} %param.27) | copy-start | bytes 100
  414.2 52.3 %copy-start.70 = (bf16[8,768]{1,0:T(8,128)(2,1)}, bf16[8,768]{1,0:T(8,128)(2,1)S(1)}, u32[]{:S(2)}) copy-start(bf16[8,768]{1,0:T(8,128)(2,1)S(1)} %multiply_convert_fusion.5) | copy-start | bytes 36868
  466.2 4.9 slice-start
  482.6 16.6 %all-to-all-start.1 = ((bf16[4,400,96]{1,2,0:T(8,128)(2,1)}), bf16[4,400,96]{1,2,0:T(8,128)(2,1)}, u32[]{:S(2)}, u32[]{:S(2)}) async-start(bf16[4,400,96]{1,2,0:T(8,128)(2,1)} %copy.135), calls=%async_computation.1 | async-start | bytes 786432 | tf_op jit(solution)/shard_map/all_to_all | solution.py:182
  486.7 114.5 %reduce-scatter.14.cloned.1.call-start = ((), (), s32[]{:S(2)}) async-start(), calls=%async_computation.15 | async-start | bytes 2764800 | tf_op jit(solution)/shard_map/reduce_scatter | solution.py:209
  486.9 5.8 copy-start.16
  501.1 4.8 copy-start.77
  533.0 90.0 %reduce-scatter.28.cloned.1.call-start = ((), (), s32[]{:S(2)}) async-start(), calls=%async_computation.22 | async-start | bytes 245760
  535.3 112.4 %reduce-scatter.22.cloned.1.call-start = ((), (), s32[]{:S(2)}) async-start(), calls=%async_computation.19 | async-start | bytes 737280 | tf_op jit(solution)/shard_map/reduce_scatter | solution.py:246
  539.8 132.6 %reduce-scatter.24.cloned.1.call-start = ((), (), s32[]{:S(2)}) async-start(), calls=%async_computation.20 | async-start | bytes 737280 | tf_op jit(solution)/shard_map/reduce_scatter | solution.py:249
  544.4 235.7 %reduce-scatter.18.cloned.1.call-start = ((), (), s32[]{:S(2)}) async-start(), calls=%async_computation.17 | async-start | bytes 3244032 | tf_op jit(solution)/shard_map/reduce_scatter | solution.py:239
  547.9 304.1 %reduce-scatter.20.cloned.1.call-start = ((), (), s32[]{:S(2)}) async-start(), calls=%async_computation.18 | async-start | bytes 3760128 | tf_op jit(solution)/shard_map/reduce_scatter | solution.py:241
  552.5 48.7 %copy-start.5 = (bf16[196,768]{1,0:T(8,128)(2,1)S(1)}, bf16[196,768]{1,0:T(8,128)(2,1)}, u32[]{:S(2)}) copy-start(bf16[196,768]{1,0:T(8,128)(2,1)} %copy-done.4) | copy-start | bytes 903172
  552.5 399.6 %reduce-scatter.26.cloned.1.call-start = ((), (), s32[]{:S(2)}) async-start(), calls=%async_computation.21 | async-start | bytes 811008
  606.5 18.0 %copy-start.78 = (f32[6,64]{1,0:T(8,128)S(1)}, f32[6,64]{1,0:T(8,128)}, u32[]{:S(2)}) copy-start(f32[6,64]{1,0:T(8,128)} %get-tuple-element.106) | copy-start | bytes 4612
  606.5 18.0 %copy-start.79 = (f32[6,64]{1,0:T(8,128)S(1)}, f32[6,64]{1,0:T(8,128)}, u32[]{:S(2)}) copy-start(f32[6,64]{1,0:T(8,128)} %get-tuple-element.108) | copy-start | bytes 4612
  606.5 449.9 %reduce-scatter.16.cloned.1.call-start = ((), (), s32[]{:S(2)}) async-start(), calls=%async_computation.16 | async-start | bytes 2433024 | tf_op jit(solution)/shard_map/reduce_scatter | solution.py:236
  609.2 453.9 %copy-start.86 = (f32[8]{0:T(128)S(1)}, f32[8]{0:T(128)}, u32[]{:S(2)}) copy-start(f32[8]{0:T(128)} %get-tuple-element.155) | copy-start | bytes 100
  609.2 495.7 %copy-start.76 = (f32[4,24]{1,0:T(4,128)S(1)}, f32[4,24]{1,0:T(4,128)}, u32[]{:S(2)}) copy-start(f32[4,24]{1,0:T(4,128)} %param.30) | copy-start | bytes 1156
  609.3 495.7 %copy-start.84 = (f32[4,24]{1,0:T(4,128)S(1)}, f32[4,24]{1,0:T(4,128)}, u32[]{:S(2)}) copy-start(f32[4,24]{1,0:T(4,128)} %param.38) | copy-start | bytes 1156
  609.3 495.7 %copy-start.85 = (f32[4,24]{1,0:T(4,128)S(1)}, f32[4,24]{1,0:T(4,128)}, u32[]{:S(2)}) copy-start(f32[4,24]{1,0:T(4,128)} %param.46) | copy-start | bytes 1156
  609.3 497.0 %copy-start.27 = (f32[96,192]{1,0:T(8,128)S(1)}, f32[96,192]{1,0:T(8,128)}, u32[]{:S(2)}) copy-start(f32[96,192]{1,0:T(8,128)} %param.33) | copy-start | bytes 221188
  609.3 497.0 %copy-start.62 = (f32[96,192]{1,0:T(8,128)S(1)}, f32[96,192]{1,0:T(8,128)}, u32[]{:S(2)}) copy-start(f32[96,192]{1,0:T(8,128)} %param.41) | copy-start | bytes 221188
  609.3 497.0 %copy-start.63 = (f32[96,192]{1,0:T(8,128)S(1)}, f32[96,192]{1,0:T(8,128)}, u32[]{:S(2)}) copy-start(f32[96,192]{1,0:T(8,128)} %param.49) | copy-start | bytes 221188
  609.3 497.7 %copy-start.50 = (f32[200,24]{0,1:T(8,128)S(1)}, f32[200,24]{0,1:T(8,128)}, u32[]{:S(2)}) copy-start(f32[200,24]{0,1:T(8,128)} %param.29) | copy-start | bytes 57604
  609.3 497.7 %copy-start.73 = (f32[200,24]{0,1:T(8,128)S(1)}, f32[200,24]{0,1:T(8,128)}, u32[]{:S(2)}) copy-start(f32[200,24]{0,1:T(8,128)} %param.37) | copy-start | bytes 57604
  609.3 497.7 %copy-start.74 = (f32[200,24]{0,1:T(8,128)S(1)}, f32[200,24]{0,1:T(8,128)}, u32[]{:S(2)}) copy-start(f32[200,24]{0,1:T(8,128)} %param.45) | copy-start | bytes 57604
  609.3 499.7 %copy-start.31 = (f32[768,24]{0,1:T(8,128)S(1)}, f32[768,24]{0,1:T(8,128)}, u32[]{:S(2)}) copy-start(f32[768,24]{0,1:T(8,128)} %param.28) | copy-start | bytes 221188
  609.3 499.7 %copy-start.66 = (f32[768,24]{0,1:T(8,128)S(1)}, f32[768,24]{0,1:T(8,128)}, u32[]{:S(2)}) copy-start(f32[768,24]{0,1:T(8,128)} %param.36) | copy-start | bytes 221188
  609.4 499.7 %copy-start.67 = (f32[768,24]{0,1:T(8,128)S(1)}, f32[768,24]{0,1:T(8,128)}, u32[]{:S(2)}) copy-start(f32[768,24]{0,1:T(8,128)} %param.44) | copy-start | bytes 221188
  609.4 501.9 %copy-start.28 = (f32[24,1000]{1,0:T(8,128)S(1)}, f32[24,1000]{1,0:T(8,128)}, u32[]{:S(2)}) copy-start(f32[24,1000]{1,0:T(8,128)} %param.31) | copy-start | bytes 288004
  609.4 501.9 %copy-start.64 = (f32[24,1000]{1,0:T(8,128)S(1)}, f32[24,1000]{1,0:T(8,128)}, u32[]{:S(2)}) copy-start(f32[24,1000]{1,0:T(8,128)} %param.39) | copy-start | bytes 288004
  609.4 501.9 %copy-start.65 = (f32[24,1000]{1,0:T(8,128)S(1)}, f32[24,1000]{1,0:T(8,128)}, u32[]{:S(2)}) copy-start(f32[24,1000]{1,0:T(8,128)} %param.47) | copy-start | bytes 288004
  609.4 503.6 %copy-start.18 = (f32[48,3,384]{2,0,1:T(8,128)S(1)}, f32[48,3,384]{2,0,1:T(8,128)}, u32[]{:S(2)}) copy-start(f32[48,3,384]{2,0,1:T(8,128)} %param.32) | copy-start | bytes 663556
  609.4 503.6 %copy-start.51 = (f32[48,3,384]{2,0,1:T(8,128)S(1)}, f32[48,3,384]{2,0,1:T(8,128)}, u32[]{:S(2)}) copy-start(f32[48,3,384]{2,0,1:T(8,128)} %param.40) | copy-start | bytes 663556
  609.4 503.5 %copy-start.52 = (f32[48,3,384]{2,0,1:T(8,128)S(1)}, f32[48,3,384]{2,0,1:T(8,128)}, u32[]{:S(2)}) copy-start(f32[48,3,384]{2,0,1:T(8,128)} %param.48) | copy-start | bytes 663556
  609.5 505.4 %copy-start.10 = (f32[384,192]{0,1:T(8,128)S(1)}, f32[384,192]{0,1:T(8,128)}, u32[]{:S(2)}) copy-start(f32[384,192]{0,1:T(8,128)} %param.35) | copy-start | bytes 884740
  672.4 442.4 %copy-start.38 = (bf16[384,192]{0,1:T(8,128)(2,1)S(1)}, bf16[384,192]{0,1:T(8,128)(2,1)}, u32[]{:S(2)}) copy-start(bf16[384,192]{0,1:T(8,128)(2,1)} %reduce-scatter.24.cloned.1.call-done) | copy-start | bytes 442372
  953.0 164.1 %copy-start.12 = (f32[192,384]{1,0:T(8,128)S(1)}, f32[192,384]{1,0:T(8,128)}, u32[]{:S(2)}) copy-start(f32[192,384]{1,0:T(8,128)} %param.34) | copy-start | bytes 884740
  953.0 164.0 %copy-start.37 = (bf16[192,384]{1,0:T(8,128)(2,1)S(1)}, bf16[192,384]{1,0:T(8,128)(2,1)}, u32[]{:S(2)}) copy-start(bf16[192,384]{1,0:T(8,128)(2,1)} %reduce-scatter.22.cloned.1.call-done) | copy-start | bytes 442372
  1107.0 72.2 %copy-start.40 = (f32[96,192]{1,0:T(8,128)}, f32[96,192]{1,0:T(8,128)S(1)}, u32[]{:S(2)}) copy-start(f32[96,192]{1,0:T(8,128)S(1)} %get-tuple-element.137) | copy-start | bytes 221188
  1107.0 72.2 %copy-start.41 = (f32[96,192]{1,0:T(8,128)}, f32[96,192]{1,0:T(8,128)S(1)}, u32[]{:S(2)}) copy-start(f32[96,192]{1,0:T(8,128)S(1)} %get-tuple-element.138) | copy-start | bytes 221188
  1113.0 66.9 %copy-start.42 = (f32[24,1000]{1,0:T(8,128)}, f32[24,1000]{1,0:T(8,128)S(1)}, u32[]{:S(2)}) copy-start(f32[24,1000]{1,0:T(8,128)S(1)} %get-tuple-element.141) | copy-start | bytes 288004
  1113.0 66.9 %copy-start.43 = (f32[24,1000]{1,0:T(8,128)}, f32[24,1000]{1,0:T(8,128)S(1)}, u32[]{:S(2)}) copy-start(f32[24,1000]{1,0:T(8,128)S(1)} %get-tuple-element.142) | copy-start | bytes 288004
  1114.9 66.6 %copy-start.29 = (f32[48,3,384]{2,0,1:T(8,128)}, f32[48,3,384]{2,0,1:T(8,128)S(1)}, u32[]{:S(2)}) copy-start(f32[48,3,384]{2,0,1:T(8,128)S(1)} %get-tuple-element.139) | copy-start | bytes 663556
  1114.9 66.6 %copy-start.30 = (f32[48,3,384]{2,0,1:T(8,128)}, f32[48,3,384]{2,0,1:T(8,128)S(1)}, u32[]{:S(2)}) copy-start(f32[48,3,384]{2,0,1:T(8,128)S(1)} %get-tuple-element.140) | copy-start | bytes 663556
  1117.0 65.3 %copy-start.21 = (f32[384,192]{0,1:T(8,128)}, f32[384,192]{0,1:T(8,128)S(1)}, u32[]{:S(2)}) copy-start(f32[384,192]{0,1:T(8,128)S(1)} %get-tuple-element.133) | copy-start | bytes 884740
  1117.0 65.3 %copy-start.22 = (f32[384,192]{0,1:T(8,128)}, f32[384,192]{0,1:T(8,128)S(1)}, u32[]{:S(2)}) copy-start(f32[384,192]{0,1:T(8,128)S(1)} %get-tuple-element.134) | copy-start | bytes 884740
  1119.3 63.9 %copy-start.23 = (f32[192,384]{1,0:T(8,128)}, f32[192,384]{1,0:T(8,128)S(1)}, u32[]{:S(2)}) copy-start(f32[192,384]{1,0:T(8,128)S(1)} %get-tuple-element.135) | copy-start | bytes 884740
  1119.3 63.9 %copy-start.24 = (f32[192,384]{1,0:T(8,128)}, f32[192,384]{1,0:T(8,128)S(1)}, u32[]{:S(2)}) copy-start(f32[192,384]{1,0:T(8,128)S(1)} %get-tuple-element.136) | copy-start | bytes 884740
  (41 other events, 89.8 us)
Sparse Core Ops, SparseCore 0:
  11.4 56.9 all-gather.5
  87.7 49.6 all-gather.7
  140.2 39.9 all-gather.9
  229.7 172.6 all-reduce.4
  406.1 54.0 all-gather.11
  533.1 68.0 reduce-scatter.13
  604.4 18.5 reduce-scatter.27
  625.6 22.0 reduce-scatter.21
  650.3 22.0 reduce-scatter.23
  678.6 101.4 reduce-scatter.17
  784.5 67.5 reduce-scatter.19
  857.9 94.2 reduce-scatter.25
  958.3 98.0 reduce-scatter.15
where the time goes:
time: 1200 us; the launch traced here: 1190 us
  waiting for transfers between devices  662 us (55%)
  blocking collectives  282 us (24%)
  other arithmetic  94.4 us (8%)
  matrix products  66.2 us (6%)
  local copies, waits for them, and re-layouts  54.3 us (5%)
  between operations  22.4 us (2%)
    psum x1, waiting for transfers between devices, per_device(): total = lax.psum(partial_sum, ('heads', 'hidden'))  168 us
    unnamed x15, waiting for transfers between devices  111 us
    reduce_scatter x1, waiting for transfers between devices, per_device(): lax.psum_scatter(d_head, ('dp', 'heads', 'hidden'), scatter_dimension=0,...  106 us
    reduce_scatter x1, waiting for transfers between devices, per_device(): lax.psum_scatter(d_patch, ('dp', 'heads', 'hidden'), scatter_dimension=1,...  103 us
    psum x2, blocking collectives, per_device(): lax.psum((grad_squares, weight_squares, jnp.sum(loss_terms)), ('dp', 'hea...  79.4 us
    all_gather x1, blocking collectives, per_device(): lax.all_gather(table.astype(bfloat), ('dp', 'heads', 'hidden'), axis=1, t...  73.5 us
    all_gather x1, blocking collectives, per_device(): lax.all_gather(gains.astype(bfloat), ('dp', 'heads', 'hidden'), axis=1, t...  63.7 us
    reduce_scatter x1, waiting for transfers between devices, per_device(): lax.psum_scatter(d_normed.reshape(row_count, width).astype(jnp.bfloat16),...  47.5 us
  transfers between devices with their start and end apart: 15, of which 12 were waited for; matrix products, arithmetic and copies ran while one was open for 7% of the time, Pallas kernels for 0%

commit v1 on v0

--- a/solution.py
+++ b/solution.py
@@ -1,11 +1,20 @@
+import functools
+import types
+
 import jax
 import jax.numpy as jnp
 from jax import lax
+from jax.experimental import pallas as pl
+from jax.experimental.pallas import tpu as pltpu
 from jax.sharding import PartitionSpec as P
 
 HD = 64
 PD = 768
 STEP = 10
+MESH = pl.DeviceIdType.MESH
+ALL = ("dp", "heads", "hidden")
+DATA = ("dp", "hidden")
+MODEL = ("heads", "hidden")
 
 
 beta_one = 0.9
@@ -97,12 +106,12 @@
     bfloat = jnp.bfloat16
     single = jnp.float32
     patch_b, table_b, gains_b, head_b = (
-        lax.all_gather(w_patch.astype(bfloat), ("dp", "heads", "hidden"), axis=1, tiled=True),
-        lax.all_gather(table.astype(bfloat), ("dp", "heads", "hidden"), axis=1, tiled=True),
-        lax.all_gather(gains.astype(bfloat), ("dp", "heads", "hidden"), axis=1, tiled=True),
-        lax.all_gather(w_head.astype(bfloat), ("dp", "heads", "hidden"), axis=0, tiled=True),
-    )
-    qkv_b = lax.all_gather(w_qkv.astype(bfloat), ("dp", "hidden"), axis=0, tiled=True)
+        lax.all_gather(w_patch.astype(bfloat), ALL, axis=1, tiled=True),
+        lax.all_gather(table.astype(bfloat), ALL, axis=1, tiled=True),
+        lax.all_gather(gains.astype(bfloat), ALL, axis=1, tiled=True),
+        lax.all_gather(w_head.astype(bfloat), ALL, axis=0, tiled=True),
+    )
+    qkv_b = lax.all_gather(w_qkv.astype(bfloat), DATA, axis=0, tiled=True)
     out_b, up_b, down_b = (
         lax.all_gather(w_out.astype(bfloat), "dp", axis=1, tiled=True),
         lax.all_gather(w_up.astype(bfloat), "dp", axis=0, tiled=True),
@@ -123,7 +132,7 @@
     embedded = embedded.reshape(n_own, npatch, width) + table_vals[:npatch]
     registers = jnp.broadcast_to(table_vals[npatch:], (n_own, seq_len - npatch, width))
     stream_own = jnp.concatenate([embedded, registers], axis=1).astype(bfloat)
-    stream_in = lax.all_gather(stream_own, ("heads", "hidden"), axis=0, tiled=True)
+    stream_in = lax.all_gather(stream_own, MODEL, axis=0, tiled=True)
     n_img = stream_in.shape[0]
     row_count = n_img * seq_len
     stream_flat = stream_in.astype(single).reshape(row_count, width)
@@ -158,7 +167,7 @@
     activated, gelu_back = jax.vjp(jax.nn.gelu, upper)
     activated_b = activated.astype(bfloat)
     partial_sum = attn_part + jnp.dot(activated_b, down_b, preferred_element_type=single)
-    total = lax.psum(partial_sum, ("heads", "hidden"))
+    total = lax.psum(partial_sum, MODEL)
     stream_out = (stream_flat + total).reshape(n_img, seq_len, width)
     terms, pooled_b, d_logits, d_stream, d_gain_rows = head_loss(
         stream_out, labels, gain_vals[1], head_b, npatch, total_images
@@ -208,7 +217,7 @@
     )
     d_normed_own = lax.psum_scatter(
         d_normed.reshape(row_count, width).astype(jnp.bfloat16),
-        ("heads", "hidden"),
+        MODEL,
         scatter_dimension=0,
         tiled=True,
     ).astype(jnp.float32)
@@ -233,12 +242,12 @@
         ]
     )
     grad_patch, grad_table, grad_gains, grad_head = (
-        lax.psum_scatter(d_patch, ("dp", "heads", "hidden"), scatter_dimension=1, tiled=True),
-        lax.psum_scatter(d_table, ("dp", "heads", "hidden"), scatter_dimension=1, tiled=True),
-        lax.psum_scatter(d_gains, ("dp", "heads", "hidden"), scatter_dimension=1, tiled=True),
-        lax.psum_scatter(d_head, ("dp", "heads", "hidden"), scatter_dimension=0, tiled=True),
-    )
-    grad_qkv = lax.psum_scatter(d_qkv, ("dp", "hidden"), scatter_dimension=0, tiled=True)
+        lax.psum_scatter(d_patch, ALL, scatter_dimension=1, tiled=True),
+        lax.psum_scatter(d_table, ALL, scatter_dimension=1, tiled=True),
+        lax.psum_scatter(d_gains, ALL, scatter_dimension=1, tiled=True),
+        lax.psum_scatter(d_head, ALL, scatter_dimension=0, tiled=True),
+    )
+    grad_qkv = lax.psum_scatter(d_qkv, DATA, scatter_dimension=0, tiled=True)
     grad_out, grad_up, grad_down = (
         lax.psum_scatter(d_out.astype(jnp.bfloat16), "dp", scatter_dimension=1, tiled=True).astype(
             jnp.float32
@@ -254,7 +263,7 @@
     grad_squares = jnp.stack([jnp.sum(grad * grad) for grad in grads])
     weight_squares = jnp.stack([jnp.sum(master * master) for master in masters])
     grad_squares, weight_squares, loss_sum = lax.psum(
-        (grad_squares, weight_squares, jnp.sum(loss_terms)), ("dp", "heads", "hidden")
+        (grad_squares, weight_squares, jnp.sum(loss_terms)), ALL
     )
     grad_norm = jnp.sqrt(jnp.sum(grad_squares))
     clip = jnp.minimum(1.0, clip_at / grad_norm)
@@ -272,7 +281,7 @@
         new_firsts.append(first_new)
         new_seconds.append(second_new)
     update_squares = lax.psum(
-        jnp.stack([jnp.sum(update * update) for update in updates]), ("dp", "heads", "hidden")
+        jnp.stack([jnp.sum(update * update) for update in updates]), ALL
     )
     ratios = jnp.sqrt(weight_squares) / jnp.sqrt(update_squares)
     new_weights = [
@@ -309,66 +318,901 @@
     )
 
 
+def dot(a, b):
+    return jnp.dot(a, b, preferred_element_type=jnp.float32)
+
+
+def dot_nt(a, b, precision=None):
+    return lax.dot_general(
+        a, b, (((1,), (1,)), ((), ())), precision=precision, preferred_element_type=jnp.float32
+    )
+
+
+def dot_tn(a, b, precision=None):
+    return lax.dot_general(
+        a, b, (((0,), (0,)), ((), ())), precision=precision, preferred_element_type=jnp.float32
+    )
+
+
+def norm_parts(values):
+    center = values - jnp.mean(values, axis=-1, keepdims=True)
+    scale = lax.rsqrt(jnp.mean(center * center, axis=-1, keepdims=True) + norm_eps)
+    return center * scale, scale
+
+
+def norm_back(normed, scale, grad):
+    inner = jnp.mean(grad * normed, axis=-1, keepdims=True)
+    return scale * (grad - jnp.mean(grad, axis=-1, keepdims=True) - normed * inner)
+
+
+gelu_c = 0.7978845608028654
+
+
+def gelu_tanh(u):
+    return jnp.tanh(gelu_c * (u + 0.044715 * (u * u * u)))
+
+
+def iota(shape, axis):
+    return lax.broadcasted_iota(jnp.int32, shape, axis)
+
+
+def one_update(master, first, second, grad, clip):
+    clipped = grad * clip
+    first_new = beta_one * first + (1.0 - beta_one) * clipped
+    second_new = beta_two * second + (1.0 - beta_two) * clipped * clipped
+    update = (
+        first_new
+        / (1.0 - beta_one**STEP)
+        / (jnp.sqrt(second_new / (1.0 - beta_two**STEP)) + adam_eps)
+    )
+    return first_new, second_new, update + decay_rate * master
+
+
+def square_sum(values):
+    return jnp.sum(values * values, axis=(0, 1), keepdims=True)
+
+
+KINDS = ("patch", "table", "gains", "head", "qkv", "out", "up", "down")
+ROWS = 208
+N_HID = 4
+
+
+def step_kernel(sizes, names, *refs):
+    npatch, seq_len, classes, total_images = sizes
+    r = types.SimpleNamespace(**dict(zip(names, refs)))
+    bfloat, single = jnp.bfloat16, jnp.float32
+    dp, h, z = (lax.axis_index(a) for a in ALL)
+    core, y = lax.rem(dp, 2), dp // 2
+    y_dp, core_dp = (1 - y) * 2 + core, y * 2 + (1 - core)
+    x_dev, y_dev, core_dev = (dp, 1 - h, z), (y_dp, h, z), (core_dp, h, z)
+    z_up = [lax.rem(z + k, N_HID) for k in range(N_HID)]
+    z_down = [lax.rem(z + N_HID - k, N_HID) for k in range(N_HID)]
+    z_dev = [(dp, h, z_up[k]) for k in range(N_HID)]
+    group = []
+    for a in (0, 1):
+        for b in (0, 1):
+            for c in (0, 1):
+                if a + b + c:
+                    gh = 1 - h if a else h
+                    gy = 1 - y if b else y
+                    gc = 1 - core if c else core
+                    group.append((gh, gy * 2 + gc))
+    group_dev = [(gd, gh, z) for gh, gd in group]
+
+    barrier = pltpu.get_barrier_semaphore()
+    for device in z_dev[1:] + group_dev:
+        pl.semaphore_signal(barrier, inc=1, device_id=device, device_id_type=MESH)
+
+    ssem, rsem = r.ssem, r.rsem
+    count = [0]
+    sends = []
+
+    def send(source, target, device):
+        number = count[0]
+        count[0] += 1
+        copy = pltpu.make_async_remote_copy(
+            src_ref=source,
+            dst_ref=target,
+            send_sem=ssem.at[number],
+            recv_sem=rsem.at[number],
+            device_id=device,
+            device_id_type=MESH,
+        )
+        copy.start()
+        sends.append(copy)
+        return number
+
+    def arrive(target, number, device):
+        pltpu.make_async_remote_copy(
+            src_ref=target,
+            dst_ref=target,
+            send_sem=ssem.at[number],
+            recv_sem=rsem.at[number],
+            device_id=device,
+            device_id_type=MESH,
+        ).wait_recv()
+
+    gext, gqkv, gout, gup, gdn, ghd = r.gext, r.gqkv, r.gout, r.gup, r.gdn, r.ghd
+    x0, x1 = r.x0, r.x1
+    x1[0:24, :] = jnp.zeros((24, 512), single)
+    x1[0:24, 256 : 256 + seq_len] = r.w_table[...]
+    pick = (iota((4, 256), 1) == iota((4, 256), 0) + seq_len).astype(bfloat)
+    table_part = x1[0:24, 256:512] + dot_tn(r.w_gains[...].astype(bfloat), pick)
+    wp = r.w_patch[...]
+    gext[dp, z] = jnp.concatenate(
+        [wp[:, 0:512], jnp.concatenate([wp[:, 512:768], table_part], axis=1)], axis=0
+    ).astype(bfloat)
+    gqkv[:, z // 2, dp, lax.rem(z, 2)] = r.w_qkv[...].astype(bfloat)
+    gup[z, :, dp] = r.w_up[...].astype(bfloat).reshape(2, 96, 384)
+    gdn[z, :, dp] = r.w_down[...].astype(bfloat).reshape(2, 96, 384)
+    gout[dp, z] = jnp.zeros((96, 256), bfloat)
+    gout[dp, z, :, 0:192] = r.w_out[...].astype(bfloat)
+    x0[0:24, :] = r.w_head[:, 0:512]
+    x1[0:24, :] = jnp.zeros((24, 512), single)
+    x1[0:24, 0 : classes - 512] = r.w_head[:, 512:classes]
+    ghd[h, dp, z] = jnp.concatenate([x0[0:24, :], x1[0:24, :]], axis=0).astype(bfloat)
+    px = r.px
+    row, col = iota((ROWS, 256), 0), iota((ROWS, 256), 1)
+    spot = jnp.where((row == col) & (row < seq_len), 1.0, 0.0).astype(bfloat)
+    px[0, :, 768:1024] = spot
+    px[1, :, 768:1024] = spot
+    px[0, :, 0:768] = jnp.zeros((ROWS, 768), bfloat)
+    px[0, 0:npatch, 0:768] = r.patches[0]
+
+    pl.semaphore_wait(barrier, len(z_dev) - 1 + len(group_dev))
+
+    def at_ext(d, w):
+        return gext.at[d, w]
+
+    def at_qkv(d, w):
+        return gqkv.at[:, w // 2, d, lax.rem(w, 2)]
+
+    def at_out(d, w):
+        return gout.at[d, w]
+
+    def at_up(half):
+        return lambda d, w: gup.at[w, half, d]
+
+    def at_dn(half):
+        return lambda d, w: gdn.at[w, half, d]
+
+    def at_hd(d, w):
+        return ghd.at[h, d, w]
+
+    slot = {
+        "ext": at_ext,
+        "qkv": at_qkv,
+        "out": at_out,
+        "up0": at_up(0),
+        "up1": at_up(1),
+        "dn0": at_dn(0),
+        "dn1": at_dn(1),
+        "hd": at_hd,
+    }
+    lines = {
+        "ext": lambda d: gext.at[d],
+        "qkv": lambda d: gqkv.at[:, :, d],
+        "out": lambda d: gout.at[d],
+        "up0": lambda d: gup.at[:, 0, d],
+        "up1": lambda d: gup.at[:, 1, d],
+        "dn0": lambda d: gdn.at[:, 0, d],
+        "dn1": lambda d: gdn.at[:, 1, d],
+        "hd": lambda d: ghd.at[h, d],
+    }
+    tags = {}
+
+    def first_send(name):
+        at = slot[name]
+        own = at(dp, z)
+        for k in range(1, N_HID):
+            tags[name, "z", k] = send(own, own, z_dev[k])
+        tags[name, "y", 0] = send(own, own, y_dev)
+
+    def pass_on(name):
+        at = slot[name]
+        for k in range(1, N_HID):
+            theirs = at(dp, z_down[k])
+            arrive(theirs, tags[name, "z", k], z_dev[k])
+            tags[name, "y", k] = send(theirs, theirs, y_dev)
+        if name != "hd":
+            line = lines[name](dp)
+            tags[name, "c", 0] = send(line, line, core_dev)
+
+    def pass_core(name):
+        at = slot[name]
+        for k in range(N_HID):
+            arrive(at(y_dp, z_down[k]), tags[name, "y", k], y_dev)
+        line = lines[name](y_dp)
+        if name != "hd":
+            tags[name, "c", 1] = send(line, line, core_dev)
+        else:
+            own = lines[name](dp)
+            tags[name, "x", 0] = send(own, own, x_dev)
+            tags[name, "x", 1] = send(line, line, x_dev)
+
+    def complete(name):
+        far = (1 - y) * 2 + (1 - core)
+        arrive(lines[name](core_dp), tags[name, "c", 0], core_dev)
+        arrive(lines[name](far), tags[name, "c", 1], core_dev)
+
+    def head_core():
+        for i, d in enumerate((dp, y_dp)):
+            arrive(ghd.at[1 - h, d], tags["hd", "x", i], x_dev)
+        for i, d in enumerate((dp, y_dp)):
+            block = ghd.at[:, d]
+            tags["hd", "c", i] = send(block, block, core_dev)
+
+    def head_complete():
+        far = (1 - y) * 2 + (1 - core)
+        for i, d in enumerate((core_dp, far)):
+            arrive(ghd.at[:, d], tags["hd", "c", i], core_dev)
+
+    first_send("ext")
+    images = px.at[0, :, pl.ds(0, 768)]
+    tag_px = send(images, px.at[1, :, pl.ds(0, 768)], x_dev)
+    first_send("qkv")
+    pass_on("ext")
+    first_send("up0")
+    pass_core("ext")
+    complete("ext")
+
+    for d in range(4):
+        for w in range(N_HID):
+            s = (d * N_HID + w) * 24
+            block = gext[d, w].astype(single)
+            x0[s : s + 24, :] = block[0:24]
+            x1[s : s + 24, :] = block[24:48]
+    x1b = x1[...].astype(bfloat)
+    ga = r.ga
+    rows_of = (iota((8, 512), 1) == iota((8, 512), 0) + (256 + seq_len)) & (iota((8, 512), 0) < 4)
+    ga[h] = dot_nt(rows_of.astype(bfloat), x1b)
+    tag_ga = send(ga.at[h], ga.at[h], x_dev)
+    x0b = x0[...].astype(bfloat)
+    st = r.st
+    st[h, 0] = (dot_nt(px[0, :, 0:512], x0b) + dot_nt(px[0, :, 512:1024], x1b)).astype(bfloat)
+    tag_st0 = send(st.at[h, 0], st.at[h, 1], x_dev)
+    arrive(px.at[1, :, pl.ds(0, 768)], tag_px, x_dev)
+    st[h, 1] = (dot_nt(px[1, :, 0:512], x0b) + dot_nt(px[1, :, 512:1024], x1b)).astype(bfloat)
+    tag_st1 = send(st.at[h, 1], st.at[h, 0], x_dev)
+    pass_on("qkv")
+    first_send("up1")
+    arrive(ga.at[1 - h], tag_ga, x_dev)
+    arrive(st.at[1 - h, 1], tag_st0, x_dev)
+    arrive(st.at[1 - h, 0], tag_st1, x_dev)
+
+    def gain_row(i):
+        return jnp.concatenate([ga[0, i : i + 1, :], ga[1, i : i + 1, :]], axis=1)
+
+    def head_gain(i):
+        pieces = []
+        both = [ga[0, i : i + 1, :], ga[1, i : i + 1, :]]
+        for d in range(4):
+            pieces.extend(half[:, d * 96 : d * 96 + 96] for half in both)
+        low = jnp.concatenate(pieces[0:4], axis=1)
+        high = jnp.concatenate(pieces[4:8], axis=1)
+        return jnp.where(h == 0, low, high)
+
+    nb, nbt = r.nb, r.nbt
+    block_gain = gain_row(0)
+    for i in range(2):
+        stream = jnp.concatenate([st[0, i], st[1, i]], axis=1).astype(single)
+        nb[i * ROWS : (i + 1) * ROWS, :] = (norm_parts(stream)[0] * block_gain).astype(bfloat)
+    pass_core("qkv")
+    first_send("hd")
+    pass_on("up0")
+    first_send("out")
+    complete("qkv")
+
+    qn, kn, qr, kr = r.qn, r.kn, r.qr, r.kr
+    q_ref, k_ref, v_ref = r.q, r.k, r.v
+    q_gain, k_gain = head_gain(2), head_gain(3)
+    for c, (keep, scales, out, gain) in enumerate(
+        ((qn, qr, q_ref, q_gain), (kn, kr, k_ref, k_gain), (None, None, v_ref, None))
+    ):
+        mixed = dot(nb[...], gqkv[c].reshape(768, 384))
+        for n in range(6):
+            part = mixed[:, n * HD : (n + 1) * HD]
+            if keep is not None:
+                part, scale = norm_parts(part)
+                keep[n] = part
+                scales[n] = scale
+                part = part * gain[:, n * HD : (n + 1) * HD]
+            part = part.astype(bfloat)
+            out[2 * n] = part[0:ROWS]
+            out[2 * n + 1] = part[ROWS : 2 * ROWS]
+        if c == 0:
+            pass_on("up1")
+            first_send("dn0")
+
+    pr, ho = r.pr, r.ho
+    dead = iota((ROWS, ROWS), 1) >= seq_len
+
+    def attend(i, carry):
+        scores = dot_nt(q_ref[i], k_ref[i]) * HD ** (-0.5)
+        scores = jnp.where(dead, -1e30, scores)
+        scores = scores - jnp.max(scores, axis=-1, keepdims=True)
+        weights = jnp.exp(scores)
+        probs = weights / jnp.sum(weights, axis=-1, keepdims=True)
+        pr[i] = probs
+        ho[i] = dot(probs.astype(bfloat), v_ref[i])
+        return carry
+
+    lax.fori_loop(0, 4, attend, 0)
+    pass_core("up0")
+    pass_on("hd")
+    first_send("dn1")
+    lax.fori_loop(4, 8, attend, 0)
+    pass_on("out")
+    lax.fori_loop(8, 12, attend, 0)
+    pass_core("up1")
+    pass_core("hd")
+    hof = r.hof
+    for i in range(2):
+        joined = jnp.concatenate([ho[2 * n + i] for n in range(6)], axis=1)
+        hof[i * ROWS : (i + 1) * ROWS, :] = joined.astype(bfloat)
+    complete("up0")
+    complete("up1")
+    pass_on("dn0")
+
+    us, hb, br = r.us, r.hb, r.br
+
+    def rise(w, carry):
+        upper = dot(nb[...], gup[w].reshape(768, 384))
+        us[w] = upper
+        hb[w] = (0.5 * upper * (1.0 + gelu_tanh(upper))).astype(bfloat)
+        return carry
+
+    lax.fori_loop(0, N_HID, rise, 0)
+    head_core()
+    pass_core("out")
+    pass_on("dn1")
+    complete("out")
+    lefts, rights = [], []
+    for d in range(4):
+        part = dot(hof[...], gout[d].reshape(384, 256))
+        lefts.append(part[:, 0:96])
+        rights.append(part[:, 96:192])
+    br[:, 0:384] = jnp.concatenate(lefts, axis=1)
+    br[:, 384:768] = jnp.concatenate(rights, axis=1)
+    nbt[...] = nb[...].T
+    brs, brr = r.brs, r.brr
+    tag_br = []
+    for half in range(2):
+        name = "dn%d" % half
+        lanes = slice(half * 384, half * 384 + 384)
+        pass_core(name)
+        complete(name)
+
+        def fall(w, carry):
+            br[:, lanes] += dot_nt(hb[w], gdn[w, half].reshape(384, 384))
+            return carry
+
+        lax.fori_loop(0, N_HID, fall, 0)
+        brs[half] = br[ROWS : 2 * ROWS, lanes].astype(bfloat)
+        tag_br.append(send(brs.at[half], brr.at[half], x_dev))
+    head_complete()
+    x2, x3 = r.x2, r.x3
+    for a in range(2):
+        for d in range(4):
+            for w in range(N_HID):
+                s = (a * 16 + d * 4 + w) * 24
+                block = ghd[a, d, w].astype(single)
+                x2[s : s + 24, :] = block[0:24]
+                x3[s : s + 24, :] = block[24:48]
+    for half in range(2):
+        arrive(brr.at[half], tag_br[half], x_dev)
+
+    stream0 = jnp.concatenate([st[0, 0], st[1, 0]], axis=1).astype(single)
+    theirs = jnp.concatenate([brr[0], brr[1]], axis=1).astype(single)
+    out_n, out_scale = norm_parts(stream0 + (br[0:ROWS, :] + theirs))
+    is_patch = iota((ROWS, 1), 0) < npatch
+    final_gain = gain_row(1)
+    n_sum = jnp.sum(jnp.where(is_patch, out_n, 0.0), axis=0, keepdims=True)
+    pooled = n_sum * final_gain / npatch
+    pooled_b = pooled.astype(bfloat)
+    heads_b = [x2[...].astype(bfloat), x3[...].astype(bfloat)]
+    pooled_8 = jnp.broadcast_to(pooled_b, (16, 768))
+    logits = jnp.concatenate([dot(pooled_8, m)[0:1] for m in heads_b], axis=1)
+    lane = iota((1, 1024), 1)
+    logits = jnp.where(lane < classes, logits, -1e30)
+    top = jnp.max(logits, axis=-1, keepdims=True)
+    log_total = top + jnp.log(jnp.sum(jnp.exp(logits - top), axis=-1, keepdims=True))
+    onehot = jnp.where(lane == r.labels[h * N_HID + z], 1.0, 0.0)
+    term = log_total - jnp.sum(jnp.where(lane < classes, logits, 0.0) * onehot, axis=-1, keepdims=True)
+    d_logits = (jnp.exp(logits - log_total) - onehot) / total_images
+    hi = d_logits.astype(bfloat).astype(single)
+    both = jnp.concatenate([hi, d_logits - hi, jnp.zeros((14, 1024), single)], axis=0).astype(bfloat)
+    back = dot_nt(both[:, 0:512], heads_b[0]) + dot_nt(both[:, 512:1024], heads_b[1])
+    d_pooled = (back[0:1] + back[1:2]) / npatch
+    d_row = d_pooled * final_gain
+    d_stream = jnp.where(is_patch, norm_back(out_n, out_scale, d_row), 0.0)
+    ds, db, dbt = r.ds, r.db, r.dbt
+    ds[...] = d_stream
+    db[0] = d_stream.astype(bfloat)
+    tag_db = send(db.at[0], db.at[1], x_dev)
+    d_final_gain = d_pooled * n_sum
+    al = r.al
+    pooled_f = pooled_b.astype(single)
+    al[h, dp, z] = jnp.concatenate(
+        [d_logits[:, q * 256 : q * 256 + 256] for q in range(4)]
+        + [pooled_f[:, q * 256 : q * 256 + 256] for q in range(3)]
+        + [jnp.zeros((1, 256), single)],
+        axis=0,
+    )
+    tag_al = [send(al.at[h, dp, z], al.at[h, dp, z], z_dev[k]) for k in range(1, N_HID)]
+    dbt[:, 0:ROWS] = d_stream.T.astype(bfloat)
+    arrive(db.at[1], tag_db, x_dev)
+    dbt[:, ROWS : 2 * ROWS] = db[1].astype(single).T.astype(bfloat)
+    db2 = db[...].reshape(2 * ROWS, 768)
+
+    rff, f1, f2, ft, f3 = r.rff, r.f1, r.f2, r.ft, r.f3
+    dn = br
+    ff_tags = {}
+
+    def ff_block(k):
+        w = z_up[k]
+        upper = us[w]
+        t = gelu_tanh(upper)
+        slope = 0.5 * (1.0 + t) + 0.5 * upper * (1.0 - t * t) * gelu_c * (
+            1.0 + 3 * 0.044715 * (upper * upper)
+        )
+        d_hidden = dot(db2, gdn[w].reshape(768, 384))
+        d_upper = (d_hidden * slope).astype(bfloat)
+        rff[k, 1] = dot(dbt[...], hb[w]).astype(bfloat).reshape(2, 2, 2, 96, 384)
+        rff[k, 0] = dot(nbt[...], d_upper).astype(bfloat).reshape(2, 2, 2, 96, 384)
+        ff_tags[k, 0] = send(rff.at[k, :, :, :, 1 - core], f1.at[k], core_dev)
+        part = dot_nt(d_upper, gup[w].reshape(768, 384))
+        if k == 1:
+            dn[...] = part
+        else:
+            dn[...] += part
+
+    def ff_y(k):
+        arrive(f1.at[k], ff_tags[k, 0], core_dev)
+        f1[k] = f1[k] + rff[k, :, :, :, core]
+        ff_tags[k, 1] = send(f1.at[k, :, :, 1 - y], f2.at[k], y_dev)
+
+    def ff_z(k):
+        arrive(f2.at[k], ff_tags[k, 1], y_dev)
+        if k:
+            ft[k - 1] = f1[k, :, :, y] + f2[k]
+            ff_tags[k, 2] = send(ft.at[k - 1], f3.at[k - 1], z_dev[k])
+
+    def ff_end():
+        total = f1[0, :, :, y].astype(single) + f2[0].astype(single)
+        for k in range(1, N_HID):
+            arrive(f3.at[k - 1], ff_tags[k, 2], z_dev[k])
+            total = total + f3[k - 1].astype(single)
+        r.g_up[...] = total[0].reshape(192, 384)
+        r.g_down[...] = total[1].reshape(192, 384)
+
+    ff_block(1)
+    ff_block(2)
+    ff_y(1)
+    for k in range(1, N_HID):
+        arrive(al.at[h, dp, z_down[k]], tag_al[k - 1], z_dev[k])
+    tag_ag = [send(al.at[h, dp], al.at[h, dp], device) for device in group_dev]
+    ff_block(3)
+    ff_y(2)
+    ff_z(1)
+    ff_block(0)
+    ff_y(3)
+    ff_z(2)
+
+    rout, o1, o2, ot, o3 = r.rout, r.o1, r.o2, r.ot, r.o3
+    pieces = [
+        jnp.concatenate([db2[:, d * 96 : d * 96 + 96], db2[:, 384 + d * 96 : 384 + d * 96 + 96]], axis=1)
+        for d in range(4)
+    ]
+    hot = hof[...].T
+    d_heads = None
+    for d in range(4):
+        rout[:, d // 2, d % 2] = jnp.zeros((N_HID, 96, 256), bfloat)
+        rout[:, d // 2, d % 2, :, 0:192] = dot(hot, pieces[d]).astype(bfloat).reshape(N_HID, 96, 192)
+        part = dot_nt(pieces[d], gout[d].reshape(384, 256)[:, 0:192])
+        d_heads = part if d_heads is None else d_heads + part
+    tag_o1 = send(rout.at[:, :, 1 - core], o1, core_dev)
+    dh = r.dh
+    for n in range(6):
+        part = d_heads[:, n * HD : (n + 1) * HD].astype(bfloat)
+        dh[2 * n] = part[0:ROWS]
+        dh[2 * n + 1] = part[ROWS : 2 * ROWS]
+    ff_y(0)
+
+    dq, dk, dv = ho, r.dk, r.dv
+
+    def attend_back(i, carry):
+        probs = pr[i]
+        d_out = dh[i]
+        d_probs = dot_nt(d_out, v_ref[i])
+        dv[i] = dot_tn(probs.astype(bfloat), d_out)
+        inner = jnp.sum(probs * d_probs, axis=-1, keepdims=True)
+        d_scores = (probs * (d_probs - inner)).astype(bfloat)
+        dq[i] = dot(d_scores, k_ref[i]) * HD ** (-0.5)
+        dk[i] = dot_tn(d_scores, q_ref[i]) * HD ** (-0.5)
+        return carry
+
+    lax.fori_loop(0, 4, attend_back, 0)
+    ff_z(3)
+    arrive(o1, tag_o1, core_dev)
+    o1[...] = o1[...] + rout[:, :, core]
+    tag_o2 = send(o1.at[:, 1 - y], o2, y_dev)
+    lax.fori_loop(4, 8, attend_back, 0)
+    ff_z(0)
+    lax.fori_loop(8, 12, attend_back, 0)
+
+    rqkv, q1, q2, qt, q3 = r.rqkv, r.q1, r.q2, r.qt, r.q3
+    gain_sums = []
+    for c, (grads, normed, scales, gain) in enumerate(
+        ((dq, qn, qr, q_gain), (dk, kn, kr, k_gain), (dv, None, None, None))
+    ):
+        parts, sums = [], []
+        for n in range(6):
+            grad = jnp.concatenate([grads[2 * n], grads[2 * n + 1]], axis=0)
+            if normed is not None:
+                sums.append(jnp.sum(grad * normed[n], axis=0, keepdims=True))
+                grad = norm_back(normed[n], scales[n], grad * gain[:, n * HD : (n + 1) * HD])
+            parts.append(grad)
+        if sums:
+            gain_sums.append(jnp.concatenate(sums, axis=1))
+        d_mixed = jnp.concatenate(parts, axis=1).astype(bfloat)
+        rqkv[c] = dot(nbt[...], d_mixed).astype(bfloat).reshape(2, 2, 2, 2, 48, 384)
+        dn[...] += dot_nt(d_mixed, gqkv[c].reshape(768, 384))
+    tag_q1 = send(rqkv.at[:, :, :, 1 - core], q1, core_dev)
+    dns, dnr = r.dns, r.dnr
+    dns[...] = dn[ROWS : 2 * ROWS, :].astype(bfloat)
+    tag_dn = send(dns, dnr, x_dev)
+    arrive(o2, tag_o2, y_dev)
+    ot[...] = o1[:, y] + o2[...]
+    tag_o3 = [send(ot.at[z_up[k]], o3.at[k - 1], z_dev[k]) for k in range(1, N_HID)]
+    arrive(q1, tag_q1, core_dev)
+    q1[...] = q1[...] + rqkv[:, :, :, core]
+    tag_q2 = send(q1.at[:, :, 1 - y], q2, y_dev)
+
+    for i, (gh, gd) in enumerate(group):
+        arrive(al.at[gh, gd], tag_ag[i], group_dev[i])
+    rows_all = al[...].reshape(32, 8, 256)
+    d_logits_all = jnp.concatenate([rows_all[:, q, :] for q in range(4)], axis=1)
+    pooled_all = jnp.concatenate([rows_all[:, 4 + q, :] for q in range(3)], axis=1)
+    start = ((h * 4 + dp) * N_HID + z) * 24
+    chosen = (iota((24, 768), 1) == iota((24, 768), 0) + start).astype(bfloat)
+    mine = dot_nt(chosen, pooled_all.astype(bfloat))
+    g_head = jnp.dot(mine, d_logits_all, precision=highest, preferred_element_type=single)
+    r.g_head[...] = g_head[:, 0:classes]
+
+    arrive(dnr, tag_dn, x_dev)
+    d_normed = dn[0:ROWS, :] + dnr[...].astype(single)
+    block_n, block_scale = norm_parts(stream0)
+    d_block_gain = jnp.sum(d_normed * block_n, axis=0, keepdims=True)
+    d_in = ds[...] + norm_back(block_n, block_scale, d_normed * block_gain)
+    dx, gg = r.dx, r.gg
+    low, high = d_in[:, 0:384], d_in[:, 384:768]
+    dx[0] = jnp.where(h == 0, low, high).astype(bfloat)
+    dx[2] = jnp.where(h == 0, high, low).astype(bfloat)
+    tag_dx = send(dx.at[2], dx.at[1], x_dev)
+
+    def spread(row):
+        blank = jnp.zeros((1, 192), single)
+        halves = []
+        for a in range(2):
+            part = jnp.concatenate([row[:, a * 96 : a * 96 + 96], row[:, 192 + a * 96 : 288 + a * 96]], axis=1)
+            halves.append(
+                jnp.where(
+                    h == 0,
+                    jnp.concatenate([part, blank], axis=1),
+                    jnp.concatenate([blank, part], axis=1),
+                )
+            )
+        return jnp.concatenate(halves, axis=1)
+
+    d_gains = jnp.concatenate(
+        [d_block_gain, d_final_gain, spread(gain_sums[0]), spread(gain_sums[1]), jnp.zeros((4, 768), single)],
+        axis=0,
+    )
+    low, high = d_gains[:, 0:384], d_gains[:, 384:768]
+    gg[0] = jnp.where(h == 0, low, high)
+    gg[2] = jnp.where(h == 0, high, low)
+    tag_gg = send(gg.at[2], gg.at[1], x_dev)
+    arrive(dx.at[1], tag_dx, x_dev)
+    arrive(gg.at[1], tag_gg, x_dev)
+    rext, e1, e2, et, e3 = r.rext, r.e1, r.e2, r.et, r.e3
+    dxt = jnp.concatenate([dx[0].astype(single), dx[1].astype(single)], axis=0).T.astype(bfloat)
+    px2 = px[...].reshape(2 * ROWS, 1024)
+    d_gains = (gg[0] + gg[1]).astype(bfloat)
+    x0[...] = dot(dxt, px2[:, 0:512])
+    x1[...] = dot(dxt, px2[:, 512:1024]) + dot_tn(d_gains, rows_of.astype(bfloat))
+    for d in range(4):
+        for w in range(N_HID):
+            s = (d * N_HID + w) * 24
+            rext[d // 2, d % 2, w] = jnp.concatenate(
+                [x0[s : s + 24, :], x1[s : s + 24, :]], axis=0
+            ).astype(bfloat)
+    tag_e1 = send(rext.at[:, 1 - core], e1, core_dev)
+    arrive(q2, tag_q2, y_dev)
+    qt[...] = q1[:, :, y] + q2[...]
+    tag_q3 = [
+        send(qt.at[:, z_up[k] // 2, lax.rem(z_up[k], 2)], q3.at[k - 1], z_dev[k])
+        for k in range(1, N_HID)
+    ]
+    arrive(e1, tag_e1, core_dev)
+    e1[...] = e1[...] + rext[:, core]
+    tag_e2 = send(e1.at[1 - y], e2, y_dev)
+    ff_end()
+    total = ot[z].astype(single)
+    for k in range(1, N_HID):
+        arrive(o3.at[k - 1], tag_o3[k - 1], z_dev[k])
+        total = total + o3[k - 1].astype(single)
+    r.g_out[...] = total[:, 0:192]
+    arrive(e2, tag_e2, y_dev)
+    et[...] = e1[y] + e2[...]
+    tag_e3 = [send(et.at[z_up[k]], e3.at[k - 1], z_dev[k]) for k in range(1, N_HID)]
+    total = qt[:, z // 2, lax.rem(z, 2)].astype(single)
+    for k in range(1, N_HID):
+        arrive(q3.at[k - 1], tag_q3[k - 1], z_dev[k])
+        total = total + q3[k - 1].astype(single)
+    r.g_qkv[...] = total
+    total = et[z].astype(single)
+    for k in range(1, N_HID):
+        arrive(e3.at[k - 1], tag_e3[k - 1], z_dev[k])
+        total = total + e3[k - 1].astype(single)
+    r.g_patch[:, 0:512] = total[0:24]
+    r.g_patch[:, 512:768] = total[24:48, 0:256]
+    r.g_table[...] = total[24:48, 256 : 256 + seq_len]
+    columns = total[24:48, 256:512]
+    pick_f = (iota((8, 256), 1) == iota((8, 256), 0) + seq_len).astype(single)
+    r.g_gains[...] = dot_nt(pick_f, columns, precision=highest)[0:4]
+
+
+    def read(prefix, kind):
+        values = getattr(r, prefix + kind)[...]
+        return values.reshape(-1, values.shape[-1])
+
+    lane = iota((8, 128), 1)
+    own = jnp.where(lane == 0, term, 0.0)
+    grad_square = None
+    for n, kind in enumerate(KINDS):
+        value = square_sum(read("g_", kind))
+        grad_square = value if grad_square is None else grad_square + value
+        own = jnp.where(lane == 8 + n, square_sum(read("w_", kind)), own)
+    own = jnp.where(lane == 1, grad_square, own)
+
+    def all_sum(vector, line, every):
+        line[z] = vector
+        tags_z = [send(line.at[z], line.at[z], z_dev[k]) for k in range(1, N_HID)]
+        for k in range(1, N_HID):
+            arrive(line.at[z_down[k]], tags_z[k - 1], z_dev[k])
+        every[h, dp] = (line[0] + line[1]) + (line[2] + line[3])
+        tags_g = [send(every.at[h, dp], every.at[h, dp], device) for device in group_dev]
+        for i, (gh, gd) in enumerate(group):
+            arrive(every.at[gh, gd], tags_g[i], group_dev[i])
+        total = None
+        for a in range(2):
+            for d in range(4):
+                total = every[a, d] if total is None else total + every[a, d]
+        return total
+
+    sums = all_sum(own, r.l1, r.v1)
+    grad_norm = jnp.sqrt(jnp.sum(jnp.where(lane == 1, sums, 0.0), axis=1, keepdims=True))[0:1]
+    clip = jnp.minimum(1.0, clip_at / grad_norm)
+    own = jnp.zeros((8, 128), single)
+    for n, kind in enumerate(KINDS):
+        update = one_update(read("w_", kind), read("m_", kind), read("v_", kind), read("g_", kind), clip)[2]
+        own = jnp.where(lane == 8 + n, square_sum(update), own)
+    updates = all_sum(own, r.l2, r.v2)
+    result = jnp.sqrt(sums) / jnp.sqrt(updates)
+    result = jnp.where(lane == 0, sums, result)
+    result = jnp.where(lane == 1, grad_norm, result)
+    result = jnp.where(lane == 2, clip, result)
+    r.scalars[...] = result
+    for copy in sends:
+        copy.wait_send()
+
+
+def write_kernel(names, *refs):
+    r = types.SimpleNamespace(**dict(zip(names, refs)))
+    lane = iota((8, 128), 1)
+
+    def pick(n):
+        return jnp.sum(jnp.where(lane == n, r.scalars[...], 0.0), axis=1, keepdims=True)[0:1]
+
+    clip = pick(2)
+    for n, kind in enumerate(KINDS):
+        master = getattr(r, "w_" + kind)[...]
+        grad = getattr(r, "g_" + kind)[...]
+        ratio = pick(8 + n)
+        if len(master.shape) == 3:
+            c, ratio = clip[None], ratio[None]
+        else:
+            c = clip
+        first, second, update = one_update(master, getattr(r, "m_" + kind)[...], getattr(r, "v_" + kind)[...], grad, c)
+        getattr(r, "nm_" + kind)[...] = first
+        getattr(r, "nv_" + kind)[...] = second
+        getattr(r, "nw_" + kind)[...] = master - learn_rate * ratio * update
+
+
+def fast_device(patches, labels, *state):
+    bfloat, single = jnp.bfloat16, jnp.float32
+
+    def turn(kind, value):
+        if kind in ("patch", "table", "down"):
+            return value.T
+        if kind == "qkv":
+            return value.transpose(1, 0, 2)
+        return value
+
+    flat = [turn(KINDS[i % 8], value) for i, value in enumerate(state)]
+    vmem = pl.BlockSpec(memory_space=pltpu.VMEM)
+    smem = pl.BlockSpec(memory_space=pltpu.SMEM)
+    in_names = ["labels", "patches"] + [p + k for p in ("w_", "m_", "v_") for k in KINDS]
+    out_names = ["g_" + k for k in KINDS] + ["scalars"]
+    scratch = dict(
+        px=((2, ROWS, 1024), bfloat),
+        gext=((4, 4, 48, 512), bfloat),
+        gqkv=((3, 2, 4, 2, 48, 384), bfloat),
+        gout=((4, 4, 96, 256), bfloat),
+        gup=((4, 2, 4, 96, 384), bfloat),
+        gdn=((4, 2, 4, 96, 384), bfloat),
+        ghd=((2, 4, 4, 48, 512), bfloat),
+        x0=((384, 512), single),
+        x1=((384, 512), single),
+        x2=((768, 512), single),
+        x3=((768, 512), single),
+        ga=((2, 8, 384), single),
+        st=((2, 2, ROWS, 384), bfloat),
+        nb=((2 * ROWS, 768), bfloat),
+        nbt=((768, 2 * ROWS), bfloat),
+        qn=((6, 2 * ROWS, HD), single),
+        kn=((6, 2 * ROWS, HD), single),
+        qr=((6, 2 * ROWS, 1), single),
+        kr=((6, 2 * ROWS, 1), single),
+        q=((12, ROWS, HD), bfloat),
+        k=((12, ROWS, HD), bfloat),
+        v=((12, ROWS, HD), bfloat),
+        pr=((12, ROWS, ROWS), single),
+        ho=((12, ROWS, HD), single),
+        hof=((2 * ROWS, 384), bfloat),
+        us=((4, 2 * ROWS, 384), single),
+        hb=((4, 2 * ROWS, 384), bfloat),
+        br=((2 * ROWS, 768), single),
+        brs=((2, ROWS, 384), bfloat),
+        brr=((2, ROWS, 384), bfloat),
+        ds=((ROWS, 768), single),
+        db=((2, ROWS, 768), bfloat),
+        dbt=((768, 2 * ROWS), bfloat),
+        al=((2, 4, 4, 8, 256), single),
+        rff=((4, 2, 2, 2, 2, 96, 384), bfloat),
+        f1=((4, 2, 2, 2, 96, 384), bfloat),
+        f2=((4, 2, 2, 96, 384), bfloat),
+        ft=((3, 2, 2, 96, 384), bfloat),
+        f3=((3, 2, 2, 96, 384), bfloat),
+        rout=((4, 2, 2, 96, 256), bfloat),
+        o1=((4, 2, 96, 256), bfloat),
+        o2=((4, 96, 256), bfloat),
+        ot=((4, 96, 256), bfloat),
+        o3=((3, 96, 256), bfloat),
+        dh=((12, ROWS, HD), bfloat),
+        dk=((12, ROWS, HD), single),
+        dv=((12, ROWS, HD), single),
+        rqkv=((3, 2, 2, 2, 2, 48, 384), bfloat),
+        q1=((3, 2, 2, 2, 48, 384), bfloat),
+        q2=((3, 2, 2, 48, 384), bfloat),
+        qt=((3, 2, 2, 48, 384), bfloat),
+        q3=((3, 3, 48, 384), bfloat),
+        dns=((ROWS, 768), bfloat),
+        dnr=((ROWS, 768), bfloat),
+        dx=((3, ROWS, 384), bfloat),
+        gg=((3, 8, 384), single),
+        rext=((2, 2, 4, 48, 512), bfloat),
+        e1=((2, 4, 48, 512), bfloat),
+        e2=((4, 48, 512), bfloat),
+        et=((4, 48, 512), bfloat),
+        e3=((3, 48, 512), bfloat),
+        l1=((4, 8, 128), single),
+        l2=((4, 8, 128), single),
+        v1=((2, 4, 8, 128), single),
+        v2=((2, 4, 8, 128), single),
+    )
+    semaphores = 180
+    shapes = [flat[i].shape for i in range(8)]
+    npatch, seq_len, classes = patches.shape[1], flat[1].shape[1], flat[3].shape[1]
+    total_images = labels.shape[0] * lax.axis_size("dp")
+    sizes = (npatch, seq_len, classes, total_images)
+    names = in_names + out_names + list(scratch) + ["ssem", "rsem"]
+    found = pl.pallas_call(
+        functools.partial(step_kernel, sizes, names),
+        out_shape=[jax.ShapeDtypeStruct(s, single) for s in shapes]
+        + [jax.ShapeDtypeStruct((8, 128), single)],
+        in_specs=[smem] + [vmem] * 25,
+        out_specs=[vmem] * 9,
+        scratch_shapes=[pltpu.VMEM(s, t) for s, t in scratch.values()]
+        + [pltpu.SemaphoreType.DMA((semaphores,))] * 2,
+        compiler_params=pltpu.CompilerParams(
+            collective_id=0, has_side_effects=True, vmem_limit_bytes=62 * 2**20
+        ),
+        name="train_step",
+    )(labels, patches, *flat)
+    grads, scalars = found[:8], found[8]
+    names = (
+        ["scalars"]
+        + [p + k for p in ("w_", "m_", "v_", "g_") for k in KINDS]
+        + [p + k for p in ("nm_", "nv_", "nw_") for k in KINDS]
+    )
+    written = pl.pallas_call(
+        functools.partial(write_kernel, names),
+        out_shape=[jax.ShapeDtypeStruct(s, single) for s in shapes * 3],
+        in_specs=[vmem] * 33,
+        out_specs=[vmem] * 24,
+        compiler_params=pltpu.CompilerParams(vmem_limit_bytes=48 * 2**20),
+        name="write_step",
+    )(scalars, *flat, *grads)
+    back = [turn(KINDS[i % 8], value) for i, value in enumerate(written)]
+    return (scalars[0, 0], scalars[0, 1], *back)
+
+
+def fits(mesh):
+    return tuple(mesh.shape[a] for a in ALL) == (4, 2, N_HID)
+
+
 def solution(mesh):
     placed = (
-        P(("dp", "heads", "hidden"), None, None),
+        P(ALL, None, None),
         P("dp"),
-        P(None, ("dp", "heads", "hidden")),
-        P(None, ("dp", "heads", "hidden")),
-        P(None, ("dp", "heads", "hidden")),
-        P(("dp", "heads", "hidden"), None),
-        P(("dp", "hidden"), None, "heads"),
-        P(("heads", "hidden"), "dp"),
-        P("dp", ("heads", "hidden")),
-        P(("heads", "hidden"), "dp"),
-        P(None, ("dp", "heads", "hidden")),
-        P(None, ("dp", "heads", "hidden")),
-        P(None, ("dp", "heads", "hidden")),
-        P(("dp", "heads", "hidden"), None),
-        P(("dp", "hidden"), None, "heads"),
-        P(("heads", "hidden"), "dp"),
-        P("dp", ("heads", "hidden")),
-        P(("heads", "hidden"), "dp"),
-        P(None, ("dp", "heads", "hidden")),
-        P(None, ("dp", "heads", "hidden")),
-        P(None, ("dp", "heads", "hidden")),
-        P(("dp", "heads", "hidden"), None),
-        P(("dp", "hidden"), None, "heads"),
-        P(("heads", "hidden"), "dp"),
-        P("dp", ("heads", "hidden")),
-        P(("heads", "hidden"), "dp"),
+        P(None, ALL),
+        P(None, ALL),
+        P(None, ALL),
+        P(ALL, None),
+        P(DATA, None, "heads"),
+        P(MODEL, "dp"),
+        P("dp", MODEL),
+        P(MODEL, "dp"),
+        P(None, ALL),
+        P(None, ALL),
+        P(None, ALL),
+        P(ALL, None),
+        P(DATA, None, "heads"),
+        P(MODEL, "dp"),
+        P("dp", MODEL),
+        P(MODEL, "dp"),
+        P(None, ALL),
+        P(None, ALL),
+        P(None, ALL),
+        P(ALL, None),
+        P(DATA, None, "heads"),
+        P(MODEL, "dp"),
+        P("dp", MODEL),
+        P(MODEL, "dp"),
     )
     return jax.shard_map(
-        per_device,
+        fast_device if fits(mesh) else per_device,
         mesh=mesh,
         in_specs=placed,
         out_specs=(
             P(),
             P(),
-            P(None, ("dp", "heads", "hidden")),
-            P(None, ("dp", "heads", "hidden")),
-            P(None, ("dp", "heads", "hidden")),
-            P(("dp", "heads", "hidden"), None),
-            P(("dp", "hidden"), None, "heads"),
-            P(("heads", "hidden"), "dp"),
-            P("dp", ("heads", "hidden")),
-            P(("heads", "hidden"), "dp"),
-            P(None, ("dp", "heads", "hidden")),
-            P(None, ("dp", "heads", "hidden")),
-            P(None, ("dp", "heads", "hidden")),
-            P(("dp", "heads", "hidden"), None),
-            P(("dp", "hidden"), None, "heads"),
-            P(("heads", "hidden"), "dp"),
-            P("dp", ("heads", "hidden")),
-            P(("heads", "hidden"), "dp"),
-            P(None, ("dp", "heads", "hidden")),
-            P(None, ("dp", "heads", "hidden")),
-            P(None, ("dp", "heads", "hidden")),
-            P(("dp", "heads", "hidden"), None),
-            P(("dp", "hidden"), None, "heads"),
-            P(("heads", "hidden"), "dp"),
-            P("dp", ("heads", "hidden")),
-            P(("heads", "hidden"), "dp"),
+            P(None, ALL),
+            P(None, ALL),
+            P(None, ALL),
+            P(ALL, None),
+            P(DATA, None, "heads"),
+            P(MODEL, "dp"),
+            P("dp", MODEL),
+            P(MODEL, "dp"),
+            P(None, ALL),
+            P(None, ALL),
+            P(None, ALL),
+            P(ALL, None),
+            P(DATA, None, "heads"),
+            P(MODEL, "dp"),
+            P("dp", MODEL),
+            P(MODEL, "dp"),
+            P(None, ALL),
+            P(None, ALL),
+            P(None, ALL),
+            P(ALL, None),
+            P(DATA, None, "heads"),
+            P(MODEL, "dp"),
+            P("dp", MODEL),
+            P(MODEL, "dp"),
         ),
         check_vma=False,
     )

time: 1200 us -> 202 us (0.17)
  waiting for transfers between devices: 662 us -> 0 us
  blocking collectives: 282 us -> 0 us
  Pallas kernels: 0 us -> 181 us
  other arithmetic: 94.4 us -> 0 us
  matrix products: 66.2 us -> 0 us
  local copies, waits for them, and re-layouts: 54.3 us -> 18.8 us
  between operations: 22.4 us -> 0.88 us
    reduce_scatter x6 -> x0, waiting for transfers between devices: 332 us -> none  [the longest x1 106 us: per_device(): lax.psum_scatter(d_head, ('dp', 'heads', 'hidden'), scatter_dimension=0,...]
    pallas_call x0 -> x2, Pallas kernels: none -> 181 us  [the longest x1 179 us: fast_device(): pl.pallas_call(functools.partial(step_kernel, sizes, names), out_shape=[j...]
    psum x1 -> x0, waiting for transfers between devices: 168 us -> none  [per_device(): total = lax.psum(partial_sum, ('heads', 'hidden'))]
    all_gather x5 -> x0, blocking collectives: 163 us -> none  [the longest x1 73.5 us: per_device(): lax.all_gather(table.astype(bfloat), ('dp', 'heads', 'hidden'), axis=1, t...]
    unnamed x15 -> x0, waiting for transfers between devices: 111 us -> none
    psum x2 -> x0, blocking collectives: 79.4 us -> none  [per_device(): lax.psum((grad_squares, weight_squares, jnp.sum(loss_terms)), ('dp', 'hea...]
    dot_general x21 -> x0, matrix products: 61.8 us -> none  [the longest x1 5.68 us: per_device(): attn_part = jnp.dot(columns, out_b, preferred_element_type=single)]
    reduce_sum x34 -> x0, other arithmetic: 50.5 us -> none  [the longest x8 13.5 us: per_device(): weight_squares = jnp.stack([jnp.sum(master * master) for master in masters])]
  transfers between devices with their start and end apart: 15 -> 0, of which waited for: 12 -> 0; matrix products, arithmetic and copies ran while one was open for 7% -> 0% of each run, Pallas kernels for 0% -> 0%
where the time goes in v1:
time: 202 us; the launch traced here: 201 us
  Pallas kernels  181 us (90%)
  local copies, waits for them, and re-layouts  18.8 us (9%)
    pallas_call x1, Pallas kernels, fast_device(): pl.pallas_call(functools.partial(step_kernel, sizes, names), out_shape=[j...  179 us
    unnamed x66, local copies, waits for them, and re-layouts  18.2 us

profile of v1, /device:TPU:0, one launch (start us, length us, event | category | flops | bytes accessed | tf_op | source)
XLA Modules:
  0.0 200.7 jit_solution(7759973279446510272)
XLA Ops:
  0.7 0.0 copy-start
  0.7 0.0 copy-start.1
  0.7 0.0 copy-start.2
  0.7 0.0 copy-start.3
  0.7 0.0 copy-start.4
  0.7 0.0 copy-start.5
  0.7 0.0 copy-start.6
  0.7 0.0 copy-start.21
  0.8 0.0 copy-start.30
  0.8 178.6 %train_step.1 = (f32[24,768]{1,0:T(8,128)}, f32[24,200]{1,0:T(8,128)}, f32[4,24]{1,0:T(4,128)}, f32[24,1000]{1,0:T(8,128)}, f32[3,48,384]{2,1,0:T(8,128)}, /*ind...) custom-call(s32[8]{0:T(128)} %refs_0_.1, bf16[1,196,768]{2,1,0:T(8,128)(2,1)} %refs_1_.1, ...), custom_call_target="tpu_custom_call" | custom-call | tf_op jit(solution)/shard_map/train_step/pallas_call | solution.py:1121
  179.4 0.0 copy-start.32
  179.4 0.0 copy-start.31
  179.4 0.0 copy-start.29
  179.4 0.0 copy-start.28
  179.5 0.0 copy-done
  179.5 0.0 copy-done.1
  179.5 0.0 copy-done.2
  179.5 0.0 copy-done.3
  179.5 0.0 copy-done.4
  179.5 0.0 copy-done.5
  179.5 0.0 copy-done.6
  179.5 0.0 copy-done.21
  179.5 0.0 copy-done.30
  179.5 0.5 copy-done.32
  180.1 0.0 copy-done.31
  180.1 0.0 copy-done.29
  180.1 0.0 copy-done.28
  180.1 0.0 copy-start.7
  180.1 0.9 copy-done.7
  181.1 0.0 copy-start.8
  181.1 0.9 copy-done.8
  182.0 0.0 copy-start.9
  182.0 0.9 copy-done.9
  182.9 0.9 copy-done.10
  183.8 0.0 copy-start.11
  183.8 0.9 copy-done.11
  184.7 0.0 copy-start.12
  184.7 0.9 copy-done.12
  185.6 0.0 copy-start.13
  185.6 0.9 copy-done.13
  186.5 0.0 copy-start.14
  186.5 0.9 copy-done.14
  187.4 0.0 copy-start.15
  187.4 1.0 copy-done.15
  188.3 0.0 copy-start.16
  188.3 1.0 copy-done.16
  189.3 0.9 copy-done.17
  190.2 0.0 copy-start.18
  190.2 0.9 copy-done.18
  191.1 0.0 copy-start.19
  191.1 0.9 copy-done.19
  191.9 0.0 copy-start.20
  191.9 0.9 copy-done.20
  192.9 0.0 copy-start.22
  192.9 0.7 copy-done.22
  193.6 0.0 copy-start.23
  193.6 0.7 copy-done.23
  194.4 0.0 copy-start.24
  194.4 0.9 copy-done.24
  195.2 0.9 copy-done.25
  196.1 0.9 copy-done.26
  197.0 0.7 copy-done.27
  197.8 2.3 %write_step.1 = (f32[24,768]{1,0:T(8,128)}, f32[24,200]{1,0:T(8,128)}, f32[4,24]{1,0:T(4,128)}, f32[24,1000]{1,0:T(8,128)}, f32[3,48,384]{2,1,0:T(8,128)}, /*ind...) custom-call(f32[8,128]{1,0:T(8,128)S(1)} %copy-done.31, ...), custom_call_target="tpu_custom_call" | custom-call | tf_op jit(solution)/shard_map/write_step/pallas_call | solution.py:1140
  200.1 0.6 fusion
  (5 shorter events, 0.0 us)
Async XLA Ops:
  0.7 178.8 %copy-start = (f32[192,384]{1,0:T(8,128)S(1)}, f32[192,384]{1,0:T(8,128)}, u32[]{:S(2)}) copy-start(f32[192,384]{1,0:T(8,128)} %refs_7_.3) | copy-start | bytes 884740
  0.7 178.8 %copy-start.1 = (f32[384,192]{0,1:T(8,128)S(1)}, f32[384,192]{0,1:T(8,128)}, u32[]{:S(2)}) copy-start(f32[384,192]{0,1:T(8,128)} %param.35) | copy-start | bytes 884740
  0.7 178.8 %copy-start.2 = (f32[192,384]{1,0:T(8,128)S(1)}, f32[192,384]{1,0:T(8,128)}, u32[]{:S(2)}) copy-start(f32[192,384]{1,0:T(8,128)} %refs_15_.3) | copy-start | bytes 884740
  0.7 178.8 %copy-start.3 = (f32[384,192]{0,1:T(8,128)S(1)}, f32[384,192]{0,1:T(8,128)}, u32[]{:S(2)}) copy-start(f32[384,192]{0,1:T(8,128)} %param.43) | copy-start | bytes 884740
  0.7 178.8 %copy-start.4 = (f32[192,384]{1,0:T(8,128)S(1)}, f32[192,384]{1,0:T(8,128)}, u32[]{:S(2)}) copy-start(f32[192,384]{1,0:T(8,128)} %refs_23_.3) | copy-start | bytes 884740
  0.7 178.8 %copy-start.5 = (f32[384,192]{0,1:T(8,128)S(1)}, f32[384,192]{0,1:T(8,128)}, u32[]{:S(2)}) copy-start(f32[384,192]{0,1:T(8,128)} %param.51) | copy-start | bytes 884740
  0.7 178.8 %copy-start.6 = (f32[48,3,384]{2,0,1:T(8,128)S(1)}, f32[48,3,384]{2,0,1:T(8,128)}, u32[]{:S(2)}) copy-start(f32[48,3,384]{2,0,1:T(8,128)} %param.32) | copy-start | bytes 663556
  0.7 178.8 %copy-start.21 = (f32[200,24]{0,1:T(8,128)S(1)}, f32[200,24]{0,1:T(8,128)}, u32[]{:S(2)}) copy-start(f32[200,24]{0,1:T(8,128)} %param.29) | copy-start | bytes 57604
  0.8 178.8 %copy-start.30 = (f32[4,24]{1,0:T(4,128)S(1)}, f32[4,24]{1,0:T(4,128)}, u32[]{:S(2)}) copy-start(f32[4,24]{1,0:T(4,128)} %refs_19_.1) | copy-start | bytes 1156
  179.4 0.7 copy-start.32
  179.4 0.7 copy-start.31
  179.4 0.7 copy-start.29
  179.4 0.7 copy-start.28
  180.1 0.9 copy-start.7
  181.1 0.9 copy-start.8
  182.0 0.9 copy-start.9
  182.9 0.9 copy-start.10
  183.8 0.9 copy-start.11
  184.7 0.9 copy-start.12
  185.6 0.9 copy-start.13
  186.5 0.9 copy-start.14
  187.4 1.0 copy-start.15
  188.3 1.0 copy-start.16
  189.3 0.9 copy-start.17
  190.2 0.9 copy-start.18
  191.1 0.9 copy-start.19
  191.9 0.9 copy-start.20
  192.9 0.7 copy-start.22
  193.6 0.7 copy-start.23
  194.4 0.9 copy-start.24
  195.2 0.9 copy-start.25
  196.1 0.9 copy-start.26
  197.0 0.7 copy-start.27

commit v2 on v1

--- a/solution.py
+++ b/solution.py
@@ -403,11 +403,38 @@
     for device in z_dev[1:] + group_dev:
         pl.semaphore_signal(barrier, inc=1, device_id=device, device_id_type=MESH)
 
+    loads = {}
+    order = ["w_patch", "w_table", "w_gains", "patches"]
+    order += [p + k for p in ("w_", "m_", "v_") for k in KINDS if p + k not in order]
+    for number, name in enumerate(order):
+        loads[name] = pltpu.make_async_copy(
+            getattr(r, "h_" + name), getattr(r, name), r.lsem.at[number]
+        )
+        loads[name].start()
+    stores = []
+
+    def store(name):
+        copy = pltpu.make_async_copy(
+            getattr(r, name), getattr(r, "h_" + name), r.lsem.at[len(order) + len(stores)]
+        )
+        copy.start()
+        stores.append(copy)
+
     ssem, rsem = r.ssem, r.rsem
     count = [0]
-    sends = []
-
-    def send(source, target, device):
+    sends = {}
+    last = N_HID - 1
+    holds = {}
+    for d in range(1, N_HID):
+        holds["left", d] = z >= d
+        holds["right", d] = z + d <= last
+        holds["on_right", d] = (z >= d) & (z < last)
+        holds["on_left", d] = (z + d <= last) & (z > 0)
+    holds["on_right", 0] = z < last
+    holds["on_left", 0] = z > 0
+    next_z = {"left": (dp, h, z_up[1]), "right": (dp, h, z_down[1])}
+
+    def send(source, target, device, key=None):
         number = count[0]
         count[0] += 1
         copy = pltpu.make_async_remote_copy(
@@ -418,8 +445,11 @@
             device_id=device,
             device_id_type=MESH,
         )
-        copy.start()
-        sends.append(copy)
+        if key is None:
+            copy.start()
+        else:
+            pl.when(holds[key])(copy.start)
+        sends.setdefault(key, []).append(copy)
         return number
 
     def arrive(target, number, device):
@@ -433,33 +463,49 @@
         ).wait_recv()
 
     gext, gqkv, gout, gup, gdn, ghd = r.gext, r.gqkv, r.gout, r.gup, r.gdn, r.ghd
-    x0, x1 = r.x0, r.x1
-    x1[0:24, :] = jnp.zeros((24, 512), single)
-    x1[0:24, 256 : 256 + seq_len] = r.w_table[...]
-    pick = (iota((4, 256), 1) == iota((4, 256), 0) + seq_len).astype(bfloat)
-    table_part = x1[0:24, 256:512] + dot_tn(r.w_gains[...].astype(bfloat), pick)
-    wp = r.w_patch[...]
-    gext[dp, z] = jnp.concatenate(
-        [wp[:, 0:512], jnp.concatenate([wp[:, 512:768], table_part], axis=1)], axis=0
-    ).astype(bfloat)
-    gqkv[:, z // 2, dp, lax.rem(z, 2)] = r.w_qkv[...].astype(bfloat)
-    gup[z, :, dp] = r.w_up[...].astype(bfloat).reshape(2, 96, 384)
-    gdn[z, :, dp] = r.w_down[...].astype(bfloat).reshape(2, 96, 384)
-    gout[dp, z] = jnp.zeros((96, 256), bfloat)
-    gout[dp, z, :, 0:192] = r.w_out[...].astype(bfloat)
-    x0[0:24, :] = r.w_head[:, 0:512]
-    x1[0:24, :] = jnp.zeros((24, 512), single)
-    x1[0:24, 0 : classes - 512] = r.w_head[:, 512:classes]
-    ghd[h, dp, z] = jnp.concatenate([x0[0:24, :], x1[0:24, :]], axis=0).astype(bfloat)
-    px = r.px
-    row, col = iota((ROWS, 256), 0), iota((ROWS, 256), 1)
-    spot = jnp.where((row == col) & (row < seq_len), 1.0, 0.0).astype(bfloat)
-    px[0, :, 768:1024] = spot
-    px[1, :, 768:1024] = spot
-    px[0, :, 0:768] = jnp.zeros((ROWS, 768), bfloat)
-    px[0, 0:npatch, 0:768] = r.patches[0]
-
-    pl.semaphore_wait(barrier, len(z_dev) - 1 + len(group_dev))
+    x0, x1, px = r.x0, r.x1, r.px
+
+    def pack_ext():
+        x1[0:24, :] = jnp.zeros((24, 512), single)
+        for name in order[0:3]:
+            loads[name].wait()
+        x1[0:24, 256 : 256 + seq_len] = r.w_table[...]
+        pick = (iota((4, 256), 1) == iota((4, 256), 0) + seq_len).astype(bfloat)
+        table_part = x1[0:24, 256:512] + dot_tn(r.w_gains[...].astype(bfloat), pick)
+        wp = r.w_patch[...]
+        gext[dp, z] = jnp.concatenate(
+            [wp[:, 0:512], jnp.concatenate([wp[:, 512:768], table_part], axis=1)], axis=0
+        ).astype(bfloat)
+
+    def pack_patches():
+        row, col = iota((ROWS, 256), 0), iota((ROWS, 256), 1)
+        spot = jnp.where((row == col) & (row < seq_len), 1.0, 0.0).astype(bfloat)
+        px[0, :, 768:1024] = spot
+        px[1, :, 768:1024] = spot
+        px[0, ROWS - 16 : ROWS, 0:768] = jnp.zeros((16, 768), bfloat)
+        loads["patches"].wait()
+        px[0, 0:npatch, 0:768] = r.patches[0]
+
+    def pack_rest():
+        loads["w_qkv"].wait()
+        gqkv[:, z // 2, dp, lax.rem(z, 2)] = r.w_qkv[...].astype(bfloat)
+        yield
+        loads["w_up"].wait()
+        gup[z, :, dp] = r.w_up[...].astype(bfloat).reshape(2, 96, 384)
+        yield
+        loads["w_head"].wait()
+        x0[0:24, :] = r.w_head[:, 0:512]
+        x1[0:24, :] = jnp.zeros((24, 512), single)
+        x1[0:24, 0 : classes - 512] = r.w_head[:, 512:classes]
+        ghd[h, dp, z] = jnp.concatenate([x0[0:24, :], x1[0:24, :]], axis=0).astype(bfloat)
+        yield
+        loads["w_out"].wait()
+        gout[dp, z] = jnp.zeros((96, 256), bfloat)
+        gout[dp, z, :, 0:192] = r.w_out[...].astype(bfloat)
+        yield
+        loads["w_down"].wait()
+        gdn[z, :, dp] = r.w_down[...].astype(bfloat).reshape(2, 96, 384)
+        yield
 
     def at_ext(d, w):
         return gext.at[d, w]
@@ -501,27 +547,31 @@
     }
     tags = {}
 
-    def first_send(name):
-        at = slot[name]
-        own = at(dp, z)
-        for k in range(1, N_HID):
-            tags[name, "z", k] = send(own, own, z_dev[k])
+    def send_own(name):
+        own = slot[name](dp, z)
+        tags[name, "left", 1] = send(own, own, next_z["left"], ("on_right", 0))
+        tags[name, "right", 1] = send(own, own, next_z["right"], ("on_left", 0))
         tags[name, "y", 0] = send(own, own, y_dev)
 
-    def pass_on(name):
-        at = slot[name]
-        for k in range(1, N_HID):
-            theirs = at(dp, z_down[k])
-            arrive(theirs, tags[name, "z", k], z_dev[k])
-            tags[name, "y", k] = send(theirs, theirs, y_dev)
-        if name != "hd":
+    def pass_z(name, d):
+        for side, on, theirs in (("left", "on_right", z_down[d]), ("right", "on_left", z_up[d])):
+            block = slot[name](dp, theirs)
+            number = tags[name, side, d]
+            pl.when(holds[side, d])(functools.partial(arrive, block, number, y_dev))
+            if d < last:
+                tags[name, side, d + 1] = send(block, block, next_z[side], (on, d))
+            tags[name, "y", side, d] = send(block, block, y_dev, (side, d))
+        if d == last and name != "hd":
             line = lines[name](dp)
             tags[name, "c", 0] = send(line, line, core_dev)
 
     def pass_core(name):
         at = slot[name]
-        for k in range(N_HID):
-            arrive(at(y_dp, z_down[k]), tags[name, "y", k], y_dev)
+        arrive(at(y_dp, z), tags[name, "y", 0], y_dev)
+        for d in range(1, N_HID):
+            for side, theirs in (("left", z_down[d]), ("right", z_up[d])):
+                number = tags[name, "y", side, d]
+                pl.when(holds[side, d])(functools.partial(arrive, at(y_dp, theirs), number, y_dev))
         line = lines[name](y_dp)
         if name != "hd":
             tags[name, "c", 1] = send(line, line, core_dev)
@@ -547,12 +597,27 @@
         for i, d in enumerate((core_dp, far)):
             arrive(ghd.at[:, d], tags["hd", "c", i], core_dev)
 
-    first_send("ext")
+    pack_ext()
+    pl.semaphore_wait(barrier, len(z_dev) - 1 + len(group_dev))
+    send_own("ext")
+    packing = pack_rest()
+    next(packing)
+    send_own("qkv")
+    pass_z("ext", 1)
+    pack_patches()
     images = px.at[0, :, pl.ds(0, 768)]
     tag_px = send(images, px.at[1, :, pl.ds(0, 768)], x_dev)
-    first_send("qkv")
-    pass_on("ext")
-    first_send("up0")
+    next(packing)
+    send_own("up0")
+    pass_z("ext", 2)
+    pass_z("qkv", 1)
+    send_own("up1")
+    pass_z("ext", 3)
+    for _ in packing:
+        pass
+    pass_z("qkv", 2)
+    pass_z("up0", 1)
+    send_own("hd")
     pass_core("ext")
     complete("ext")
 
@@ -574,8 +639,10 @@
     arrive(px.at[1, :, pl.ds(0, 768)], tag_px, x_dev)
     st[h, 1] = (dot_nt(px[1, :, 0:512], x0b) + dot_nt(px[1, :, 512:1024], x1b)).astype(bfloat)
     tag_st1 = send(st.at[h, 1], st.at[h, 0], x_dev)
-    pass_on("qkv")
-    first_send("up1")
+    pass_z("qkv", 3)
+    pass_z("up0", 2)
+    pass_z("up1", 1)
+    send_own("out")
     arrive(ga.at[1 - h], tag_ga, x_dev)
     arrive(st.at[1 - h, 1], tag_st0, x_dev)
     arrive(st.at[1 - h, 0], tag_st1, x_dev)
@@ -597,54 +664,60 @@
     for i in range(2):
         stream = jnp.concatenate([st[0, i], st[1, i]], axis=1).astype(single)
         nb[i * ROWS : (i + 1) * ROWS, :] = (norm_parts(stream)[0] * block_gain).astype(bfloat)
+    pass_z("up0", 3)
+    pass_z("up1", 2)
+    pass_z("hd", 1)
+    send_own("dn0")
     pass_core("qkv")
-    first_send("hd")
-    pass_on("up0")
-    first_send("out")
     complete("qkv")
 
-    qn, kn, qr, kr = r.qn, r.kn, r.qr, r.kr
+    qn, kn = r.qn, r.kn
     q_ref, k_ref, v_ref = r.q, r.k, r.v
     q_gain, k_gain = head_gain(2), head_gain(3)
-    for c, (keep, scales, out, gain) in enumerate(
-        ((qn, qr, q_ref, q_gain), (kn, kr, k_ref, k_gain), (None, None, v_ref, None))
+    for c, (keep, out, gain) in enumerate(
+        ((qn, q_ref, q_gain), (kn, k_ref, k_gain), (None, v_ref, None))
     ):
         mixed = dot(nb[...], gqkv[c].reshape(768, 384))
         for n in range(6):
             part = mixed[:, n * HD : (n + 1) * HD]
             if keep is not None:
                 part, scale = norm_parts(part)
-                keep[n] = part
-                scales[n] = scale
+                keep[n, :, 0:HD] = part
+                keep[n, :, HD : 2 * HD] = jnp.broadcast_to(scale, (2 * ROWS, HD))
                 part = part * gain[:, n * HD : (n + 1) * HD]
             part = part.astype(bfloat)
             out[2 * n] = part[0:ROWS]
             out[2 * n + 1] = part[ROWS : 2 * ROWS]
         if c == 0:
-            pass_on("up1")
-            first_send("dn0")
+            pass_z("up1", 3)
+            pass_z("hd", 2)
+            pass_z("out", 1)
+            send_own("dn1")
+            pass_core("up0")
 
     pr, ho = r.pr, r.ho
     dead = iota((ROWS, ROWS), 1) >= seq_len
 
-    def attend(i, carry):
-        scores = dot_nt(q_ref[i], k_ref[i]) * HD ** (-0.5)
-        scores = jnp.where(dead, -1e30, scores)
-        scores = scores - jnp.max(scores, axis=-1, keepdims=True)
-        weights = jnp.exp(scores)
-        probs = weights / jnp.sum(weights, axis=-1, keepdims=True)
-        pr[i] = probs
-        ho[i] = dot(probs.astype(bfloat), v_ref[i])
+    def attend(n, carry):
+        for i in (2 * n, 2 * n + 1):
+            scores = dot_nt(q_ref[i], k_ref[i]) * HD ** (-0.5)
+            scores = jnp.where(dead, -1e30, scores)
+            scores = scores - jnp.max(scores, axis=-1, keepdims=True)
+            weights = jnp.exp(scores)
+            probs = weights / jnp.sum(weights, axis=-1, keepdims=True)
+            pr[i] = probs
+            ho[i] = dot(probs.astype(bfloat), v_ref[i])
         return carry
 
-    lax.fori_loop(0, 4, attend, 0)
-    pass_core("up0")
-    pass_on("hd")
-    first_send("dn1")
-    lax.fori_loop(4, 8, attend, 0)
-    pass_on("out")
-    lax.fori_loop(8, 12, attend, 0)
+    lax.fori_loop(0, 2, attend, 0)
+    pass_z("hd", 3)
+    pass_z("out", 2)
+    pass_z("dn0", 1)
     pass_core("up1")
+    lax.fori_loop(2, 6, attend, 0)
+    pass_z("out", 3)
+    pass_z("dn0", 2)
+    pass_z("dn1", 1)
     pass_core("hd")
     hof = r.hof
     for i in range(2):
@@ -652,7 +725,6 @@
         hof[i * ROWS : (i + 1) * ROWS, :] = joined.astype(bfloat)
     complete("up0")
     complete("up1")
-    pass_on("dn0")
 
     us, hb, br = r.us, r.hb, r.br
 
@@ -663,9 +735,9 @@
         return carry
 
     lax.fori_loop(0, N_HID, rise, 0)
-    head_core()
+    pass_z("dn0", 3)
+    pass_z("dn1", 2)
     pass_core("out")
-    pass_on("dn1")
     complete("out")
     lefts, rights = [], []
     for d in range(4):
@@ -674,12 +746,17 @@
         rights.append(part[:, 96:192])
     br[:, 0:384] = jnp.concatenate(lefts, axis=1)
     br[:, 384:768] = jnp.concatenate(rights, axis=1)
+    head_core()
     nbt[...] = nb[...].T
     brs, brr = r.brs, r.brr
-    tag_br = []
+    tag_br = {}
     for half in range(2):
         name = "dn%d" % half
         lanes = slice(half * 384, half * 384 + 384)
+        if half:
+            head_complete()
+        else:
+            pass_z("dn1", 3)
         pass_core(name)
         complete(name)
 
@@ -688,29 +765,34 @@
             return carry
 
         lax.fori_loop(0, N_HID, fall, 0)
-        brs[half] = br[ROWS : 2 * ROWS, lanes].astype(bfloat)
-        tag_br.append(send(brs.at[half], brr.at[half], x_dev))
-    head_complete()
-    x2, x3 = r.x2, r.x3
+        for i in (1, 0):
+            brs[half, i] = br[i * ROWS : (i + 1) * ROWS, lanes].astype(bfloat)
+            tag_br[half, i] = send(brs.at[half, i], brr.at[half, 1 - i], x_dev)
+    hw = r.hw
     for a in range(2):
         for d in range(4):
             for w in range(N_HID):
-                s = (a * 16 + d * 4 + w) * 24
+                s = (d * N_HID + w) * 24
                 block = ghd[a, d, w].astype(single)
-                x2[s : s + 24, :] = block[0:24]
-                x3[s : s + 24, :] = block[24:48]
-    for half in range(2):
-        arrive(brr.at[half], tag_br[half], x_dev)
-
-    stream0 = jnp.concatenate([st[0, 0], st[1, 0]], axis=1).astype(single)
-    theirs = jnp.concatenate([brr[0], brr[1]], axis=1).astype(single)
-    out_n, out_scale = norm_parts(stream0 + (br[0:ROWS, :] + theirs))
+                x0[s : s + 24, :] = block[0:24]
+                x1[s : s + 24, :] = block[24:48]
+        hw[0, a * 384 : a * 384 + 384, :] = x0[...].astype(bfloat)
+        hw[1, a * 384 : a * 384 + 384, :] = x1[...].astype(bfloat)
+
+    def stream_out(i):
+        for half in range(2):
+            arrive(brr.at[half, i], tag_br[half, 1 - i], x_dev)
+        stream = jnp.concatenate([st[0, i], st[1, i]], axis=1).astype(single)
+        theirs = jnp.concatenate([brr[0, i], brr[1, i]], axis=1).astype(single)
+        return norm_parts(stream + (br[i * ROWS : (i + 1) * ROWS, :] + theirs))
+
+    out_n, out_scale = stream_out(0)
     is_patch = iota((ROWS, 1), 0) < npatch
     final_gain = gain_row(1)
     n_sum = jnp.sum(jnp.where(is_patch, out_n, 0.0), axis=0, keepdims=True)
     pooled = n_sum * final_gain / npatch
     pooled_b = pooled.astype(bfloat)
-    heads_b = [x2[...].astype(bfloat), x3[...].astype(bfloat)]
+    heads_b = [hw[0], hw[1]]
     pooled_8 = jnp.broadcast_to(pooled_b, (16, 768))
     logits = jnp.concatenate([dot(pooled_8, m)[0:1] for m in heads_b], axis=1)
     lane = iota((1, 1024), 1)
@@ -725,11 +807,14 @@
     back = dot_nt(both[:, 0:512], heads_b[0]) + dot_nt(both[:, 512:1024], heads_b[1])
     d_pooled = (back[0:1] + back[1:2]) / npatch
     d_row = d_pooled * final_gain
+    rw = r.rw
+    rw[0] = jnp.broadcast_to(d_row, (8, 768))
+    tag_rw = send(rw.at[0], rw.at[1], x_dev)
+    ds, db, dbt = r.ds, r.db, r.dbt
     d_stream = jnp.where(is_patch, norm_back(out_n, out_scale, d_row), 0.0)
-    ds, db, dbt = r.ds, r.db, r.dbt
     ds[...] = d_stream
     db[0] = d_stream.astype(bfloat)
-    tag_db = send(db.at[0], db.at[1], x_dev)
+    dbt[:, 0:ROWS] = d_stream.T.astype(bfloat)
     d_final_gain = d_pooled * n_sum
     al = r.al
     pooled_f = pooled_b.astype(single)
@@ -740,9 +825,11 @@
         axis=0,
     )
     tag_al = [send(al.at[h, dp, z], al.at[h, dp, z], z_dev[k]) for k in range(1, N_HID)]
-    dbt[:, 0:ROWS] = d_stream.T.astype(bfloat)
-    arrive(db.at[1], tag_db, x_dev)
-    dbt[:, ROWS : 2 * ROWS] = db[1].astype(single).T.astype(bfloat)
+    out_n, out_scale = stream_out(1)
+    arrive(rw.at[1], tag_rw, x_dev)
+    d_stream = jnp.where(is_patch, norm_back(out_n, out_scale, rw[1, 0:1, :]), 0.0)
+    db[1] = d_stream.astype(bfloat)
+    dbt[:, ROWS : 2 * ROWS] = d_stream.T.astype(bfloat)
     db2 = db[...].reshape(2 * ROWS, 768)
 
     rff, f1, f2, ft, f3 = r.rff, r.f1, r.f2, r.ft, r.f3
@@ -785,19 +872,20 @@
             total = total + f3[k - 1].astype(single)
         r.g_up[...] = total[0].reshape(192, 384)
         r.g_down[...] = total[1].reshape(192, 384)
+        store("g_up")
+        store("g_down")
 
     ff_block(1)
+    ff_y(1)
     ff_block(2)
-    ff_y(1)
+    ff_y(2)
     for k in range(1, N_HID):
         arrive(al.at[h, dp, z_down[k]], tag_al[k - 1], z_dev[k])
     tag_ag = [send(al.at[h, dp], al.at[h, dp], device) for device in group_dev]
     ff_block(3)
-    ff_y(2)
-    ff_z(1)
+    ff_y(3)
     ff_block(0)
-    ff_y(3)
-    ff_z(2)
+    ff_y(0)
 
     rout, o1, o2, ot, o3 = r.rout, r.o1, r.o2, r.ot, r.o3
     pieces = [
@@ -817,57 +905,60 @@
         part = d_heads[:, n * HD : (n + 1) * HD].astype(bfloat)
         dh[2 * n] = part[0:ROWS]
         dh[2 * n + 1] = part[ROWS : 2 * ROWS]
-    ff_y(0)
+    ff_z(1)
 
     dq, dk, dv = ho, r.dk, r.dv
 
-    def attend_back(i, carry):
-        probs = pr[i]
-        d_out = dh[i]
-        d_probs = dot_nt(d_out, v_ref[i])
-        dv[i] = dot_tn(probs.astype(bfloat), d_out)
-        inner = jnp.sum(probs * d_probs, axis=-1, keepdims=True)
-        d_scores = (probs * (d_probs - inner)).astype(bfloat)
-        dq[i] = dot(d_scores, k_ref[i]) * HD ** (-0.5)
-        dk[i] = dot_tn(d_scores, q_ref[i]) * HD ** (-0.5)
+    def attend_back(n, carry):
+        for i in (2 * n, 2 * n + 1):
+            probs = pr[i]
+            d_out = dh[i]
+            d_probs = dot_nt(d_out, v_ref[i])
+            dv[i] = dot_tn(probs.astype(bfloat), d_out)
+            inner = jnp.sum(probs * d_probs, axis=-1, keepdims=True)
+            d_scores = (probs * (d_probs - inner)).astype(bfloat)
+            dq[i] = dot(d_scores, k_ref[i]) * HD ** (-0.5)
+            dk[i] = dot_tn(d_scores, q_ref[i]) * HD ** (-0.5)
         return carry
 
-    lax.fori_loop(0, 4, attend_back, 0)
-    ff_z(3)
     arrive(o1, tag_o1, core_dev)
     o1[...] = o1[...] + rout[:, :, core]
     tag_o2 = send(o1.at[:, 1 - y], o2, y_dev)
-    lax.fori_loop(4, 8, attend_back, 0)
-    ff_z(0)
-    lax.fori_loop(8, 12, attend_back, 0)
+    lax.fori_loop(0, 3, attend_back, 0)
+    ff_z(2)
+    lax.fori_loop(3, 6, attend_back, 0)
+    ff_z(3)
 
     rqkv, q1, q2, qt, q3 = r.rqkv, r.q1, r.q2, r.qt, r.q3
-    gain_sums = []
-    for c, (grads, normed, scales, gain) in enumerate(
-        ((dq, qn, qr, q_gain), (dk, kn, kr, k_gain), (dv, None, None, None))
+    gain_sums, dm = [], hb
+    for c, (grads, kept, gain) in enumerate(
+        ((dq, qn, q_gain), (dk, kn, k_gain), (dv, None, None))
     ):
         parts, sums = [], []
         for n in range(6):
             grad = jnp.concatenate([grads[2 * n], grads[2 * n + 1]], axis=0)
-            if normed is not None:
-                sums.append(jnp.sum(grad * normed[n], axis=0, keepdims=True))
-                grad = norm_back(normed[n], scales[n], grad * gain[:, n * HD : (n + 1) * HD])
+            if kept is not None:
+                normed, scale = kept[n, :, 0:HD], kept[n, :, HD : HD + 1]
+                sums.append(jnp.sum(grad * normed, axis=0, keepdims=True))
+                grad = norm_back(normed, scale, grad * gain[:, n * HD : (n + 1) * HD])
             parts.append(grad)
         if sums:
             gain_sums.append(jnp.concatenate(sums, axis=1))
-        d_mixed = jnp.concatenate(parts, axis=1).astype(bfloat)
-        rqkv[c] = dot(nbt[...], d_mixed).astype(bfloat).reshape(2, 2, 2, 2, 48, 384)
-        dn[...] += dot_nt(d_mixed, gqkv[c].reshape(768, 384))
-    tag_q1 = send(rqkv.at[:, :, :, 1 - core], q1, core_dev)
+        dm[c] = jnp.concatenate(parts, axis=1).astype(bfloat)
+        dn[...] += dot_nt(dm[c], gqkv[c].reshape(768, 384))
     dns, dnr = r.dns, r.dnr
     dns[...] = dn[ROWS : 2 * ROWS, :].astype(bfloat)
     tag_dn = send(dns, dnr, x_dev)
+    for c in range(3):
+        rqkv[c] = dot(nbt[...], dm[c]).astype(bfloat).reshape(2, 2, 2, 2, 48, 384)
+    tag_q1 = send(rqkv.at[:, :, :, 1 - core], q1, core_dev)
+    ff_z(0)
+    arrive(q1, tag_q1, core_dev)
+    q1[...] = q1[...] + rqkv[:, :, :, core]
+    tag_q2 = send(q1.at[:, :, 1 - y], q2, y_dev)
     arrive(o2, tag_o2, y_dev)
     ot[...] = o1[:, y] + o2[...]
     tag_o3 = [send(ot.at[z_up[k]], o3.at[k - 1], z_dev[k]) for k in range(1, N_HID)]
-    arrive(q1, tag_q1, core_dev)
-    q1[...] = q1[...] + rqkv[:, :, :, core]
-    tag_q2 = send(q1.at[:, :, 1 - y], q2, y_dev)
 
     for i, (gh, gd) in enumerate(group):
         arrive(al.at[gh, gd], tag_ag[i], group_dev[i])
@@ -879,10 +970,11 @@
     mine = dot_nt(chosen, pooled_all.astype(bfloat))
     g_head = jnp.dot(mine, d_logits_all, precision=highest, preferred_element_type=single)
     r.g_head[...] = g_head[:, 0:classes]
+    store("g_head")
 
     arrive(dnr, tag_dn, x_dev)
     d_normed = dn[0:ROWS, :] + dnr[...].astype(single)
-    block_n, block_scale = norm_parts(stream0)
+    block_n, block_scale = norm_parts(jnp.concatenate([st[0, 0], st[1, 0]], axis=1).astype(single))
     d_block_gain = jnp.sum(d_normed * block_n, axis=0, keepdims=True)
     d_in = ds[...] + norm_back(block_n, block_scale, d_normed * block_gain)
     dx, gg = r.dx, r.gg
@@ -943,6 +1035,7 @@
         arrive(o3.at[k - 1], tag_o3[k - 1], z_dev[k])
         total = total + o3[k - 1].astype(single)
     r.g_out[...] = total[:, 0:192]
+    store("g_out")
     arrive(e2, tag_e2, y_dev)
     et[...] = e1[y] + e2[...]
     tag_e3 = [send(et.at[z_up[k]], e3.at[k - 1], z_dev[k]) for k in range(1, N_HID)]
@@ -951,6 +1044,7 @@
         arrive(q3.at[k - 1], tag_q3[k - 1], z_dev[k])
         total = total + q3[k - 1].astype(single)
     r.g_qkv[...] = total
+    store("g_qkv")
     total = et[z].astype(single)
     for k in range(1, N_HID):
         arrive(e3.at[k - 1], tag_e3[k - 1], z_dev[k])
@@ -961,6 +1055,8 @@
     columns = total[24:48, 256:512]
     pick_f = (iota((8, 256), 1) == iota((8, 256), 0) + seq_len).astype(single)
     r.g_gains[...] = dot_nt(pick_f, columns, precision=highest)[0:4]
+    for name in ("g_patch", "g_table", "g_gains"):
+        store(name)
 
 
     def read(prefix, kind):
@@ -995,6 +1091,8 @@
     grad_norm = jnp.sqrt(jnp.sum(jnp.where(lane == 1, sums, 0.0), axis=1, keepdims=True))[0:1]
     clip = jnp.minimum(1.0, clip_at / grad_norm)
     own = jnp.zeros((8, 128), single)
+    for name in order[9:]:
+        loads[name].wait()
     for n, kind in enumerate(KINDS):
         update = one_update(read("w_", kind), read("m_", kind), read("v_", kind), read("g_", kind), clip)[2]
         own = jnp.where(lane == 8 + n, square_sum(update), own)
@@ -1004,30 +1102,61 @@
     result = jnp.where(lane == 1, grad_norm, result)
     result = jnp.where(lane == 2, clip, result)
     r.scalars[...] = result
-    for copy in sends:
-        copy.wait_send()
+    store("scalars")
+    for copy in stores:
+        copy.wait()
+    for key, copies in sends.items():
+
+        def settle(copies=copies):
+            for copy in copies:
+                copy.wait_send()
+
+        if key is None:
+            settle()
+        else:
+            pl.when(holds[key])(settle)
 
 
 def write_kernel(names, *refs):
     r = types.SimpleNamespace(**dict(zip(names, refs)))
     lane = iota((8, 128), 1)
+    inputs = ["scalars"] + [p + k for k in KINDS for p in ("w_", "m_", "v_", "g_")]
+    loads = {}
+    for number, name in enumerate(inputs):
+        loads[name] = pltpu.make_async_copy(
+            getattr(r, "h_" + name), getattr(r, name), r.lsem.at[number]
+        )
+        loads[name].start()
+    loads["scalars"].wait()
 
     def pick(n):
         return jnp.sum(jnp.where(lane == n, r.scalars[...], 0.0), axis=1, keepdims=True)[0:1]
 
     clip = pick(2)
+    stores = []
     for n, kind in enumerate(KINDS):
+        for p in ("w_", "m_", "v_", "g_"):
+            loads[p + kind].wait()
         master = getattr(r, "w_" + kind)[...]
         grad = getattr(r, "g_" + kind)[...]
-        ratio = pick(8 + n)
+        ratio, c = pick(8 + n), clip
         if len(master.shape) == 3:
             c, ratio = clip[None], ratio[None]
-        else:
-            c = clip
-        first, second, update = one_update(master, getattr(r, "m_" + kind)[...], getattr(r, "v_" + kind)[...], grad, c)
-        getattr(r, "nm_" + kind)[...] = first
-        getattr(r, "nv_" + kind)[...] = second
-        getattr(r, "nw_" + kind)[...] = master - learn_rate * ratio * update
+        first, second, update = one_update(
+            master, getattr(r, "m_" + kind)[...], getattr(r, "v_" + kind)[...], grad, c
+        )
+        results = (first, second, master - learn_rate * ratio * update)
+        for p, value in zip(("nm_", "nv_", "nw_"), results):
+            getattr(r, p + kind)[...] = value
+            copy = pltpu.make_async_copy(
+                getattr(r, p + kind),
+                getattr(r, "h_" + p + kind),
+                r.lsem.at[len(inputs) + len(stores)],
+            )
+            copy.start()
+            stores.append(copy)
+    for copy in stores:
+        copy.wait()
 
 
 def fast_device(patches, labels, *state):
@@ -1041,9 +1170,9 @@
         return value
 
     flat = [turn(KINDS[i % 8], value) for i, value in enumerate(state)]
-    vmem = pl.BlockSpec(memory_space=pltpu.VMEM)
+    hbm = pl.BlockSpec(memory_space=pl.ANY)
     smem = pl.BlockSpec(memory_space=pltpu.SMEM)
-    in_names = ["labels", "patches"] + [p + k for p in ("w_", "m_", "v_") for k in KINDS]
+    in_names = ["patches"] + [p + k for p in ("w_", "m_", "v_") for k in KINDS]
     out_names = ["g_" + k for k in KINDS] + ["scalars"]
     scratch = dict(
         px=((2, ROWS, 1024), bfloat),
@@ -1055,16 +1184,13 @@
         ghd=((2, 4, 4, 48, 512), bfloat),
         x0=((384, 512), single),
         x1=((384, 512), single),
-        x2=((768, 512), single),
-        x3=((768, 512), single),
+        hw=((2, 768, 512), bfloat),
         ga=((2, 8, 384), single),
         st=((2, 2, ROWS, 384), bfloat),
         nb=((2 * ROWS, 768), bfloat),
         nbt=((768, 2 * ROWS), bfloat),
-        qn=((6, 2 * ROWS, HD), single),
-        kn=((6, 2 * ROWS, HD), single),
-        qr=((6, 2 * ROWS, 1), single),
-        kr=((6, 2 * ROWS, 1), single),
+        qn=((6, 2 * ROWS, 2 * HD), single),
+        kn=((6, 2 * ROWS, 2 * HD), single),
         q=((12, ROWS, HD), bfloat),
         k=((12, ROWS, HD), bfloat),
         v=((12, ROWS, HD), bfloat),
@@ -1074,8 +1200,9 @@
         us=((4, 2 * ROWS, 384), single),
         hb=((4, 2 * ROWS, 384), bfloat),
         br=((2 * ROWS, 768), single),
-        brs=((2, ROWS, 384), bfloat),
-        brr=((2, ROWS, 384), bfloat),
+        brs=((2, 2, ROWS, 384), bfloat),
+        brr=((2, 2, ROWS, 384), bfloat),
+        rw=((2, 8, 768), single),
         ds=((ROWS, 768), single),
         db=((2, ROWS, 768), bfloat),
         dbt=((768, 2 * ROWS), bfloat),
@@ -1112,37 +1239,41 @@
         v1=((2, 4, 8, 128), single),
         v2=((2, 4, 8, 128), single),
     )
-    semaphores = 180
+    semaphores = 256
     shapes = [flat[i].shape for i in range(8)]
     npatch, seq_len, classes = patches.shape[1], flat[1].shape[1], flat[3].shape[1]
     total_images = labels.shape[0] * lax.axis_size("dp")
     sizes = (npatch, seq_len, classes, total_images)
-    names = in_names + out_names + list(scratch) + ["ssem", "rsem"]
+    held = [(patches.shape, bfloat)] + [(s, single) for s in shapes * 4] + [((8, 128), single)]
+    names = ["labels"] + ["h_" + n for n in in_names + out_names] + in_names + out_names
+    names += list(scratch) + ["ssem", "rsem", "lsem"]
     found = pl.pallas_call(
         functools.partial(step_kernel, sizes, names),
         out_shape=[jax.ShapeDtypeStruct(s, single) for s in shapes]
         + [jax.ShapeDtypeStruct((8, 128), single)],
-        in_specs=[smem] + [vmem] * 25,
-        out_specs=[vmem] * 9,
-        scratch_shapes=[pltpu.VMEM(s, t) for s, t in scratch.values()]
-        + [pltpu.SemaphoreType.DMA((semaphores,))] * 2,
+        in_specs=[smem] + [hbm] * 25,
+        out_specs=[hbm] * 9,
+        scratch_shapes=[pltpu.VMEM(s, t) for s, t in held + list(scratch.values())]
+        + [pltpu.SemaphoreType.DMA((semaphores,))] * 2
+        + [pltpu.SemaphoreType.DMA((len(held),))],
         compiler_params=pltpu.CompilerParams(
             collective_id=0, has_side_effects=True, vmem_limit_bytes=62 * 2**20
         ),
         name="train_step",
     )(labels, patches, *flat)
     grads, scalars = found[:8], found[8]
-    names = (
-        ["scalars"]
-        + [p + k for p in ("w_", "m_", "v_", "g_") for k in KINDS]
-        + [p + k for p in ("nm_", "nv_", "nw_") for k in KINDS]
-    )
+    in_names = ["scalars"] + [p + k for p in ("w_", "m_", "v_", "g_") for k in KINDS]
+    out_names = [p + k for p in ("nm_", "nv_", "nw_") for k in KINDS]
+    held = [((8, 128), single)] + [(s, single) for s in shapes * 7]
+    names = ["h_" + n for n in in_names + out_names] + in_names + out_names + ["lsem"]
     written = pl.pallas_call(
         functools.partial(write_kernel, names),
         out_shape=[jax.ShapeDtypeStruct(s, single) for s in shapes * 3],
-        in_specs=[vmem] * 33,
-        out_specs=[vmem] * 24,
-        compiler_params=pltpu.CompilerParams(vmem_limit_bytes=48 * 2**20),
+        in_specs=[hbm] * 33,
+        out_specs=[hbm] * 24,
+        scratch_shapes=[pltpu.VMEM(s, t) for s, t in held]
+        + [pltpu.SemaphoreType.DMA((len(held),))],
+        compiler_params=pltpu.CompilerParams(vmem_limit_bytes=62 * 2**20),
         name="write_step",
     )(scalars, *flat, *grads)
     back = [turn(KINDS[i % 8], value) for i, value in enumerate(written)]

time: 202 us -> 171 us (0.85)
  local copies, waits for them, and re-layouts: 18.8 us -> 1.33 us
  Pallas kernels: 181 us -> 169 us
    unnamed x66 -> x0, local copies, waits for them, and re-layouts: 18.2 us -> none
    pallas_call x1, Pallas kernels: 179 us -> 165 us  [fast_device(): pl.pallas_call(functools.partial(step_kernel, sizes, names), out_shape=[j...]
    pallas_call x1, Pallas kernels: 2.34 us -> 4.49 us  [fast_device(): pl.pallas_call(functools.partial(write_kernel, names), out_shape=[jax.Sha...]
where the time goes in v2:
time: 171 us
  Pallas kernels  169 us (99%)
    pallas_call x1, Pallas kernels, fast_device(): pl.pallas_call(functools.partial(step_kernel, sizes, names), out_shape=[j...  165 us
    pallas_call x1, Pallas kernels, fast_device(): pl.pallas_call(functools.partial(write_kernel, names), out_shape=[jax.Sha...  4.49 us

profile of v2, /device:TPU:0, one launch (start us, length us, event | category | flops | bytes accessed | tf_op | source)
XLA Modules:
  0.0 171.2 jit_solution(206322974128506686)
XLA Ops:
  0.7 164.7 %train_step.1 = (f32[24,768]{1,0:T(8,128)}, f32[24,200]{1,0:T(8,128)}, f32[4,24]{1,0:T(4,128)}, f32[24,1000]{1,0:T(8,128)}, f32[3,48,384]{2,1,0:T(8,128)}, /*ind...) custom-call(s32[8]{0:T(128)} %refs_0_.1, bf16[1,196,768]{2,1,0:T(8,128)(2,1)} %refs_1_.1, ...), custom_call_target="tpu_custom_call" | custom-call | tf_op jit(solution)/shard_map/train_step/pallas_call | solution.py:1250
  165.3 4.5 %write_step.1 = (f32[24,768]{1,0:T(8,128)}, f32[24,200]{1,0:T(8,128)}, f32[4,24]{1,0:T(4,128)}, f32[24,1000]{1,0:T(8,128)}, f32[3,48,384]{2,1,0:T(8,128)}, /*ind...) custom-call(f32[8,128]{1,0:T(8,128)} %get-tuple-element.59.refs_0_, ...), custom_call_target="tpu_custom_call" | custom-call | tf_op jit(solution)/shard_map/write_step/pallas_call | solution.py:1269
  169.8 1.3 fusion

commit v3 on v2

--- a/solution.py
+++ b/solution.py
@@ -373,6 +373,8 @@
 
 
 KINDS = ("patch", "table", "gains", "head", "qkv", "out", "up", "down")
+EXT, QKV, UP0, UP1, HEAD, OUT, DN0, DN1 = range(8)
+LEFT, RIGHT, ON_LEFT, ON_RIGHT = "left", "right", "on_left", "on_right"
 ROWS = 208
 N_HID = 4
 
@@ -426,13 +428,13 @@
     last = N_HID - 1
     holds = {}
     for d in range(1, N_HID):
-        holds["left", d] = z >= d
-        holds["right", d] = z + d <= last
-        holds["on_right", d] = (z >= d) & (z < last)
-        holds["on_left", d] = (z + d <= last) & (z > 0)
-    holds["on_right", 0] = z < last
-    holds["on_left", 0] = z > 0
-    next_z = {"left": (dp, h, z_up[1]), "right": (dp, h, z_down[1])}
+        holds[LEFT, d] = z >= d
+        holds[RIGHT, d] = z + d <= last
+        holds[ON_RIGHT, d] = (z >= d) & (z < last)
+        holds[ON_LEFT, d] = (z + d <= last) & (z > 0)
+    holds[ON_RIGHT, 0] = z < last
+    holds[ON_LEFT, 0] = z > 0
+    next_z = {LEFT: (dp, h, z_up[1]), RIGHT: (dp, h, z_down[1])}
 
     def send(source, target, device, key=None):
         number = count[0]
@@ -464,6 +466,7 @@
 
     gext, gqkv, gout, gup, gdn, ghd = r.gext, r.gqkv, r.gout, r.gup, r.gdn, r.ghd
     x0, x1, px = r.x0, r.x1, r.px
+    kept = types.SimpleNamespace()
 
     def pack_ext():
         x1[0:24, :] = jnp.zeros((24, 512), single)
@@ -486,26 +489,29 @@
         loads["patches"].wait()
         px[0, 0:npatch, 0:768] = r.patches[0]
 
-    def pack_rest():
+    def pack_qkv():
         loads["w_qkv"].wait()
         gqkv[:, z // 2, dp, lax.rem(z, 2)] = r.w_qkv[...].astype(bfloat)
-        yield
+
+    def pack_up():
         loads["w_up"].wait()
         gup[z, :, dp] = r.w_up[...].astype(bfloat).reshape(2, 96, 384)
-        yield
+
+    def pack_head():
         loads["w_head"].wait()
         x0[0:24, :] = r.w_head[:, 0:512]
         x1[0:24, :] = jnp.zeros((24, 512), single)
         x1[0:24, 0 : classes - 512] = r.w_head[:, 512:classes]
         ghd[h, dp, z] = jnp.concatenate([x0[0:24, :], x1[0:24, :]], axis=0).astype(bfloat)
-        yield
+
+    def pack_out():
         loads["w_out"].wait()
         gout[dp, z] = jnp.zeros((96, 256), bfloat)
         gout[dp, z, :, 0:192] = r.w_out[...].astype(bfloat)
-        yield
+
+    def pack_down():
         loads["w_down"].wait()
         gdn[z, :, dp] = r.w_down[...].astype(bfloat).reshape(2, 96, 384)
-        yield
 
     def at_ext(d, w):
         return gext.at[d, w]
@@ -526,42 +532,45 @@
         return ghd.at[h, d, w]
 
     slot = {
-        "ext": at_ext,
-        "qkv": at_qkv,
-        "out": at_out,
-        "up0": at_up(0),
-        "up1": at_up(1),
-        "dn0": at_dn(0),
-        "dn1": at_dn(1),
-        "hd": at_hd,
+        EXT: at_ext,
+        QKV: at_qkv,
+        OUT: at_out,
+        UP0: at_up(0),
+        UP1: at_up(1),
+        DN0: at_dn(0),
+        DN1: at_dn(1),
+        HEAD: at_hd,
     }
     lines = {
-        "ext": lambda d: gext.at[d],
-        "qkv": lambda d: gqkv.at[:, :, d],
-        "out": lambda d: gout.at[d],
-        "up0": lambda d: gup.at[:, 0, d],
-        "up1": lambda d: gup.at[:, 1, d],
-        "dn0": lambda d: gdn.at[:, 0, d],
-        "dn1": lambda d: gdn.at[:, 1, d],
-        "hd": lambda d: ghd.at[h, d],
+        EXT: lambda d: gext.at[d],
+        QKV: lambda d: gqkv.at[:, :, d],
+        OUT: lambda d: gout.at[d],
+        UP0: lambda d: gup.at[:, 0, d],
+        UP1: lambda d: gup.at[:, 1, d],
+        DN0: lambda d: gdn.at[:, 0, d],
+        DN1: lambda d: gdn.at[:, 1, d],
+        HEAD: lambda d: ghd.at[h, d],
     }
     tags = {}
 
-    def send_own(name):
+    def own_z(name):
         own = slot[name](dp, z)
-        tags[name, "left", 1] = send(own, own, next_z["left"], ("on_right", 0))
-        tags[name, "right", 1] = send(own, own, next_z["right"], ("on_left", 0))
+        tags[name, LEFT, 1] = send(own, own, next_z[LEFT], (ON_RIGHT, 0))
+        tags[name, RIGHT, 1] = send(own, own, next_z[RIGHT], (ON_LEFT, 0))
+
+    def own_y(name):
+        own = slot[name](dp, z)
         tags[name, "y", 0] = send(own, own, y_dev)
 
     def pass_z(name, d):
-        for side, on, theirs in (("left", "on_right", z_down[d]), ("right", "on_left", z_up[d])):
+        for side, on, theirs in ((LEFT, ON_RIGHT, z_down[d]), (RIGHT, ON_LEFT, z_up[d])):
             block = slot[name](dp, theirs)
             number = tags[name, side, d]
             pl.when(holds[side, d])(functools.partial(arrive, block, number, y_dev))
             if d < last:
                 tags[name, side, d + 1] = send(block, block, next_z[side], (on, d))
             tags[name, "y", side, d] = send(block, block, y_dev, (side, d))
-        if d == last and name != "hd":
+        if d == last and name != HEAD:
             line = lines[name](dp)
             tags[name, "c", 0] = send(line, line, core_dev)
 
@@ -569,11 +578,11 @@
         at = slot[name]
         arrive(at(y_dp, z), tags[name, "y", 0], y_dev)
         for d in range(1, N_HID):
-            for side, theirs in (("left", z_down[d]), ("right", z_up[d])):
+            for side, theirs in ((LEFT, z_down[d]), (RIGHT, z_up[d])):
                 number = tags[name, "y", side, d]
                 pl.when(holds[side, d])(functools.partial(arrive, at(y_dp, theirs), number, y_dev))
         line = lines[name](y_dp)
-        if name != "hd":
+        if name != HEAD:
             tags[name, "c", 1] = send(line, line, core_dev)
         else:
             own = lines[name](dp)
@@ -587,65 +596,42 @@
 
     def head_core():
         for i, d in enumerate((dp, y_dp)):
-            arrive(ghd.at[1 - h, d], tags["hd", "x", i], x_dev)
+            arrive(ghd.at[1 - h, d], tags[HEAD, "x", i], x_dev)
         for i, d in enumerate((dp, y_dp)):
             block = ghd.at[:, d]
-            tags["hd", "c", i] = send(block, block, core_dev)
+            tags[HEAD, "c", i] = send(block, block, core_dev)
 
     def head_complete():
         far = (1 - y) * 2 + (1 - core)
         for i, d in enumerate((core_dp, far)):
-            arrive(ghd.at[:, d], tags["hd", "c", i], core_dev)
-
-    pack_ext()
-    pl.semaphore_wait(barrier, len(z_dev) - 1 + len(group_dev))
-    send_own("ext")
-    packing = pack_rest()
-    next(packing)
-    send_own("qkv")
-    pass_z("ext", 1)
-    pack_patches()
-    images = px.at[0, :, pl.ds(0, 768)]
-    tag_px = send(images, px.at[1, :, pl.ds(0, 768)], x_dev)
-    next(packing)
-    send_own("up0")
-    pass_z("ext", 2)
-    pass_z("qkv", 1)
-    send_own("up1")
-    pass_z("ext", 3)
-    for _ in packing:
-        pass
-    pass_z("qkv", 2)
-    pass_z("up0", 1)
-    send_own("hd")
-    pass_core("ext")
-    complete("ext")
-
-    for d in range(4):
-        for w in range(N_HID):
-            s = (d * N_HID + w) * 24
-            block = gext[d, w].astype(single)
-            x0[s : s + 24, :] = block[0:24]
-            x1[s : s + 24, :] = block[24:48]
-    x1b = x1[...].astype(bfloat)
-    ga = r.ga
+            arrive(ghd.at[:, d], tags[HEAD, "c", i], core_dev)
+
+    def send_images():
+        images = px.at[0, :, pl.ds(0, 768)]
+        tags["px"] = send(images, px.at[1, :, pl.ds(0, 768)], x_dev)
+
+    ga, st = r.ga, r.st
     rows_of = (iota((8, 512), 1) == iota((8, 512), 0) + (256 + seq_len)) & (iota((8, 512), 0) < 4)
-    ga[h] = dot_nt(rows_of.astype(bfloat), x1b)
-    tag_ga = send(ga.at[h], ga.at[h], x_dev)
-    x0b = x0[...].astype(bfloat)
-    st = r.st
-    st[h, 0] = (dot_nt(px[0, :, 0:512], x0b) + dot_nt(px[0, :, 512:1024], x1b)).astype(bfloat)
-    tag_st0 = send(st.at[h, 0], st.at[h, 1], x_dev)
-    arrive(px.at[1, :, pl.ds(0, 768)], tag_px, x_dev)
-    st[h, 1] = (dot_nt(px[1, :, 0:512], x0b) + dot_nt(px[1, :, 512:1024], x1b)).astype(bfloat)
-    tag_st1 = send(st.at[h, 1], st.at[h, 0], x_dev)
-    pass_z("qkv", 3)
-    pass_z("up0", 2)
-    pass_z("up1", 1)
-    send_own("out")
-    arrive(ga.at[1 - h], tag_ga, x_dev)
-    arrive(st.at[1 - h, 1], tag_st0, x_dev)
-    arrive(st.at[1 - h, 0], tag_st1, x_dev)
+
+    def unpack(block_of, low, high):
+        for d in range(4):
+            for w in range(N_HID):
+                s = (d * N_HID + w) * 24
+                block = block_of(d, w).astype(single)
+                low[s : s + 24, :] = block[0:24]
+                high[s : s + 24, :] = block[24:48]
+
+    def embed(i):
+        if i == 0:
+            unpack(lambda d, w: gext[d, w], x0, x1)
+            ga[h] = dot_nt(rows_of.astype(bfloat), x1[...].astype(bfloat))
+            tags["ga"] = send(ga.at[h], ga.at[h], x_dev)
+        else:
+            arrive(px.at[1, :, pl.ds(0, 768)], tags["px"], x_dev)
+        low, high = x0[...].astype(bfloat), x1[...].astype(bfloat)
+        made = dot_nt(px[i, :, 0:512], low) + dot_nt(px[i, :, 512:1024], high)
+        st[h, i] = made.astype(bfloat)
+        tags["st", i] = send(st.at[h, i], st.at[h, 1 - i], x_dev)
 
     def gain_row(i):
         return jnp.concatenate([ga[0, i : i + 1, :], ga[1, i : i + 1, :]], axis=1)
@@ -660,71 +646,60 @@
         return jnp.where(h == 0, low, high)
 
     nb, nbt = r.nb, r.nbt
-    block_gain = gain_row(0)
-    for i in range(2):
-        stream = jnp.concatenate([st[0, i], st[1, i]], axis=1).astype(single)
-        nb[i * ROWS : (i + 1) * ROWS, :] = (norm_parts(stream)[0] * block_gain).astype(bfloat)
-    pass_z("up0", 3)
-    pass_z("up1", 2)
-    pass_z("hd", 1)
-    send_own("dn0")
-    pass_core("qkv")
-    complete("qkv")
-
-    qn, kn = r.qn, r.kn
+
+    def block_norm():
+        arrive(ga.at[1 - h], tags["ga"], x_dev)
+        arrive(st.at[1 - h, 1], tags["st", 0], x_dev)
+        arrive(st.at[1 - h, 0], tags["st", 1], x_dev)
+        gain = gain_row(0)
+        for i in range(2):
+            stream = jnp.concatenate([st[0, i], st[1, i]], axis=1).astype(single)
+            nb[i * ROWS : (i + 1) * ROWS, :] = (norm_parts(stream)[0] * gain).astype(bfloat)
+
+    nq, sq, bd = r.nq, r.sq, r.bd
     q_ref, k_ref, v_ref = r.q, r.k, r.v
-    q_gain, k_gain = head_gain(2), head_gain(3)
-    for c, (keep, out, gain) in enumerate(
-        ((qn, q_ref, q_gain), (kn, k_ref, k_gain), (None, v_ref, None))
-    ):
+
+    def head_mean(values):
+        return dot(values.astype(bfloat), bd[...])
+
+    def project(c):
         mixed = dot(nb[...], gqkv[c].reshape(768, 384))
+        if c == 0:
+            same = iota((384, 384), 0) // HD == iota((384, 384), 1) // HD
+            bd[...] = jnp.where(same, 1.0 / HD, 0.0).astype(bfloat)
+        if c < 2:
+            top = mixed.astype(bfloat).astype(single)
+            center = mixed - (head_mean(top) + head_mean(mixed - top))
+            scale = lax.rsqrt(head_mean(center * center) + norm_eps)
+            normed = center * scale
+            nq[c] = normed
+            sq[c] = scale
+            mixed = normed * head_gain(2 + c)
+        out = (q_ref, k_ref, v_ref)[c]
+        mixed = mixed.astype(bfloat)
         for n in range(6):
             part = mixed[:, n * HD : (n + 1) * HD]
-            if keep is not None:
-                part, scale = norm_parts(part)
-                keep[n, :, 0:HD] = part
-                keep[n, :, HD : 2 * HD] = jnp.broadcast_to(scale, (2 * ROWS, HD))
-                part = part * gain[:, n * HD : (n + 1) * HD]
-            part = part.astype(bfloat)
             out[2 * n] = part[0:ROWS]
             out[2 * n + 1] = part[ROWS : 2 * ROWS]
-        if c == 0:
-            pass_z("up1", 3)
-            pass_z("hd", 2)
-            pass_z("out", 1)
-            send_own("dn1")
-            pass_core("up0")
-
-    pr, ho = r.pr, r.ho
+
+    pr, hof = r.pr, r.hof
     dead = iota((ROWS, ROWS), 1) >= seq_len
 
-    def attend(n, carry):
-        for i in (2 * n, 2 * n + 1):
-            scores = dot_nt(q_ref[i], k_ref[i]) * HD ** (-0.5)
-            scores = jnp.where(dead, -1e30, scores)
-            scores = scores - jnp.max(scores, axis=-1, keepdims=True)
-            weights = jnp.exp(scores)
-            probs = weights / jnp.sum(weights, axis=-1, keepdims=True)
-            pr[i] = probs
-            ho[i] = dot(probs.astype(bfloat), v_ref[i])
+    def attend(pair, carry):
+        for i in range(2):
+            made = []
+            for side in range(2):
+                n = 4 * pair + 2 * side + i
+                scores = dot_nt(q_ref[n], k_ref[n]) * HD ** (-0.5)
+                scores = jnp.where(dead, -1e30, scores)
+                scores = scores - jnp.max(scores, axis=-1, keepdims=True)
+                weights = jnp.exp(scores)
+                probs = weights / jnp.sum(weights, axis=-1, keepdims=True)
+                pr[n] = probs
+                made.append(dot(probs.astype(bfloat), v_ref[n]))
+            both = jnp.concatenate(made, axis=1).astype(bfloat)
+            hof[i * ROWS : (i + 1) * ROWS, pl.ds(pl.multiple_of(pair * 128, 128), 128)] = both
         return carry
-
-    lax.fori_loop(0, 2, attend, 0)
-    pass_z("hd", 3)
-    pass_z("out", 2)
-    pass_z("dn0", 1)
-    pass_core("up1")
-    lax.fori_loop(2, 6, attend, 0)
-    pass_z("out", 3)
-    pass_z("dn0", 2)
-    pass_z("dn1", 1)
-    pass_core("hd")
-    hof = r.hof
-    for i in range(2):
-        joined = jnp.concatenate([ho[2 * n + i] for n in range(6)], axis=1)
-        hof[i * ROWS : (i + 1) * ROWS, :] = joined.astype(bfloat)
-    complete("up0")
-    complete("up1")
 
     us, hb, br = r.us, r.hb, r.br
 
@@ -734,57 +709,136 @@
         hb[w] = (0.5 * upper * (1.0 + gelu_tanh(upper))).astype(bfloat)
         return carry
 
-    lax.fori_loop(0, N_HID, rise, 0)
-    pass_z("dn0", 3)
-    pass_z("dn1", 2)
-    pass_core("out")
-    complete("out")
-    lefts, rights = [], []
-    for d in range(4):
-        part = dot(hof[...], gout[d].reshape(384, 256))
-        lefts.append(part[:, 0:96])
-        rights.append(part[:, 96:192])
-    br[:, 0:384] = jnp.concatenate(lefts, axis=1)
-    br[:, 384:768] = jnp.concatenate(rights, axis=1)
-    head_core()
-    nbt[...] = nb[...].T
+    def project_out():
+        lefts, rights = [], []
+        for d in range(4):
+            part = dot(hof[...], gout[d].reshape(384, 256))
+            lefts.append(part[:, 0:96])
+            rights.append(part[:, 96:192])
+        br[:, 0:384] = jnp.concatenate(lefts, axis=1)
+        br[:, 384:768] = jnp.concatenate(rights, axis=1)
+
+    def turn_normed():
+        nbt[...] = nb[...].T
+
     brs, brr = r.brs, r.brr
-    tag_br = {}
-    for half in range(2):
-        name = "dn%d" % half
+
+    def fall(half):
         lanes = slice(half * 384, half * 384 + 384)
-        if half:
-            head_complete()
-        else:
-            pass_z("dn1", 3)
-        pass_core(name)
-        complete(name)
-
-        def fall(w, carry):
+
+        def add(w, carry):
             br[:, lanes] += dot_nt(hb[w], gdn[w, half].reshape(384, 384))
             return carry
 
-        lax.fori_loop(0, N_HID, fall, 0)
-        for i in (1, 0):
-            brs[half, i] = br[i * ROWS : (i + 1) * ROWS, lanes].astype(bfloat)
-            tag_br[half, i] = send(brs.at[half, i], brr.at[half, 1 - i], x_dev)
+        lax.fori_loop(0, N_HID, add, 0)
+
+    def share(half, i):
+        lanes = slice(half * 384, half * 384 + 384)
+        brs[half, i] = br[i * ROWS : (i + 1) * ROWS, lanes].astype(bfloat)
+        tags["br", half, i] = send(brs.at[half, i], brr.at[half, 1 - i], x_dev)
+
     hw = r.hw
-    for a in range(2):
-        for d in range(4):
-            for w in range(N_HID):
-                s = (d * N_HID + w) * 24
-                block = ghd[a, d, w].astype(single)
-                x0[s : s + 24, :] = block[0:24]
-                x1[s : s + 24, :] = block[24:48]
-        hw[0, a * 384 : a * 384 + 384, :] = x0[...].astype(bfloat)
-        hw[1, a * 384 : a * 384 + 384, :] = x1[...].astype(bfloat)
+
+    def unpack_head():
+        for a in range(2):
+            unpack(lambda d, w: ghd[a, d, w], x0, x1)
+            hw[0, a * 384 : a * 384 + 384, :] = x0[...].astype(bfloat)
+            hw[1, a * 384 : a * 384 + 384, :] = x1[...].astype(bfloat)
 
     def stream_out(i):
         for half in range(2):
-            arrive(brr.at[half, i], tag_br[half, 1 - i], x_dev)
+            arrive(brr.at[half, i], tags["br", half, 1 - i], x_dev)
         stream = jnp.concatenate([st[0, i], st[1, i]], axis=1).astype(single)
         theirs = jnp.concatenate([brr[0, i], brr[1, i]], axis=1).astype(single)
         return norm_parts(stream + (br[i * ROWS : (i + 1) * ROWS, :] + theirs))
+
+    pl.semaphore_wait(barrier, len(z_dev) - 1 + len(group_dev))
+    pack_qkv()
+    own_y(QKV)
+    own_z(QKV)
+    pack_head()
+    pack_ext()
+    own_y(HEAD)
+    own_z(EXT)
+    pack_up()
+    own_y(UP0)
+    pack_patches()
+    own_y(EXT)
+    send_images()
+    own_z(HEAD)
+    pass_z(EXT, 1)
+    pack_down()
+    own_y(DN1)
+    own_z(UP0)
+    pack_out()
+    pass_z(EXT, 2)
+    pass_z(HEAD, 1)
+    pass_z(EXT, 3)
+    pass_z(QKV, 1)
+    own_z(OUT)
+    pass_core(EXT)
+    pass_z(QKV, 2)
+    complete(EXT)
+    embed(0)
+    embed(1)
+    own_y(OUT)
+    pass_z(OUT, 1)
+    own_z(UP1)
+    pass_z(QKV, 3)
+    pass_z(OUT, 2)
+    pass_z(UP0, 1)
+    own_y(UP1)
+    pass_z(UP1, 1)
+    pass_z(HEAD, 2)
+    pass_z(OUT, 3)
+    own_z(DN0)
+    own_z(DN1)
+    pass_core(QKV)
+    pass_z(UP0, 2)
+    block_norm()
+    pass_z(UP1, 2)
+    complete(QKV)
+    project(0)
+    project(1)
+    project(2)
+    pass_z(HEAD, 3)
+    lax.fori_loop(0, 1, attend, 0)
+    pass_z(UP0, 3)
+    pass_z(DN1, 1)
+    pass_core(OUT)
+    lax.fori_loop(1, 2, attend, 0)
+    complete(OUT)
+    pass_z(UP1, 3)
+    pass_z(DN1, 2)
+    pass_core(HEAD)
+    pass_core(UP0)
+    lax.fori_loop(2, 3, attend, 0)
+    pass_z(DN1, 3)
+    pass_z(DN0, 1)
+    complete(UP0)
+    pass_core(UP1)
+    project_out()
+    complete(UP1)
+    lax.fori_loop(0, 2, rise, 0)
+    pass_z(DN0, 2)
+    pass_core(DN1)
+    lax.fori_loop(2, 4, rise, 0)
+    complete(DN1)
+    fall(1)
+    share(1, 1)
+    share(1, 0)
+    own_y(DN0)
+    pass_z(DN0, 3)
+    pass_core(DN0)
+    complete(DN0)
+    fall(0)
+    share(0, 1)
+    share(0, 0)
+    turn_normed()
+    head_core()
+    head_complete()
+    unpack_head()
+    block_gain, q_gain, k_gain = gain_row(0), head_gain(2), head_gain(3)
 
     out_n, out_scale = stream_out(0)
     is_patch = iota((ROWS, 1), 0) < npatch
@@ -833,155 +887,190 @@
     db2 = db[...].reshape(2 * ROWS, 768)
 
     rff, f1, f2, ft, f3 = r.rff, r.f1, r.f2, r.ft, r.f3
-    dn = br
-    ff_tags = {}
-
-    def ff_block(k):
+    dn, dm = br, r.dm
+    kept = types.SimpleNamespace(fresh=True, gains=[])
+
+    def add_in(part):
+        if kept.fresh:
+            dn[...] = part
+        else:
+            dn[...] += part
+        kept.fresh = False
+
+    def ff_send(m, k):
+        tags["ff", m, k] = send(rff.at[k, m, :, :, 1 - core], f1.at[k, m], core_dev)
+
+    def ff_down(k):
+        rff[k, 0] = dot(dbt[...], hb[z_up[k]]).astype(bfloat).reshape(2, 2, 2, 96, 384)
+        ff_send(0, k)
+
+    def ff_up(k):
         w = z_up[k]
         upper = us[w]
         t = gelu_tanh(upper)
         slope = 0.5 * (1.0 + t) + 0.5 * upper * (1.0 - t * t) * gelu_c * (
             1.0 + 3 * 0.044715 * (upper * upper)
         )
-        d_hidden = dot(db2, gdn[w].reshape(768, 384))
-        d_upper = (d_hidden * slope).astype(bfloat)
-        rff[k, 1] = dot(dbt[...], hb[w]).astype(bfloat).reshape(2, 2, 2, 96, 384)
-        rff[k, 0] = dot(nbt[...], d_upper).astype(bfloat).reshape(2, 2, 2, 96, 384)
-        ff_tags[k, 0] = send(rff.at[k, :, :, :, 1 - core], f1.at[k], core_dev)
-        part = dot_nt(d_upper, gup[w].reshape(768, 384))
-        if k == 1:
-            dn[...] = part
-        else:
-            dn[...] += part
-
-    def ff_y(k):
-        arrive(f1.at[k], ff_tags[k, 0], core_dev)
-        f1[k] = f1[k] + rff[k, :, :, :, core]
-        ff_tags[k, 1] = send(f1.at[k, :, :, 1 - y], f2.at[k], y_dev)
-
-    def ff_z(k):
-        arrive(f2.at[k], ff_tags[k, 1], y_dev)
+        d_upper = (dot(db2, gdn[w].reshape(768, 384)) * slope).astype(bfloat)
+        us[w] = d_upper.astype(single)
+        rff[k, 1] = dot(nbt[...], d_upper).astype(bfloat).reshape(2, 2, 2, 96, 384)
+        ff_send(1, k)
+
+    def ff_in(k):
+        w = z_up[k]
+        add_in(dot_nt(us[w].astype(bfloat), gup[w].reshape(768, 384)))
+
+    def ff_y(m, k):
+        arrive(f1.at[k, m], tags["ff", m, k], core_dev)
+        f1[k, m] = f1[k, m] + rff[k, m, :, :, core]
+        tags["fy", m, k] = send(f1.at[k, m, :, 1 - y], f2.at[k, m], y_dev)
+
+    def ff_z(m, k):
+        arrive(f2.at[k, m], tags["fy", m, k], y_dev)
         if k:
-            ft[k - 1] = f1[k, :, :, y] + f2[k]
-            ff_tags[k, 2] = send(ft.at[k - 1], f3.at[k - 1], z_dev[k])
+            ft[k - 1, m] = f1[k, m, :, y] + f2[k, m]
+            tags["fz", m, k] = send(ft.at[k - 1, m], f3.at[k - 1, m], z_dev[k])
 
     def ff_end():
-        total = f1[0, :, :, y].astype(single) + f2[0].astype(single)
+        for m, name in enumerate(("g_down", "g_up")):
+            total = f1[0, m, :, y].astype(single) + f2[0, m].astype(single)
+            for k in range(1, N_HID):
+                arrive(f3.at[k - 1, m], tags["fz", m, k], z_dev[k])
+                total = total + f3[k - 1, m].astype(single)
+            getattr(r, name)[...] = total.reshape(192, 384)
+            store(name)
+
+    def pass_rows():
         for k in range(1, N_HID):
-            arrive(f3.at[k - 1], ff_tags[k, 2], z_dev[k])
-            total = total + f3[k - 1].astype(single)
-        r.g_up[...] = total[0].reshape(192, 384)
-        r.g_down[...] = total[1].reshape(192, 384)
-        store("g_up")
-        store("g_down")
-
-    ff_block(1)
-    ff_y(1)
-    ff_block(2)
-    ff_y(2)
-    for k in range(1, N_HID):
-        arrive(al.at[h, dp, z_down[k]], tag_al[k - 1], z_dev[k])
-    tag_ag = [send(al.at[h, dp], al.at[h, dp], device) for device in group_dev]
-    ff_block(3)
-    ff_y(3)
-    ff_block(0)
-    ff_y(0)
-
-    rout, o1, o2, ot, o3 = r.rout, r.o1, r.o2, r.ot, r.o3
-    pieces = [
-        jnp.concatenate([db2[:, d * 96 : d * 96 + 96], db2[:, 384 + d * 96 : 384 + d * 96 + 96]], axis=1)
-        for d in range(4)
-    ]
-    hot = hof[...].T
-    d_heads = None
-    for d in range(4):
-        rout[:, d // 2, d % 2] = jnp.zeros((N_HID, 96, 256), bfloat)
-        rout[:, d // 2, d % 2, :, 0:192] = dot(hot, pieces[d]).astype(bfloat).reshape(N_HID, 96, 192)
-        part = dot_nt(pieces[d], gout[d].reshape(384, 256)[:, 0:192])
-        d_heads = part if d_heads is None else d_heads + part
-    tag_o1 = send(rout.at[:, :, 1 - core], o1, core_dev)
+            arrive(al.at[h, dp, z_down[k]], tag_al[k - 1], z_dev[k])
+        tags["ag"] = [send(al.at[h, dp], al.at[h, dp], device) for device in group_dev]
+
+    rout, o1, o2, ot, o3, pc = r.rout, r.o1, r.o2, r.ot, r.o3, r.pc
+
+    def cut_branch():
+        for d in range(4):
+            low = db2[:, d * 96 : d * 96 + 96]
+            high = db2[:, 384 + d * 96 : 384 + d * 96 + 96]
+            pc[d] = jnp.concatenate([low, high], axis=1)
+
+    def out_grad():
+        hot = hof[...].T
+        for d in range(4):
+            rout[:, d // 2, d % 2] = jnp.zeros((N_HID, 96, 256), bfloat)
+            grad = dot(hot, pc[d]).astype(bfloat).reshape(N_HID, 96, 192)
+            rout[:, d // 2, d % 2, :, 0:192] = grad
+        tags["o1"] = send(rout.at[:, :, 1 - core], o1, core_dev)
+
     dh = r.dh
-    for n in range(6):
-        part = d_heads[:, n * HD : (n + 1) * HD].astype(bfloat)
-        dh[2 * n] = part[0:ROWS]
-        dh[2 * n + 1] = part[ROWS : 2 * ROWS]
-    ff_z(1)
-
-    dq, dk, dv = ho, r.dk, r.dv
-
-    def attend_back(n, carry):
-        for i in (2 * n, 2 * n + 1):
-            probs = pr[i]
-            d_out = dh[i]
-            d_probs = dot_nt(d_out, v_ref[i])
-            dv[i] = dot_tn(probs.astype(bfloat), d_out)
-            inner = jnp.sum(probs * d_probs, axis=-1, keepdims=True)
-            d_scores = (probs * (d_probs - inner)).astype(bfloat)
-            dq[i] = dot(d_scores, k_ref[i]) * HD ** (-0.5)
-            dk[i] = dot_tn(d_scores, q_ref[i]) * HD ** (-0.5)
+
+    def out_back():
+        d_heads = None
+        for d in range(4):
+            part = dot_nt(pc[d], gout[d].reshape(384, 256)[:, 0:192])
+            d_heads = part if d_heads is None else d_heads + part
+        d_heads = d_heads.astype(bfloat)
+        for n in range(6):
+            part = d_heads[:, n * HD : (n + 1) * HD]
+            dh[2 * n] = part[0:ROWS]
+            dh[2 * n + 1] = part[ROWS : 2 * ROWS]
+
+    def out_y():
+        arrive(o1, tags["o1"], core_dev)
+        o1[...] = o1[...] + rout[:, :, core]
+        tags["o2"] = send(o1.at[:, 1 - y], o2, y_dev)
+
+    def out_z():
+        arrive(o2, tags["o2"], y_dev)
+        ot[...] = o1[:, y] + o2[...]
+        tags["o3"] = [send(ot.at[z_up[k]], o3.at[k - 1], z_dev[k]) for k in range(1, N_HID)]
+
+    def out_end():
+        total = ot[z].astype(single)
+        for k in range(1, N_HID):
+            arrive(o3.at[k - 1], tags["o3"][k - 1], z_dev[k])
+            total = total + o3[k - 1].astype(single)
+        r.g_out[...] = total[:, 0:192]
+        store("g_out")
+
+    dqkv = r.dqkv
+
+    def attend_back(pair, carry):
+        for i in range(2):
+            made = ([], [], [])
+            for side in range(2):
+                n = 4 * pair + 2 * side + i
+                probs = pr[n]
+                d_out = dh[n]
+                d_probs = dot_nt(d_out, v_ref[n])
+                inner = jnp.sum(probs * d_probs, axis=-1, keepdims=True)
+                d_scores = (probs * (d_probs - inner)).astype(bfloat)
+                made[0].append(dot(d_scores, k_ref[n]) * HD ** (-0.5))
+                made[1].append(dot_tn(d_scores, q_ref[n]) * HD ** (-0.5))
+                made[2].append(dot_tn(probs.astype(bfloat), d_out))
+            for c in range(3):
+                both = jnp.concatenate(made[c], axis=1)
+                lanes = pl.ds(pl.multiple_of(pair * 128, 128), 128)
+                dqkv[c, i * ROWS : (i + 1) * ROWS, lanes] = both
         return carry
 
-    arrive(o1, tag_o1, core_dev)
-    o1[...] = o1[...] + rout[:, :, core]
-    tag_o2 = send(o1.at[:, 1 - y], o2, y_dev)
-    lax.fori_loop(0, 3, attend_back, 0)
-    ff_z(2)
-    lax.fori_loop(3, 6, attend_back, 0)
-    ff_z(3)
-
     rqkv, q1, q2, qt, q3 = r.rqkv, r.q1, r.q2, r.qt, r.q3
-    gain_sums, dm = [], hb
-    for c, (grads, kept, gain) in enumerate(
-        ((dq, qn, q_gain), (dk, kn, k_gain), (dv, None, None))
-    ):
-        parts, sums = [], []
-        for n in range(6):
-            grad = jnp.concatenate([grads[2 * n], grads[2 * n + 1]], axis=0)
-            if kept is not None:
-                normed, scale = kept[n, :, 0:HD], kept[n, :, HD : HD + 1]
-                sums.append(jnp.sum(grad * normed, axis=0, keepdims=True))
-                grad = norm_back(normed, scale, grad * gain[:, n * HD : (n + 1) * HD])
-            parts.append(grad)
-        if sums:
-            gain_sums.append(jnp.concatenate(sums, axis=1))
-        dm[c] = jnp.concatenate(parts, axis=1).astype(bfloat)
-        dn[...] += dot_nt(dm[c], gqkv[c].reshape(768, 384))
+
+    def mix_back():
+        for c, gain in enumerate((q_gain, k_gain, None)):
+            grad = dqkv[c]
+            if gain is not None:
+                normed = nq[c]
+                kept.gains.append(jnp.sum(grad * normed, axis=0, keepdims=True))
+                grad = grad * gain
+                grad = sq[c] * (grad - head_mean(grad) - normed * head_mean(grad * normed))
+            dm[c] = grad.astype(bfloat)
+            add_in(dot_nt(dm[c], gqkv[c].reshape(768, 384)))
+
     dns, dnr = r.dns, r.dnr
-    dns[...] = dn[ROWS : 2 * ROWS, :].astype(bfloat)
-    tag_dn = send(dns, dnr, x_dev)
-    for c in range(3):
+
+    def send_in():
+        dns[...] = dn[ROWS : 2 * ROWS, :].astype(bfloat)
+        tags["dn"] = send(dns, dnr, x_dev)
+
+    def qkv_grad(c):
         rqkv[c] = dot(nbt[...], dm[c]).astype(bfloat).reshape(2, 2, 2, 2, 48, 384)
-    tag_q1 = send(rqkv.at[:, :, :, 1 - core], q1, core_dev)
-    ff_z(0)
-    arrive(q1, tag_q1, core_dev)
-    q1[...] = q1[...] + rqkv[:, :, :, core]
-    tag_q2 = send(q1.at[:, :, 1 - y], q2, y_dev)
-    arrive(o2, tag_o2, y_dev)
-    ot[...] = o1[:, y] + o2[...]
-    tag_o3 = [send(ot.at[z_up[k]], o3.at[k - 1], z_dev[k]) for k in range(1, N_HID)]
-
-    for i, (gh, gd) in enumerate(group):
-        arrive(al.at[gh, gd], tag_ag[i], group_dev[i])
-    rows_all = al[...].reshape(32, 8, 256)
-    d_logits_all = jnp.concatenate([rows_all[:, q, :] for q in range(4)], axis=1)
-    pooled_all = jnp.concatenate([rows_all[:, 4 + q, :] for q in range(3)], axis=1)
-    start = ((h * 4 + dp) * N_HID + z) * 24
-    chosen = (iota((24, 768), 1) == iota((24, 768), 0) + start).astype(bfloat)
-    mine = dot_nt(chosen, pooled_all.astype(bfloat))
-    g_head = jnp.dot(mine, d_logits_all, precision=highest, preferred_element_type=single)
-    r.g_head[...] = g_head[:, 0:classes]
-    store("g_head")
-
-    arrive(dnr, tag_dn, x_dev)
-    d_normed = dn[0:ROWS, :] + dnr[...].astype(single)
-    block_n, block_scale = norm_parts(jnp.concatenate([st[0, 0], st[1, 0]], axis=1).astype(single))
-    d_block_gain = jnp.sum(d_normed * block_n, axis=0, keepdims=True)
-    d_in = ds[...] + norm_back(block_n, block_scale, d_normed * block_gain)
+        tags["q1", c] = send(rqkv.at[c, :, :, 1 - core], q1.at[c], core_dev)
+
+    def qkv_y(c):
+        arrive(q1.at[c], tags["q1", c], core_dev)
+        q1[c] = q1[c] + rqkv[c, :, :, core]
+        tags["q2", c] = send(q1.at[c, :, 1 - y], q2.at[c], y_dev)
+
+    def qkv_z(c):
+        arrive(q2.at[c], tags["q2", c], y_dev)
+        qt[c] = q1[c, :, y] + q2[c]
+        for k in range(1, N_HID):
+            block = qt.at[c, z_up[k] // 2, lax.rem(z_up[k], 2)]
+            tags["q3", c, k] = send(block, q3.at[k - 1, c], z_dev[k])
+
+    def qkv_end():
+        for c in range(3):
+            total = qt[c, z // 2, lax.rem(z, 2)].astype(single)
+            for k in range(1, N_HID):
+                arrive(q3.at[k - 1, c], tags["q3", c, k], z_dev[k])
+                total = total + q3[k - 1, c].astype(single)
+            r.g_qkv[c] = total
+        store("g_qkv")
+
+    def head_grad():
+        for i, (gh, gd) in enumerate(group):
+            arrive(al.at[gh, gd], tags["ag"][i], group_dev[i])
+        rows_all = al[...].reshape(32, 8, 256)
+        d_logits_all = jnp.concatenate([rows_all[:, q, :] for q in range(4)], axis=1)
+        pooled_all = jnp.concatenate([rows_all[:, 4 + q, :] for q in range(3)], axis=1)
+        start = ((h * 4 + dp) * N_HID + z) * 24
+        chosen = (iota((24, 768), 1) == iota((24, 768), 0) + start).astype(bfloat)
+        mine = dot_nt(chosen, pooled_all.astype(bfloat))
+        g_head = jnp.dot(mine, d_logits_all, precision=highest, preferred_element_type=single)
+        r.g_head[...] = g_head[:, 0:classes]
+        store("g_head")
+
     dx, gg = r.dx, r.gg
-    low, high = d_in[:, 0:384], d_in[:, 384:768]
-    dx[0] = jnp.where(h == 0, low, high).astype(bfloat)
-    dx[2] = jnp.where(h == 0, high, low).astype(bfloat)
-    tag_dx = send(dx.at[2], dx.at[1], x_dev)
 
     def spread(row):
         blank = jnp.zeros((1, 192), single)
@@ -997,66 +1086,125 @@
             )
         return jnp.concatenate(halves, axis=1)
 
-    d_gains = jnp.concatenate(
-        [d_block_gain, d_final_gain, spread(gain_sums[0]), spread(gain_sums[1]), jnp.zeros((4, 768), single)],
-        axis=0,
-    )
-    low, high = d_gains[:, 0:384], d_gains[:, 384:768]
-    gg[0] = jnp.where(h == 0, low, high)
-    gg[2] = jnp.where(h == 0, high, low)
-    tag_gg = send(gg.at[2], gg.at[1], x_dev)
-    arrive(dx.at[1], tag_dx, x_dev)
-    arrive(gg.at[1], tag_gg, x_dev)
+    def norm_in():
+        arrive(dnr, tags["dn"], x_dev)
+        d_normed = dn[0:ROWS, :] + dnr[...].astype(single)
+        block_n, block_scale = norm_parts(jnp.concatenate([st[0, 0], st[1, 0]], axis=1).astype(single))
+        d_block_gain = jnp.sum(d_normed * block_n, axis=0, keepdims=True)
+        d_in = ds[...] + norm_back(block_n, block_scale, d_normed * block_gain)
+        low, high = d_in[:, 0:384], d_in[:, 384:768]
+        dx[2] = jnp.where(h == 0, high, low).astype(bfloat)
+        tags["dx"] = send(dx.at[2], dx.at[1], x_dev)
+        dx[0] = jnp.where(h == 0, low, high).astype(bfloat)
+        d_gains = jnp.concatenate(
+            [d_block_gain, d_final_gain, spread(kept.gains[0]), spread(kept.gains[1])]
+            + [jnp.zeros((4, 768), single)],
+            axis=0,
+        )
+        low, high = d_gains[:, 0:384], d_gains[:, 384:768]
+        gg[0] = jnp.where(h == 0, low, high)
+        gg[2] = jnp.where(h == 0, high, low)
+        tags["gg"] = send(gg.at[2], gg.at[1], x_dev)
+
     rext, e1, e2, et, e3 = r.rext, r.e1, r.e2, r.et, r.e3
-    dxt = jnp.concatenate([dx[0].astype(single), dx[1].astype(single)], axis=0).T.astype(bfloat)
-    px2 = px[...].reshape(2 * ROWS, 1024)
-    d_gains = (gg[0] + gg[1]).astype(bfloat)
-    x0[...] = dot(dxt, px2[:, 0:512])
-    x1[...] = dot(dxt, px2[:, 512:1024]) + dot_tn(d_gains, rows_of.astype(bfloat))
-    for d in range(4):
-        for w in range(N_HID):
-            s = (d * N_HID + w) * 24
-            rext[d // 2, d % 2, w] = jnp.concatenate(
-                [x0[s : s + 24, :], x1[s : s + 24, :]], axis=0
-            ).astype(bfloat)
-    tag_e1 = send(rext.at[:, 1 - core], e1, core_dev)
-    arrive(q2, tag_q2, y_dev)
-    qt[...] = q1[:, :, y] + q2[...]
-    tag_q3 = [
-        send(qt.at[:, z_up[k] // 2, lax.rem(z_up[k], 2)], q3.at[k - 1], z_dev[k])
-        for k in range(1, N_HID)
-    ]
-    arrive(e1, tag_e1, core_dev)
-    e1[...] = e1[...] + rext[:, core]
-    tag_e2 = send(e1.at[1 - y], e2, y_dev)
+
+    def ext_grad():
+        arrive(dx.at[1], tags["dx"], x_dev)
+        arrive(gg.at[1], tags["gg"], x_dev)
+        dxt = jnp.concatenate([dx[0].astype(single), dx[1].astype(single)], axis=0).T.astype(bfloat)
+        px2 = px[...].reshape(2 * ROWS, 1024)
+        d_gains = (gg[0] + gg[1]).astype(bfloat)
+        x0[...] = dot(dxt, px2[:, 0:512])
+        x1[...] = dot(dxt, px2[:, 512:1024]) + dot_tn(d_gains, rows_of.astype(bfloat))
+        for d in range(4):
+            for w in range(N_HID):
+                s = (d * N_HID + w) * 24
+                rext[d // 2, d % 2, w] = jnp.concatenate(
+                    [x0[s : s + 24, :], x1[s : s + 24, :]], axis=0
+                ).astype(bfloat)
+        tags["e1"] = send(rext.at[:, 1 - core], e1, core_dev)
+
+    def ext_y():
+        arrive(e1, tags["e1"], core_dev)
+        e1[...] = e1[...] + rext[:, core]
+        tags["e2"] = send(e1.at[1 - y], e2, y_dev)
+
+    def ext_z():
+        arrive(e2, tags["e2"], y_dev)
+        et[...] = e1[y] + e2[...]
+        tags["e3"] = [send(et.at[z_up[k]], e3.at[k - 1], z_dev[k]) for k in range(1, N_HID)]
+
+    def ext_end():
+        total = et[z].astype(single)
+        for k in range(1, N_HID):
+            arrive(e3.at[k - 1], tags["e3"][k - 1], z_dev[k])
+            total = total + e3[k - 1].astype(single)
+        r.g_patch[:, 0:512] = total[0:24]
+        r.g_patch[:, 512:768] = total[24:48, 0:256]
+        r.g_table[...] = total[24:48, 256 : 256 + seq_len]
+        columns = total[24:48, 256:512]
+        pick_f = (iota((8, 256), 1) == iota((8, 256), 0) + seq_len).astype(single)
+        r.g_gains[...] = dot_nt(pick_f, columns, precision=highest)[0:4]
+        for name in ("g_patch", "g_table", "g_gains"):
+            store(name)
+
+    ff_down(1)
+    ff_down(2)
+    ff_y(0, 1)
+    cut_branch()
+    out_back()
+    ff_down(3)
+    pass_rows()
+    ff_up(2)
+    ff_y(0, 2)
+    ff_in(2)
+    ff_up(3)
+    ff_y(0, 3)
+    ff_z(0, 1)
+    out_grad()
+    ff_up(1)
+    ff_up(0)
+    ff_y(1, 2)
+    ff_y(1, 1)
+    ff_y(1, 3)
+    ff_z(0, 2)
+    lax.fori_loop(0, 1, attend_back, 0)
+    ff_in(3)
+    ff_y(1, 0)
+    ff_z(0, 3)
+    lax.fori_loop(1, 2, attend_back, 0)
+    lax.fori_loop(2, 3, attend_back, 0)
+    out_y()
+    ff_z(1, 2)
+    ff_in(0)
+    mix_back()
+    ff_in(1)
+    send_in()
+    qkv_grad(0)
+    ff_z(1, 3)
+    qkv_grad(2)
+    qkv_y(2)
+    qkv_grad(1)
+    ff_down(0)
+    qkv_y(0)
+    ff_z(1, 1)
+    out_z()
+    qkv_y(1)
+    norm_in()
+    qkv_z(2)
+    ff_z(1, 0)
+    qkv_z(0)
+    ext_grad()
+    out_end()
+    ext_y()
+    head_grad()
+    ff_y(0, 0)
+    qkv_z(1)
+    ext_z()
+    qkv_end()
+    ff_z(0, 0)
     ff_end()
-    total = ot[z].astype(single)
-    for k in range(1, N_HID):
-        arrive(o3.at[k - 1], tag_o3[k - 1], z_dev[k])
-        total = total + o3[k - 1].astype(single)
-    r.g_out[...] = total[:, 0:192]
-    store("g_out")
-    arrive(e2, tag_e2, y_dev)
-    et[...] = e1[y] + e2[...]
-    tag_e3 = [send(et.at[z_up[k]], e3.at[k - 1], z_dev[k]) for k in range(1, N_HID)]
-    total = qt[:, z // 2, lax.rem(z, 2)].astype(single)
-    for k in range(1, N_HID):
-        arrive(q3.at[k - 1], tag_q3[k - 1], z_dev[k])
-        total = total + q3[k - 1].astype(single)
-    r.g_qkv[...] = total
-    store("g_qkv")
-    total = et[z].astype(single)
-    for k in range(1, N_HID):
-        arrive(e3.at[k - 1], tag_e3[k - 1], z_dev[k])
-        total = total + e3[k - 1].astype(single)
-    r.g_patch[:, 0:512] = total[0:24]
-    r.g_patch[:, 512:768] = total[24:48, 0:256]
-    r.g_table[...] = total[24:48, 256 : 256 + seq_len]
-    columns = total[24:48, 256:512]
-    pick_f = (iota((8, 256), 1) == iota((8, 256), 0) + seq_len).astype(single)
-    r.g_gains[...] = dot_nt(pick_f, columns, precision=highest)[0:4]
-    for name in ("g_patch", "g_table", "g_gains"):
-        store(name)
+    ext_end()
 
 
     def read(prefix, kind):
@@ -1189,13 +1337,13 @@
         st=((2, 2, ROWS, 384), bfloat),
         nb=((2 * ROWS, 768), bfloat),
         nbt=((768, 2 * ROWS), bfloat),
-        qn=((6, 2 * ROWS, 2 * HD), single),
-        kn=((6, 2 * ROWS, 2 * HD), single),
+        nq=((2, 2 * ROWS, 384), single),
+        sq=((2, 2 * ROWS, 384), single),
+        bd=((384, 384), bfloat),
         q=((12, ROWS, HD), bfloat),
         k=((12, ROWS, HD), bfloat),
         v=((12, ROWS, HD), bfloat),
         pr=((12, ROWS, ROWS), single),
-        ho=((12, ROWS, HD), single),
         hof=((2 * ROWS, 384), bfloat),
         us=((4, 2 * ROWS, 384), single),
         hb=((4, 2 * ROWS, 384), bfloat),
@@ -1218,8 +1366,9 @@
         ot=((4, 96, 256), bfloat),
         o3=((3, 96, 256), bfloat),
         dh=((12, ROWS, HD), bfloat),
-        dk=((12, ROWS, HD), single),
-        dv=((12, ROWS, HD), single),
+        dm=((3, 2 * ROWS, 384), bfloat),
+        pc=((4, 2 * ROWS, 192), bfloat),
+        dqkv=((3, 2 * ROWS, 384), single),
         rqkv=((3, 2, 2, 2, 2, 48, 384), bfloat),
         q1=((3, 2, 2, 2, 48, 384), bfloat),
         q2=((3, 2, 2, 48, 384), bfloat),

time: 171 us -> 154 us (0.901)
  Pallas kernels: 169 us -> 152 us
    pallas_call x1, Pallas kernels: 165 us -> 147 us  [fast_device(): pl.pallas_call(functools.partial(step_kernel, sizes, names), out_shape=[j...]
where the time goes in v3:
time: 154 us
  Pallas kernels  152 us (99%)
    pallas_call x1, Pallas kernels, fast_device(): pl.pallas_call(functools.partial(step_kernel, sizes, names), out_shape=[j...  147 us
    pallas_call x1, Pallas kernels, fast_device(): pl.pallas_call(functools.partial(write_kernel, names), out_shape=[jax.Sha...  4.49 us

profile of v3, /device:TPU:0, one launch (start us, length us, event | category | flops | bytes accessed | tf_op | source)
XLA Modules:
  0.0 153.7 jit_solution(3159240521600687444)
XLA Ops:
  0.7 147.2 %train_step.1 = (f32[24,768]{1,0:T(8,128)}, f32[24,200]{1,0:T(8,128)}, f32[4,24]{1,0:T(4,128)}, f32[24,1000]{1,0:T(8,128)}, f32[3,48,384]{2,1,0:T(8,128)}, /*ind...) custom-call(s32[8]{0:T(128)} %refs_0_.1, bf16[1,196,768]{2,1,0:T(8,128)(2,1)} %refs_1_.1, ...), custom_call_target="tpu_custom_call" | custom-call | tf_op jit(solution)/shard_map/train_step/pallas_call | solution.py:1399
  147.9 4.5 %write_step.1 = (f32[24,768]{1,0:T(8,128)}, f32[24,200]{1,0:T(8,128)}, f32[4,24]{1,0:T(4,128)}, f32[24,1000]{1,0:T(8,128)}, f32[3,48,384]{2,1,0:T(8,128)}, /*ind...) custom-call(f32[8,128]{1,0:T(8,128)} %get-tuple-element.59.refs_0_, ...), custom_call_target="tpu_custom_call" | custom-call | tf_op jit(solution)/shard_map/write_step/pallas_call | solution.py:1418
  152.4 1.3 fusion

commit v4 on v3

--- a/solution.py
+++ b/solution.py
@@ -360,11 +360,8 @@
     clipped = grad * clip
     first_new = beta_one * first + (1.0 - beta_one) * clipped
     second_new = beta_two * second + (1.0 - beta_two) * clipped * clipped
-    update = (
-        first_new
-        / (1.0 - beta_one**STEP)
-        / (jnp.sqrt(second_new / (1.0 - beta_two**STEP)) + adam_eps)
-    )
+    one, two = 1.0 / (1.0 - beta_one**STEP), 1.0 / (1.0 - beta_two**STEP)
+    update = (first_new * one) / (jnp.sqrt(second_new * two) + adam_eps)
     return first_new, second_new, update + decay_rate * master
 
 
@@ -390,29 +387,31 @@
     z_up = [lax.rem(z + k, N_HID) for k in range(N_HID)]
     z_down = [lax.rem(z + N_HID - k, N_HID) for k in range(N_HID)]
     z_dev = [(dp, h, z_up[k]) for k in range(N_HID)]
-    group = []
-    for a in (0, 1):
-        for b in (0, 1):
-            for c in (0, 1):
-                if a + b + c:
-                    gh = 1 - h if a else h
-                    gy = 1 - y if b else y
-                    gc = 1 - core if c else core
-                    group.append((gh, gy * 2 + gc))
-    group_dev = [(gd, gh, z) for gh, gd in group]
+    group = [(h, y, z_up[k]) for k in range(1, N_HID)]
+    for gh, gy in ((1 - h, y), (h, 1 - y), (1 - h, 1 - y)):
+        group.extend((gh, gy, z_up[k]) for k in range(N_HID))
+    source = [(h, y, z_down[k]) for k in range(1, N_HID)]
+    for gh, gy in ((1 - h, y), (h, 1 - y), (1 - h, 1 - y)):
+        source.extend((gh, gy, z_down[k]) for k in range(N_HID))
+    group_dev = [(gy * 2 + core, gh, gz) for gh, gy, gz in group]
 
     barrier = pltpu.get_barrier_semaphore()
-    for device in z_dev[1:] + group_dev:
+    for device in [core_dev] + group_dev:
         pl.semaphore_signal(barrier, inc=1, device_id=device, device_id_type=MESH)
 
     loads = {}
-    order = ["w_patch", "w_table", "w_gains", "patches"]
-    order += [p + k for p in ("w_", "m_", "v_") for k in KINDS if p + k not in order]
-    for number, name in enumerate(order):
-        loads[name] = pltpu.make_async_copy(
-            getattr(r, "h_" + name), getattr(r, name), r.lsem.at[number]
-        )
-        loads[name].start()
+    order = ["w_up", "w_patch", "w_table", "w_gains"]
+    order += ["w_" + k for k in KINDS if "w_" + k not in order] + ["patches"]
+    order += [p + k for p in ("m_", "v_") for k in KINDS]
+
+    def load(names):
+        for name in names:
+            loads[name] = pltpu.make_async_copy(
+                getattr(r, "h_" + name), getattr(r, name), r.lsem.at[order.index(name)]
+            )
+            loads[name].start()
+
+    load(order[0:9])
     stores = []
 
     def store(name):
@@ -470,7 +469,7 @@
 
     def pack_ext():
         x1[0:24, :] = jnp.zeros((24, 512), single)
-        for name in order[0:3]:
+        for name in order[1:4]:
             loads[name].wait()
         x1[0:24, 256 : 256 + seq_len] = r.w_table[...]
         pick = (iota((4, 256), 1) == iota((4, 256), 0) + seq_len).astype(bfloat)
@@ -752,91 +751,92 @@
         theirs = jnp.concatenate([brr[0, i], brr[1, i]], axis=1).astype(single)
         return norm_parts(stream + (br[i * ROWS : (i + 1) * ROWS, :] + theirs))
 
-    pl.semaphore_wait(barrier, len(z_dev) - 1 + len(group_dev))
+    pl.semaphore_wait(barrier, 1 + len(group_dev))
+    pack_up()
+    own_y(UP0)
+    own_z(UP0)
+    pack_head()
+    own_z(HEAD)
+    own_y(HEAD)
+    pack_ext()
+    own_y(EXT)
+    own_y(UP1)
+    own_z(EXT)
     pack_qkv()
+    pass_z(UP0, 1)
+    pass_z(EXT, 1)
+    pack_out()
     own_y(QKV)
     own_z(QKV)
-    pack_head()
-    pack_ext()
-    own_y(HEAD)
-    own_z(EXT)
-    pack_up()
-    own_y(UP0)
+    own_z(OUT)
+    pass_z(EXT, 2)
     pack_patches()
-    own_y(EXT)
+    pass_z(UP0, 2)
     send_images()
-    own_z(HEAD)
-    pass_z(EXT, 1)
-    pack_down()
-    own_y(DN1)
-    own_z(UP0)
-    pack_out()
-    pass_z(EXT, 2)
+    pass_z(QKV, 1)
     pass_z(HEAD, 1)
     pass_z(EXT, 3)
-    pass_z(QKV, 1)
-    own_z(OUT)
+    pack_down()
+    own_z(UP1)
+    own_y(OUT)
+    pass_z(QKV, 2)
     pass_core(EXT)
-    pass_z(QKV, 2)
+    pass_z(UP0, 3)
     complete(EXT)
     embed(0)
+    load(order[9:])
+    pass_z(HEAD, 2)
+    pass_z(QKV, 3)
+    pass_z(UP1, 1)
+    pass_z(HEAD, 3)
     embed(1)
-    own_y(OUT)
+    pass_z(UP1, 2)
+    own_z(DN1)
+    pass_z(UP1, 3)
+    own_y(DN1)
     pass_z(OUT, 1)
-    own_z(UP1)
-    pass_z(QKV, 3)
+    pass_core(UP0)
+    pass_core(QKV)
+    own_z(DN0)
+    block_norm()
+    pass_z(DN1, 1)
     pass_z(OUT, 2)
-    pass_z(UP0, 1)
-    own_y(UP1)
-    pass_z(UP1, 1)
-    pass_z(HEAD, 2)
-    pass_z(OUT, 3)
-    own_z(DN0)
-    own_z(DN1)
-    pass_core(QKV)
-    pass_z(UP0, 2)
-    block_norm()
-    pass_z(UP1, 2)
     complete(QKV)
     project(0)
     project(1)
     project(2)
-    pass_z(HEAD, 3)
+    pass_core(HEAD)
+    pass_core(UP1)
+    turn_normed()
+    pass_z(DN1, 2)
     lax.fori_loop(0, 1, attend, 0)
-    pass_z(UP0, 3)
-    pass_z(DN1, 1)
-    pass_core(OUT)
+    complete(UP0)
+    pass_z(OUT, 3)
     lax.fori_loop(1, 2, attend, 0)
-    complete(OUT)
-    pass_z(UP1, 3)
-    pass_z(DN1, 2)
-    pass_core(HEAD)
-    pass_core(UP0)
     lax.fori_loop(2, 3, attend, 0)
     pass_z(DN1, 3)
     pass_z(DN0, 1)
-    complete(UP0)
-    pass_core(UP1)
-    project_out()
     complete(UP1)
     lax.fori_loop(0, 2, rise, 0)
+    own_y(DN0)
+    lax.fori_loop(2, 4, rise, 0)
     pass_z(DN0, 2)
+    pass_core(OUT)
     pass_core(DN1)
-    lax.fori_loop(2, 4, rise, 0)
+    complete(OUT)
+    project_out()
     complete(DN1)
     fall(1)
     share(1, 1)
+    pass_z(DN0, 3)
     share(1, 0)
-    own_y(DN0)
-    pass_z(DN0, 3)
     pass_core(DN0)
     complete(DN0)
     fall(0)
     share(0, 1)
-    share(0, 0)
-    turn_normed()
     head_core()
     head_complete()
+    share(0, 0)
     unpack_head()
     block_gain, q_gain, k_gain = gain_row(0), head_gain(2), head_gain(3)
 
@@ -872,13 +872,14 @@
     d_final_gain = d_pooled * n_sum
     al = r.al
     pooled_f = pooled_b.astype(single)
-    al[h, dp, z] = jnp.concatenate(
+    al[core, h, y, z] = jnp.concatenate(
         [d_logits[:, q * 256 : q * 256 + 256] for q in range(4)]
         + [pooled_f[:, q * 256 : q * 256 + 256] for q in range(3)]
         + [jnp.zeros((1, 256), single)],
         axis=0,
     )
-    tag_al = [send(al.at[h, dp, z], al.at[h, dp, z], z_dev[k]) for k in range(1, N_HID)]
+    own = al.at[core, h, y, z]
+    tag_al = [send(own, own, device) for device in group_dev]
     out_n, out_scale = stream_out(1)
     arrive(rw.at[1], tag_rw, x_dev)
     d_stream = jnp.where(is_patch, norm_back(out_n, out_scale, rw[1, 0:1, :]), 0.0)
@@ -941,9 +942,9 @@
             store(name)
 
     def pass_rows():
-        for k in range(1, N_HID):
-            arrive(al.at[h, dp, z_down[k]], tag_al[k - 1], z_dev[k])
-        tags["ag"] = [send(al.at[h, dp], al.at[h, dp], device) for device in group_dev]
+        for i, place in enumerate(source):
+            arrive(al.at[(core, *place)], tag_al[i], core_dev)
+        tags["al"] = send(al.at[core], al.at[core], core_dev)
 
     rout, o1, o2, ot, o3, pc = r.rout, r.o1, r.o2, r.ot, r.o3, r.pc
 
@@ -1058,8 +1059,7 @@
         store("g_qkv")
 
     def head_grad():
-        for i, (gh, gd) in enumerate(group):
-            arrive(al.at[gh, gd], tags["ag"][i], group_dev[i])
+        arrive(al.at[1 - core], tags["al"], core_dev)
         rows_all = al[...].reshape(32, 8, 256)
         d_logits_all = jnp.concatenate([rows_all[:, q, :] for q in range(4)], axis=1)
         pooled_all = jnp.concatenate([rows_all[:, 4 + q, :] for q in range(3)], axis=1)
@@ -1148,92 +1148,90 @@
         for name in ("g_patch", "g_table", "g_gains"):
             store(name)
 
-    ff_down(1)
     ff_down(2)
-    ff_y(0, 1)
+    ff_up(3)
+    ff_y(0, 2)
     cut_branch()
     out_back()
+    ff_down(1)
+    ff_up(1)
+    ff_y(0, 1)
+    pass_rows()
+    ff_y(1, 3)
+    ff_up(2)
+    ff_z(0, 2)
+    ff_in(2)
+    out_grad()
+    ff_up(0)
+    ff_in(0)
+    ff_z(0, 1)
+    ff_y(1, 2)
+    lax.fori_loop(0, 1, attend_back, 0)
+    lax.fori_loop(1, 2, attend_back, 0)
+    ff_y(1, 1)
+    ff_z(1, 3)
+    ff_down(0)
+    ff_in(3)
+    ff_in(1)
     ff_down(3)
-    pass_rows()
-    ff_up(2)
-    ff_y(0, 2)
-    ff_in(2)
-    ff_up(3)
+    out_y()
+    lax.fori_loop(2, 3, attend_back, 0)
     ff_y(0, 3)
-    ff_z(0, 1)
-    out_grad()
-    ff_up(1)
-    ff_up(0)
-    ff_y(1, 2)
-    ff_y(1, 1)
-    ff_y(1, 3)
-    ff_z(0, 2)
-    lax.fori_loop(0, 1, attend_back, 0)
-    ff_in(3)
-    ff_y(1, 0)
-    ff_z(0, 3)
-    lax.fori_loop(1, 2, attend_back, 0)
-    lax.fori_loop(2, 3, attend_back, 0)
-    out_y()
+    ff_z(1, 1)
     ff_z(1, 2)
-    ff_in(0)
     mix_back()
-    ff_in(1)
     send_in()
     qkv_grad(0)
-    ff_z(1, 3)
+    qkv_y(0)
     qkv_grad(2)
+    qkv_grad(1)
     qkv_y(2)
-    qkv_grad(1)
-    ff_down(0)
-    qkv_y(0)
-    ff_z(1, 1)
     out_z()
     qkv_y(1)
+    ff_y(1, 0)
     norm_in()
+    ff_z(0, 3)
     qkv_z(2)
-    ff_z(1, 0)
+    ext_grad()
+    qkv_z(1)
     qkv_z(0)
-    ext_grad()
-    out_end()
     ext_y()
     head_grad()
+    ext_z()
     ff_y(0, 0)
-    qkv_z(1)
-    ext_z()
+    ff_z(0, 0)
     qkv_end()
-    ff_z(0, 0)
+    ff_z(1, 0)
+    out_end()
     ff_end()
-    ext_end()
-
 
     def read(prefix, kind):
         values = getattr(r, prefix + kind)[...]
         return values.reshape(-1, values.shape[-1])
-
     lane = iota((8, 128), 1)
-    own = jnp.where(lane == 0, term, 0.0)
-    grad_square = None
+    own = jnp.zeros((8, 128), single)
+    grad_square = jnp.zeros((1, 1), single)
     for n, kind in enumerate(KINDS):
-        value = square_sum(read("g_", kind))
-        grad_square = value if grad_square is None else grad_square + value
         own = jnp.where(lane == 8 + n, square_sum(read("w_", kind)), own)
+        if n > 2:
+            grad_square = grad_square + square_sum(read("g_", kind))
+    ext_end()
+
+    own = jnp.where(lane == 0, term, own)
+    for kind in KINDS[0:3]:
+        grad_square = grad_square + square_sum(read("g_", kind))
     own = jnp.where(lane == 1, grad_square, own)
 
-    def all_sum(vector, line, every):
-        line[z] = vector
-        tags_z = [send(line.at[z], line.at[z], z_dev[k]) for k in range(1, N_HID)]
-        for k in range(1, N_HID):
-            arrive(line.at[z_down[k]], tags_z[k - 1], z_dev[k])
-        every[h, dp] = (line[0] + line[1]) + (line[2] + line[3])
-        tags_g = [send(every.at[h, dp], every.at[h, dp], device) for device in group_dev]
-        for i, (gh, gd) in enumerate(group):
-            arrive(every.at[gh, gd], tags_g[i], group_dev[i])
-        total = None
-        for a in range(2):
-            for d in range(4):
-                total = every[a, d] if total is None else total + every[a, d]
-        return total
+    def all_sum(vector, pair, every):
+        pair[0] = vector
+        tag = send(pair.at[0], pair.at[1], core_dev)
+        arrive(pair.at[1], tag, core_dev)
+        every[h, y, z] = pair[0] + pair[1]
+        mine = every.at[h, y, z]
+        numbers = [send(mine, mine, device) for device in group_dev]
+        for i, place in enumerate(source):
+            arrive(every.at[place], numbers[i], core_dev)
+        return jnp.sum(every[...].reshape(16, 8, 128), axis=0)
 
     sums = all_sum(own, r.l1, r.v1)
     grad_norm = jnp.sqrt(jnp.sum(jnp.where(lane == 1, sums, 0.0), axis=1, keepdims=True))[0:1]
@@ -1281,6 +1279,8 @@
         return jnp.sum(jnp.where(lane == n, r.scalars[...], 0.0), axis=1, keepdims=True)[0:1]
 
     clip = pick(2)
+    r.o_loss[...] = pick(0)
+    r.o_norm[...] = pick(1)
     stores = []
     for n, kind in enumerate(KINDS):
         for p in ("w_", "m_", "v_", "g_"):
@@ -1354,7 +1354,7 @@
         ds=((ROWS, 768), single),
         db=((2, ROWS, 768), bfloat),
         dbt=((768, 2 * ROWS), bfloat),
-        al=((2, 4, 4, 8, 256), single),
+        al=((2, 2, 2, 4, 8, 256), single),
         rff=((4, 2, 2, 2, 2, 96, 384), bfloat),
         f1=((4, 2, 2, 2, 96, 384), bfloat),
         f2=((4, 2, 2, 96, 384), bfloat),
@@ -1383,12 +1383,12 @@
         e2=((4, 48, 512), bfloat),
         et=((4, 48, 512), bfloat),
         e3=((3, 48, 512), bfloat),
-        l1=((4, 8, 128), single),
-        l2=((4, 8, 128), single),
-        v1=((2, 4, 8, 128), single),
-        v2=((2, 4, 8, 128), single),
-    )
-    semaphores = 256
+        l1=((2, 8, 128), single),
+        l2=((2, 8, 128), single),
+        v1=((2, 2, 4, 8, 128), single),
+        v2=((2, 2, 4, 8, 128), single),
+    )
+    semaphores = 320
     shapes = [flat[i].shape for i in range(8)]
     npatch, seq_len, classes = patches.shape[1], flat[1].shape[1], flat[3].shape[1]
     total_images = labels.shape[0] * lax.axis_size("dp")
@@ -1414,19 +1414,20 @@
     in_names = ["scalars"] + [p + k for p in ("w_", "m_", "v_", "g_") for k in KINDS]
     out_names = [p + k for p in ("nm_", "nv_", "nw_") for k in KINDS]
     held = [((8, 128), single)] + [(s, single) for s in shapes * 7]
-    names = ["h_" + n for n in in_names + out_names] + in_names + out_names + ["lsem"]
+    names = ["h_" + n for n in in_names + out_names] + ["o_loss", "o_norm"]
+    names += in_names + out_names + ["lsem"]
     written = pl.pallas_call(
         functools.partial(write_kernel, names),
-        out_shape=[jax.ShapeDtypeStruct(s, single) for s in shapes * 3],
+        out_shape=[jax.ShapeDtypeStruct(s, single) for s in shapes * 3 + [(1, 1), (1, 1)]],
         in_specs=[hbm] * 33,
-        out_specs=[hbm] * 24,
+        out_specs=[hbm] * 24 + [pl.BlockSpec(memory_space=pltpu.VMEM)] * 2,
         scratch_shapes=[pltpu.VMEM(s, t) for s, t in held]
         + [pltpu.SemaphoreType.DMA((len(held),))],
         compiler_params=pltpu.CompilerParams(vmem_limit_bytes=62 * 2**20),
         name="write_step",
     )(scalars, *flat, *grads)
-    back = [turn(KINDS[i % 8], value) for i, value in enumerate(written)]
-    return (scalars[0, 0], scalars[0, 1], *back)
+    back = [turn(KINDS[i % 8], value) for i, value in enumerate(written[:24])]
+    return (written[24].reshape(()), written[25].reshape(()), *back)
 
 
 def fits(mesh):

time: 154 us -> 149 us (0.968)
  Pallas kernels: 152 us -> 148 us
    pallas_call x1, Pallas kernels: 147 us -> 143 us  [fast_device(): pl.pallas_call(functools.partial(step_kernel, sizes, names), out_shape=[j...]
where the time goes in v4:
time: 149 us
  Pallas kernels  148 us (99%)
    pallas_call x1, Pallas kernels, fast_device(): pl.pallas_call(functools.partial(step_kernel, sizes, names), out_shape=[j...  143 us
    pallas_call x1, Pallas kernels, fast_device(): pl.pallas_call(functools.partial(write_kernel, names), out_shape=[jax.Sha...  5.04 us

profile of v4, /device:TPU:0, one launch (start us, length us, event | category | flops | bytes accessed | tf_op | source)
XLA Modules:
  0.0 148.7 jit_solution(6311553943266408076)
XLA Ops:
  0.7 142.8 %train_step.1 = (f32[24,768]{1,0:T(8,128)}, f32[24,200]{1,0:T(8,128)}, f32[4,24]{1,0:T(4,128)}, f32[24,1000]{1,0:T(8,128)}, f32[3,48,384]{2,1,0:T(8,128)}, /*ind...) custom-call(s32[8]{0:T(128)} %refs_0_.1, bf16[1,196,768]{2,1,0:T(8,128)(2,1)} %refs_1_.1, ...), custom_call_target="tpu_custom_call" | custom-call | tf_op jit(solution)/shard_map/train_step/pallas_call | solution.py:1399
  143.5 5.0 %write_step.1 = (f32[24,768]{1,0:T(8,128)}, f32[24,200]{1,0:T(8,128)}, f32[4,24]{1,0:T(4,128)}, f32[24,1000]{1,0:T(8,128)}, f32[3,48,384]{2,1,0:T(8,128)}, /*ind...) custom-call(f32[8,128]{1,0:T(8,128)} %get-tuple-element.61.refs_0_, ...), custom_call_target="tpu_custom_call" | custom-call | tf_op jit(solution)/shard_map/write_step/pallas_call | solution.py:1419

commit v5 on v4

--- a/solution.py
+++ b/solution.py
@@ -510,7 +510,7 @@
 
     def pack_down():
         loads["w_down"].wait()
-        gdn[z, :, dp] = r.w_down[...].astype(bfloat).reshape(2, 96, 384)
+        gdn[z, :, y, core] = r.w_down[...].astype(bfloat).reshape(2, 96, 384)
 
     def at_ext(d, w):
         return gext.at[d, w]
@@ -525,7 +525,7 @@
         return lambda d, w: gup.at[w, half, d]
 
     def at_dn(half):
-        return lambda d, w: gdn.at[w, half, d]
+        return lambda d, w: gdn.at[w, half, d // 2, lax.rem(d, 2)]
 
     def at_hd(d, w):
         return ghd.at[h, d, w]
@@ -546,8 +546,8 @@
         OUT: lambda d: gout.at[d],
         UP0: lambda d: gup.at[:, 0, d],
         UP1: lambda d: gup.at[:, 1, d],
-        DN0: lambda d: gdn.at[:, 0, d],
-        DN1: lambda d: gdn.at[:, 1, d],
+        DN0: lambda d: gdn.at[:, 0, d // 2, lax.rem(d, 2)],
+        DN1: lambda d: gdn.at[:, 1, d // 2, lax.rem(d, 2)],
         HEAD: lambda d: ghd.at[h, d],
     }
     tags = {}
@@ -572,6 +572,26 @@
         if d == last and name != HEAD:
             line = lines[name](dp)
             tags[name, "c", 0] = send(line, line, core_dev)
+
+    def pair_own():
+        arrive(slot[DN0](y_dp, z), tags[DN0, "y", 0], y_dev)
+        own = gdn.at[z, 0, :, core]
+        tags[DN0, LEFT, 1] = send(own, own, next_z[LEFT], (ON_RIGHT, 0))
+        tags[DN0, RIGHT, 1] = send(own, own, next_z[RIGHT], (ON_LEFT, 0))
+
+    def pair_z(d):
+        for side, on, theirs in ((LEFT, ON_RIGHT, z_down[d]), (RIGHT, ON_LEFT, z_up[d])):
+            block = gdn.at[theirs, 0, :, core]
+            number = tags[DN0, side, d]
+            pl.when(holds[side, d])(functools.partial(arrive, block, number, y_dev))
+            if d < last:
+                tags[DN0, side, d + 1] = send(block, block, next_z[side], (on, d))
+        if d == last:
+            block = gdn.at[:, 0, :, core]
+            tags[DN0, "c", 0] = send(block, block, core_dev)
+
+    def pair_complete():
+        arrive(gdn.at[:, 0, :, 1 - core], tags[DN0, "c", 0], core_dev)
 
     def pass_core(name):
         at = slot[name]
@@ -753,91 +773,90 @@
 
     pl.semaphore_wait(barrier, 1 + len(group_dev))
     pack_up()
+    own_z(UP1)
+    own_y(UP1)
+    pack_ext()
+    own_z(EXT)
+    own_z(UP0)
     own_y(UP0)
-    own_z(UP0)
+    pack_patches()
     pack_head()
+    pack_down()
+    own_y(DN0)
+    pass_z(UP1, 1)
+    pass_z(EXT, 1)
+    send_images()
+    pass_z(UP0, 1)
+    own_y(EXT)
     own_z(HEAD)
-    own_y(HEAD)
-    pack_ext()
-    own_y(EXT)
-    own_y(UP1)
-    own_z(EXT)
+    pass_z(EXT, 2)
+    pass_z(UP1, 2)
     pack_qkv()
-    pass_z(UP0, 1)
-    pass_z(EXT, 1)
-    pack_out()
     own_y(QKV)
     own_z(QKV)
+    pass_z(EXT, 3)
+    pack_out()
     own_z(OUT)
-    pass_z(EXT, 2)
-    pack_patches()
+    pass_z(HEAD, 1)
+    pass_z(UP1, 3)
+    pair_own()
     pass_z(UP0, 2)
-    send_images()
+    pass_core(EXT)
+    complete(EXT)
     pass_z(QKV, 1)
-    pass_z(HEAD, 1)
-    pass_z(EXT, 3)
-    pack_down()
-    own_z(UP1)
-    own_y(OUT)
-    pass_z(QKV, 2)
-    pass_core(EXT)
-    pass_z(UP0, 3)
-    complete(EXT)
     embed(0)
     load(order[9:])
     pass_z(HEAD, 2)
-    pass_z(QKV, 3)
-    pass_z(UP1, 1)
-    pass_z(HEAD, 3)
     embed(1)
-    pass_z(UP1, 2)
-    own_z(DN1)
-    pass_z(UP1, 3)
-    own_y(DN1)
+    pass_z(UP0, 3)
+    pass_core(UP1)
+    own_y(HEAD)
+    pass_z(QKV, 2)
     pass_z(OUT, 1)
     pass_core(UP0)
+    own_z(DN1)
+    pass_z(HEAD, 3)
+    pass_z(QKV, 3)
+    complete(UP0)
+    complete(UP1)
+    pair_z(1)
+    own_y(OUT)
+    pass_z(OUT, 2)
+    block_norm()
+    lax.fori_loop(0, 2, rise, 0)
+    lax.fori_loop(2, 4, rise, 0)
+    pass_z(DN1, 1)
+    pass_core(HEAD)
     pass_core(QKV)
-    own_z(DN0)
-    block_norm()
-    pass_z(DN1, 1)
-    pass_z(OUT, 2)
+    pass_z(OUT, 3)
+    own_y(DN1)
+    pair_z(2)
     complete(QKV)
     project(0)
     project(1)
     project(2)
-    pass_core(HEAD)
-    pass_core(UP1)
-    turn_normed()
+    lax.fori_loop(0, 1, attend, 0)
+    lax.fori_loop(1, 2, attend, 0)
+    pass_core(OUT)
     pass_z(DN1, 2)
-    lax.fori_loop(0, 1, attend, 0)
-    complete(UP0)
-    pass_z(OUT, 3)
-    lax.fori_loop(1, 2, attend, 0)
+    pair_z(3)
     lax.fori_loop(2, 3, attend, 0)
-    pass_z(DN1, 3)
-    pass_z(DN0, 1)
-    complete(UP1)
-    lax.fori_loop(0, 2, rise, 0)
-    own_y(DN0)
-    lax.fori_loop(2, 4, rise, 0)
-    pass_z(DN0, 2)
-    pass_core(OUT)
-    pass_core(DN1)
     complete(OUT)
     project_out()
+    pair_complete()
+    fall(0)
+    share(0, 1)
+    share(0, 0)
+    pass_z(DN1, 3)
+    pass_core(DN1)
     complete(DN1)
     fall(1)
     share(1, 1)
-    pass_z(DN0, 3)
     share(1, 0)
-    pass_core(DN0)
-    complete(DN0)
-    fall(0)
-    share(0, 1)
     head_core()
     head_complete()
-    share(0, 0)
     unpack_head()
+    turn_normed()
     block_gain, q_gain, k_gain = gain_row(0), head_gain(2), head_gain(3)
 
     out_n, out_scale = stream_out(0)
@@ -1328,7 +1347,7 @@
         gqkv=((3, 2, 4, 2, 48, 384), bfloat),
         gout=((4, 4, 96, 256), bfloat),
         gup=((4, 2, 4, 96, 384), bfloat),
-        gdn=((4, 2, 4, 96, 384), bfloat),
+        gdn=((4, 2, 2, 2, 96, 384), bfloat),
         ghd=((2, 4, 4, 48, 512), bfloat),
         x0=((384, 512), single),
         x1=((384, 512), single),

time: 149 us -> 146 us (0.980)
  Pallas kernels: 148 us -> 145 us
    pallas_call x1, Pallas kernels: 143 us -> 140 us  [fast_device(): pl.pallas_call(functools.partial(step_kernel, sizes, names), out_shape=[j...]
where the time goes in v5:
time: 146 us
  Pallas kernels  145 us (99%)
    pallas_call x1, Pallas kernels, fast_device(): pl.pallas_call(functools.partial(step_kernel, sizes, names), out_shape=[j...  140 us
    pallas_call x1, Pallas kernels, fast_device(): pl.pallas_call(functools.partial(write_kernel, names), out_shape=[jax.Sha...  5.04 us

profile of v5, /device:TPU:0, one launch (start us, length us, event | category | flops | bytes accessed | tf_op | source)
XLA Modules:
  0.0 145.8 jit_solution(3177558436736752646)
XLA Ops:
  0.7 139.9 %train_step.1 = (f32[24,768]{1,0:T(8,128)}, f32[24,200]{1,0:T(8,128)}, f32[4,24]{1,0:T(4,128)}, f32[24,1000]{1,0:T(8,128)}, f32[3,48,384]{2,1,0:T(8,128)}, /*ind...) custom-call(s32[8]{0:T(128)} %refs_0_.1, bf16[1,196,768]{2,1,0:T(8,128)(2,1)} %refs_1_.1, ...), custom_call_target="tpu_custom_call" | custom-call | tf_op jit(solution)/shard_map/train_step/pallas_call | solution.py:1418
  140.6 5.0 %write_step.1 = (f32[24,768]{1,0:T(8,128)}, f32[24,200]{1,0:T(8,128)}, f32[4,24]{1,0:T(4,128)}, f32[24,1000]{1,0:T(8,128)}, f32[3,48,384]{2,1,0:T(8,128)}, /*ind...) custom-call(f32[8,128]{1,0:T(8,128)} %get-tuple-element.61.refs_0_, ...), custom_call_target="tpu_custom_call" | custom-call | tf_op jit(solution)/shard_map/write_step/pallas_call | solution.py:1438

commit v6 on v5

--- a/solution.py
+++ b/solution.py
@@ -1242,7 +1242,7 @@
     own = jnp.where(lane == 1, grad_square, own)
 
     def all_sum(vector, pair, every):
-        pair[0] = vector
+        pair[0] = vector[0:1]
         tag = send(pair.at[0], pair.at[1], core_dev)
         arrive(pair.at[1], tag, core_dev)
         every[h, y, z] = pair[0] + pair[1]
@@ -1250,7 +1250,8 @@
         numbers = [send(mine, mine, device) for device in group_dev]
         for i, place in enumerate(source):
             arrive(every.at[place], numbers[i], core_dev)
-        return jnp.sum(every[...].reshape(16, 8, 128), axis=0)
+        total = jnp.sum(every[...].reshape(16, 1, 128), axis=0)
+        return jnp.broadcast_to(total, (8, 128))
 
     sums = all_sum(own, r.l1, r.v1)
     grad_norm = jnp.sqrt(jnp.sum(jnp.where(lane == 1, sums, 0.0), axis=1, keepdims=True))[0:1]
@@ -1285,7 +1286,8 @@
 def write_kernel(names, *refs):
     r = types.SimpleNamespace(**dict(zip(names, refs)))
     lane = iota((8, 128), 1)
-    inputs = ["scalars"] + [p + k for k in KINDS for p in ("w_", "m_", "v_", "g_")]
+    turns = (3, 4, 6, 7, 0, 5, 1, 2)
+    inputs = ["scalars"] + [p + KINDS[n] for n in turns for p in ("w_", "m_", "v_", "g_")]
     loads = {}
     for number, name in enumerate(inputs):
         loads[name] = pltpu.make_async_copy(
@@ -1301,7 +1303,8 @@
     r.o_loss[...] = pick(0)
     r.o_norm[...] = pick(1)
     stores = []
-    for n, kind in enumerate(KINDS):
+    for n in turns:
+        kind = KINDS[n]
         for p in ("w_", "m_", "v_", "g_"):
             loads[p + kind].wait()
         master = getattr(r, "w_" + kind)[...]
@@ -1402,10 +1405,10 @@
         e2=((4, 48, 512), bfloat),
         et=((4, 48, 512), bfloat),
         e3=((3, 48, 512), bfloat),
-        l1=((2, 8, 128), single),
-        l2=((2, 8, 128), single),
-        v1=((2, 2, 4, 8, 128), single),
-        v2=((2, 2, 4, 8, 128), single),
+        l1=((2, 1, 128), single),
+        l2=((2, 1, 128), single),
+        v1=((2, 2, 4, 1, 128), single),
+        v2=((2, 2, 4, 1, 128), single),
     )
     semaphores = 320
     shapes = [flat[i].shape for i in range(8)]

time: 146 us -> 144 us (0.986)
  Pallas kernels: 145 us -> 143 us
    pallas_call x1, Pallas kernels: 140 us -> 138 us  [fast_device(): pl.pallas_call(functools.partial(step_kernel, sizes, names), out_shape=[j...]
where the time goes in v6:
time: 144 us
  Pallas kernels  143 us (99%)
    pallas_call x1, Pallas kernels, fast_device(): pl.pallas_call(functools.partial(step_kernel, sizes, names), out_shape=[j...  138 us
    pallas_call x1, Pallas kernels, fast_device(): pl.pallas_call(functools.partial(write_kernel, names), out_shape=[jax.Sha...  4.76 us

profile of v6, /device:TPU:0, one launch (start us, length us, event | category | flops | bytes accessed | tf_op | source)
XLA Modules:
  0.0 144.0 jit_solution(12534634558569917838)
XLA Ops:
  0.7 138.4 %train_step.1 = (f32[24,768]{1,0:T(8,128)}, f32[24,200]{1,0:T(8,128)}, f32[4,24]{1,0:T(4,128)}, f32[24,1000]{1,0:T(8,128)}, f32[3,48,384]{2,1,0:T(8,128)}, /*ind...) custom-call(s32[8]{0:T(128)} %refs_0_.1, bf16[1,196,768]{2,1,0:T(8,128)(2,1)} %refs_1_.1, ...), custom_call_target="tpu_custom_call" | custom-call | tf_op jit(solution)/shard_map/train_step/pallas_call | solution.py:1421
  139.1 4.8 %write_step.1 = (f32[24,768]{1,0:T(8,128)}, f32[24,200]{1,0:T(8,128)}, f32[4,24]{1,0:T(4,128)}, f32[24,1000]{1,0:T(8,128)}, f32[3,48,384]{2,1,0:T(8,128)}, /*ind...) custom-call(f32[8,128]{1,0:T(8,128)} %get-tuple-element.61.refs_0_, ...), custom_call_target="tpu_custom_call" | custom-call | tf_op jit(solution)/shard_map/write_step/pallas_call | solution.py:1441
